TPU v7x, 32 devices: a whole 2x2x4 slice. The times are simulated.
32 devices in a mesh: front: 4 (over x, core), wide: 8 (over z, y).
Axes of the slice: x: 2, y: 2, z: 4, core: 2. Of those that a mesh axis runs over, the one named last changes fastest.
Arguments:
- inv_diag: bfloat16 [4, 8192, 8192], P('front', 'wide'), as said below
- below: bfloat16 [4, 6144, 8192], P('front', 'wide'), may hold values from -0.0625 to 0.0625
- rhs: bfloat16 [4, 8192, 256], P('front', 'wide'), may hold values from -6 to 6
- tile_count: int32 [4], replicated, may hold values from 36 to 48, as said below
- tile_owner: int32 [4, 48, 1], P('front', 'wide'), may hold values from 0 to 3; in each aligned block of 6 rows (0 to 5, 6 to 11, ..., all dimensions but the last counted through in order) at most 2 rows name the same one
- tile_rows: int32 [4, 48, 128], P('front', 'wide'), may hold values from 0 to 511
- parent_rhs: bfloat16 [4, 4096, 256], P('front', 'wide'), may hold values from -6 to 6
Outputs:
- solved: bfloat16 [4, 8192, 256], P('front', 'wide')
- parent_new: float32 [4, 4096, 256], P('front', 'wide')
Inputs may be any that keep to these rules, and one draw needn't show every extreme that they name: Each inv_diag[f] is lower triangular. Tiles of front f with index at least tile_count[f] carry nothing; some front has all 48 tiles live. `tile_owner`: among the 6 tiles of one device (aligned blocks of tiles), no front index is named more than 2 times.
All inputs are finite; a program needn't handle non-finite values.
Results may differ from a plain program's by a relative error of at most 0.0037.
Values may be sent and summed in bfloat16 or wider, within the bound.
No kernel may reach another device: no remote copies, remote signals or barrier semaphores. Data moves between devices by JAX's collectives and lax.ppermute only.
A program may use at most 128 MiB of HBM per device.

v0:
```python
import jax
import jax.numpy as jnp
from jax import lax
from jax.sharding import PartitionSpec as P

CAPACITY = 2
LANES = 128
ROUTING_STEPS = (2, 4)


def ring_order(count):
    if count % 8:
        return list(range(count))
    depth = 4
    columns = count // depth
    walk = [z * columns for z in range(depth)]
    for step, z in enumerate(range(depth - 1, -1, -1)):
        ys = range(1, columns) if step % 2 == 0 else range(columns - 1, 0, -1)
        walk += [z * columns + y for y in ys]
    return walk


def lookup(table, index):
    result = jnp.int32(table[0])
    for place in range(1, len(table)):
        result = jnp.where(index == place, jnp.int32(table[place]), result)
    return result


def dot(a, b):
    return jnp.dot(a, b, preferred_element_type=jnp.float32)


def body(inv_diag, below, rhs, tile_count, tile_owner, tile_rows, parent_rhs):
    width = rhs.shape[2]
    rows = rhs.shape[1]
    half = rows // 2
    tiles = tile_owner.shape[1]
    height = tile_rows.shape[2]
    parent_height = parent_rhs.shape[1]
    fronts = lax.axis_size("front")
    wide = lax.axis_size("wide")
    me = lax.axis_index("front")
    wide_index = lax.axis_index("wide")
    order = ring_order(wide)
    place = lookup([order.index(i) for i in range(wide)], wide_index)
    onward = [(order[i], order[(i + 1) % wide]) for i in range(wide)]
    backward = [(b, a) for a, b in onward]
    from_left = [lookup(order, (place + wide - step) % wide) for step in range(wide)]
    from_right = [lookup(order, (place + step) % wide) for step in range(wide)]

    def part(matrix, index, offset, values):
        columns = lax.dynamic_slice_in_dim(matrix, index * rows + offset, values.shape[0], 1)
        return dot(columns, values)

    def ring_products(matrix, blocks, aside=None):
        travelling = [(block[:half], block[half:]) for block in blocks]
        totals = [part(matrix, wide_index, 0, block) for block in blocks]
        extra = None
        for step in range(1, wide):
            for column, (first, second) in enumerate(travelling):
                first = lax.ppermute(first, "wide", onward)
                second = lax.ppermute(second, "wide", backward)
                if aside and column == 0 and step == ROUTING_STEPS[0]:
                    extra, first = aside(first)
                if aside and column == 0 and step == ROUTING_STEPS[1]:
                    first, extra = lax.optimization_barrier((first, extra))
                travelling[column] = (first, second)
                totals[column] = totals[column] + part(matrix, from_left[step], 0, first)
                totals[column] = totals[column] + part(matrix, from_right[step], half, second)
        return [total.astype(jnp.bfloat16) for total in totals], extra

    swaps = [[(i, i ^ delta) for i in range(fronts)] for delta in range(fronts)]

    def routing(after):
        counts, owners, places, after = lax.optimization_barrier(
            (tile_count, tile_owner, tile_rows, after)
        )
        serial = jnp.arange(tiles, dtype=jnp.int32)
        live_count = jnp.sum(jnp.where(jnp.arange(fronts) == me, counts, 0))
        alive = wide_index * tiles + serial < live_count
        owners = owners[0, :, 0]
        same_owner = owners[:, None] == owners[None, :]
        earlier = serial[None, :] < serial[:, None]
        slot = jnp.sum((same_owner & earlier).astype(jnp.int32), axis=1)
        seat = (owners ^ me) * CAPACITY + slot
        slots = fronts * CAPACITY
        chosen = jnp.arange(slots, dtype=jnp.int32)[:, None] == seat[None, :]
        shifted = jnp.where(alive[:, None], places[0] - parent_height, 0)
        rows_out = parent_height + jnp.sum(jnp.where(chosen[:, :, None], shifted[None], 0), axis=1)
        rows_out = rows_out.reshape(fronts, CAPACITY * height)
        rows_in = [rows_out[0]] + [
            lax.ppermute(rows_out[delta], "front", swaps[delta]) for delta in range(1, fronts)
        ]
        picker = (
            jnp.arange(slots * height, dtype=jnp.int32)[:, None]
            == (seat[:, None] * height + jnp.arange(height, dtype=jnp.int32)[None, :]).reshape(1, -1)
        ).astype(jnp.bfloat16)
        picker = picker.reshape(fronts, CAPACITY * height, tiles * height)
        alive_rows = jnp.broadcast_to(alive[:, None], (tiles, height)).reshape(-1, 1)
        return (rows_in, picker, alive_rows), after

    cuts = range(0, width, LANES)
    solved, (rows_in, picker, alive_rows) = ring_products(
        inv_diag[0], [rhs[0][:, c:c + LANES] for c in cuts], routing
    )
    numbers = jnp.arange(parent_height, dtype=jnp.int32)[:, None]

    updates, _ = ring_products(below[0], solved)
    results = []
    for c, update in zip(cuts, updates):
        update = jnp.where(alive_rows, update, jnp.zeros_like(update))
        values_out = [dot(picker[delta], update).astype(jnp.bfloat16) for delta in range(fronts)]
        values_in = [values_out[0]] + [
            lax.ppermute(values_out[delta], "front", swaps[delta]) for delta in range(1, fronts)
        ]
        total = parent_rhs[0][:, c:c + LANES].astype(jnp.float32)
        for rows_here, values in zip(rows_in, values_in):
            hits = (numbers == rows_here[None, :]).astype(jnp.bfloat16)
            total = total - dot(hits, values)
        results.append(total)
    return (
        jnp.concatenate(solved, axis=1)[None],
        jnp.concatenate(results, axis=1)[None],
    )


def solution(mesh):
    split = P("front", "wide", None)
    return jax.shard_map(
        body,
        mesh=mesh,
        in_specs=(split, split, split, P(), split, split, split),
        out_specs=(split, split),
        check_vma=False,
    )
```

profile of v0, /device:TPU:0, one launch (start us, length us, event | category | flops | bytes accessed | tf_op | source)
XLA Modules:
  0.0 173.7 jit_solution(6095295354561111668)
XLA Ops:
  1.8 3.1 %collective-permute-start = (bf16[512,128]{1,0:T(8,128)(2,1)S(1)}, bf16[512,128]{1,0:T(8,128)(2,1)S(1)}, u32[]{:S(2)}, u32[]{:S(2)}) collective-permute-start(bf16[512,128]{1,0:T(8,128)(2,1)S(1)} %get-tuple-element.33), channel_id=1, source_target_pairs={{0,2},{2,4},{4,6},{6,7},{7,5},{5,3},{3,1},{1,0},{8,10},{10,12},{12... | collective-permute-start | bytes 393224 | tf_op jit(solution)/shard_map/ppermute | solution.py:62
  4.9 2.0 %collective-permute-start.17 = (bf16[512,128]{1,0:T(8,128)(2,1)S(1)}, bf16[512,128]{1,0:T(8,128)(2,1)S(1)}, u32[]{:S(2)}, u32[]{:S(2)}) collective-permute-start(bf16[512,128]{1,0:T(8,128)(2,1)S(1)} %get-tuple-element.32), channel_id=1, source_target_pairs={{0,2},{2,4},{4,6},{6,7},{7,5},{5,3},{3,1},{1,0},{8,10},{10,12},{12... | collective-permute-start | bytes 393224 | tf_op jit(solution)/shard_map/ppermute | solution.py:62
  6.9 2.4 %fusion.2 = f32[1024,128]{0,1:T(8,128)S(1)} fusion(bf16[1,1024,8192]{2,1,0:T(8,128)(2,1)} %param.7, s32[]{:T(128)S(6)} %select_n.372, bf16[1024,256]{1,0:T(8,128)(2,1)} %bitcast.276), kind=kOutput, calls=%fused_computation.3 | convolution fusion | flops 268435456 | bytes 2883588 | tf_op jit(solution)/shard_map/dot_general | solution.py:31
  9.3 2.4 %fusion = f32[1024,128]{0,1:T(8,128)S(1)} fusion(bf16[1,1024,8192]{2,1,0:T(8,128)(2,1)} %param.7, s32[]{:T(128)S(6)} %select_n.372, bf16[1024,256]{1,0:T(8,128)(2,1)} %bitcast.277), kind=kOutput, calls=%fused_computation.1 | convolution fusion | flops 268435456 | bytes 2883588 | tf_op jit(solution)/shard_map/dot_general | solution.py:31
  13.2 2.1 %collective-permute-start.2 = (bf16[512,128]{1,0:T(8,128)(2,1)S(1)}, bf16[512,128]{1,0:T(8,128)(2,1)S(1)}, u32[]{:S(2)}, u32[]{:S(2)}) collective-permute-start(bf16[512,128]{1,0:T(8,128)(2,1)S(1)} %collective-permute-done), channel_id=1, source_target_pairs={{0,2},{2,4},{4,6},{6,7},{7,5},{5,3},{3,1},{1,0},{8,10},{10,12},{12... | collective-permute-start | bytes 393224 | tf_op jit(solution)/shard_map/ppermute | solution.py:62
  15.3 2.0 %collective-permute-start.19 = (bf16[512,128]{1,0:T(8,128)(2,1)S(1)}, bf16[512,128]{1,0:T(8,128)(2,1)S(1)}, u32[]{:S(2)}, u32[]{:S(2)}) collective-permute-start(bf16[512,128]{1,0:T(8,128)(2,1)S(1)} %collective-permute-done.17), channel_id=1, source_target_pairs={{0,2},{2,4},{4,6},{6,7},{7,5},{5,3},{3,1},{1,0},{8,10},{10,12},{12... | collective-permute-start | bytes 393224 | tf_op jit(solution)/shard_map/ppermute | solution.py:62
  17.3 1.7 convolution_add_fusion.15
  19.0 1.7 convolution_add_fusion.7
  20.8 1.7 convolution_add_fusion.14
  22.6 1.7 convolution_add_fusion.6
  24.3 2.0 %collective-permute-start.4 = (bf16[512,128]{1,0:T(8,128)(2,1)S(1)}, bf16[512,128]{1,0:T(8,128)(2,1)S(1)}, u32[]{:S(2)}, u32[]{:S(2)}) collective-permute-start(bf16[512,128]{1,0:T(8,128)(2,1)S(1)} %collective-permute-done.2), channel_id=1, source_target_pairs={{0,2},{2,4},{4,6},{6,7},{7,5},{5,3},{3,1},{1,0},{8,10},{10,12},{12... | collective-permute-start | bytes 393224 | tf_op jit(solution)/shard_map/ppermute | solution.py:62
  30.7 1.7 fusion.76
  33.1 1.7 fusion.18
  34.8 1.7 fusion.78
  36.5 1.8 %collective-permute-start.22 = (bf16[512,128]{1,0:T(8,128)(2,1)S(1)}, bf16[512,128]{1,0:T(8,128)(2,1)}, u32[]{:S(2)}, u32[]{:S(2)}) collective-permute-start(bf16[512,128]{1,0:T(8,128)(2,1)S(1)} %collective-permute-done.20), channel_id=1, source_target_pairs={{2,0},{4,2},{6,4},{7,6},{5,7},{3,5},{1,3},{0,1},{10,8},{12,10},{14... | collective-permute-start | bytes 393224 | tf_op jit(solution)/shard_map/ppermute | solution.py:63
  38.3 1.7 fusion.74
  40.0 1.7 fusion.13
  42.1 1.7 %collective-permute-start.21 = (bf16[512,128]{1,0:T(8,128)(2,1)S(1)}, bf16[512,128]{1,0:T(8,128)(2,1)}, u32[]{:S(2)}, u32[]{:S(2)}) collective-permute-start(bf16[512,128]{1,0:T(8,128)(2,1)S(1)} %collective-permute-done.19), channel_id=1, source_target_pairs={{0,2},{2,4},{4,6},{6,7},{7,5},{5,3},{3,1},{1,0},{8,10},{10,12},{12... | collective-permute-start | bytes 393224 | tf_op jit(solution)/shard_map/ppermute | solution.py:62
  43.9 1.7 fusion.70
  45.6 1.6 collective-permute-start.6
  47.2 2.8 %collective-permute-start.10 = (bf16[512,128]{1,0:T(8,128)(2,1)S(1)}, bf16[512,128]{1,0:T(8,128)(2,1)S(1)}, u32[]{:S(2)}, u32[]{:S(2)}) collective-permute-start(bf16[512,128]{1,0:T(8,128)(2,1)S(1)} %collective-permute-done.5), channel_id=1, source_target_pairs={{2,0},{4,2},{6,4},{7,6},{5,7},{3,5},{1,3},{0,1},{10,8},{12,10},{14... | collective-permute-start | bytes 393224 | tf_op jit(solution)/shard_map/ppermute | solution.py:63
  50.0 1.7 fusion.19
  51.8 1.6 collective-permute-start.24
  54.5 2.1 %collective-permute-start.12 = (bf16[512,128]{1,0:T(8,128)(2,1)S(1)}, bf16[512,128]{1,0:T(8,128)(2,1)S(1)}, u32[]{:S(2)}, u32[]{:S(2)}) collective-permute-start(bf16[512,128]{1,0:T(8,128)(2,1)S(1)} %collective-permute-done.10), channel_id=1, source_target_pairs={{2,0},{4,2},{6,4},{7,6},{5,7},{3,5},{1,3},{0,1},{10,8},{12,10},{14... | collective-permute-start | bytes 393224 | tf_op jit(solution)/shard_map/ppermute | solution.py:63
  56.5 1.7 fusion.68
  58.2 1.6 collective-permute-start.26
  59.9 1.7 fusion.64
  62.1 1.7 fusion.14
  63.8 1.7 fusion.20
  65.6 2.0 %collective-permute-start.14 = (bf16[512,128]{1,0:T(8,128)(2,1)S(1)}, bf16[512,128]{1,0:T(8,128)(2,1)S(1)}, u32[]{:S(2)}, u32[]{:S(2)}) collective-permute-start(bf16[512,128]{1,0:T(8,128)(2,1)S(1)} %collective-permute-done.12), channel_id=1, source_target_pairs={{2,0},{4,2},{6,4},{7,6},{5,7},{3,5},{1,3},{0,1},{10,8},{12,10},{14... | collective-permute-start | bytes 393224 | tf_op jit(solution)/shard_map/ppermute | solution.py:63
  67.6 1.7 fusion.62
  69.3 1.6 collective-permute-start.28
  71.0 1.7 fusion.58
  73.2 1.7 fusion.15
  74.9 1.7 fusion.21
  76.8 2.0 %collective-permute-start.16 = (bf16[512,128]{1,0:T(8,128)(2,1)S(1)}, bf16[512,128]{1,0:T(8,128)(2,1)S(1)}, u32[]{:S(2)}, u32[]{:S(2)}) collective-permute-start(bf16[512,128]{1,0:T(8,128)(2,1)S(1)} %collective-permute-done.14), channel_id=1, source_target_pairs={{2,0},{4,2},{6,4},{7,6},{5,7},{3,5},{1,3},{0,1},{10,8},{12,10},{14... | collective-permute-start | bytes 393224 | tf_op jit(solution)/shard_map/ppermute | solution.py:63
  78.7 1.7 fusion.56
  80.4 1.6 collective-permute-start.30
  82.1 1.7 fusion.52
  84.5 1.7 fusion.16
  86.2 1.7 fusion.22
  87.9 1.7 fusion.50
  89.6 1.7 fusion.17
  91.3 1.7 fusion.46
  93.1 1.7 fusion.25
  95.5 1.7 fusion.24
  98.1 2.0 %fusion.8 = f32[768,128]{1,0:T(8,128)S(1)} fusion(bf16[1024,128]{0,1:T(8,128)(2,1)S(1)} %fusion.25, bf16[1,768,8192]{2,1,0:T(8,128)(2,1)} %param.8, s32[]{:T(128)S(6)} %select_n.372), kind=kOutput, calls=%fused_computation.9 | convolution fusion | flops 201326592 | bytes 2228228 | tf_op jit(solution)/shard_map/dot_general | solution.py:31
  100.0 2.0 %collective-permute-start.32 = (bf16[512,128]{0,1:T(8,128)(2,1)}, bf16[512,128]{0,1:T(8,128)(2,1)}, u32[]{:S(2)}, u32[]{:S(2)}) collective-permute-start(bf16[512,128]{0,1:T(8,128)(2,1)} %get-tuple-element.35), channel_id=1, source_target_pairs={{2,0},{4,2},{6,4},{7,6},{5,7},{3,5},{1,3},{0,1},{10,8},{12,10},{14... | collective-permute-start | bytes 393224 | tf_op jit(solution)/shard_map/ppermute | solution.py:63
  102.1 2.0 %collective-permute-start.49 = (bf16[512,128]{0,1:T(8,128)(2,1)}, bf16[512,128]{0,1:T(8,128)(2,1)}, u32[]{:S(2)}, u32[]{:S(2)}) collective-permute-start(bf16[512,128]{0,1:T(8,128)(2,1)} %get-tuple-element.37), channel_id=1, source_target_pairs={{2,0},{4,2},{6,4},{7,6},{5,7},{3,5},{1,3},{0,1},{10,8},{12,10},{14... | collective-permute-start | bytes 393224 | tf_op jit(solution)/shard_map/ppermute | solution.py:63
  105.1 2.1 %fusion.6 = f32[768,128]{1,0:T(8,128)S(1)} fusion(bf16[1024,128]{0,1:T(8,128)(2,1)S(1)} %fusion.24, bf16[1,768,8192]{2,1,0:T(8,128)(2,1)} %param.8, s32[]{:T(128)S(6)} %select_n.372), kind=kOutput, calls=%fused_computation.7 | convolution fusion | flops 201326592 | bytes 2228228 | tf_op jit(solution)/shard_map/dot_general | solution.py:31
  108.9 2.0 %collective-permute-start.34 = (bf16[512,128]{0,1:T(8,128)(2,1)}, bf16[512,128]{0,1:T(8,128)(2,1)S(1)}, u32[]{:S(2)}, u32[]{:S(2)}) collective-permute-start(bf16[512,128]{0,1:T(8,128)(2,1)} %collective-permute-done.32), channel_id=1, source_target_pairs={{2,0},{4,2},{6,4},{7,6},{5,7},{3,5},{1,3},{0,1},{10,8},{12,10},{14... | collective-permute-start | bytes 393224 | tf_op jit(solution)/shard_map/ppermute | solution.py:63
  114.0 2.0 %collective-permute-start.51 = (bf16[512,128]{0,1:T(8,128)(2,1)}, bf16[512,128]{0,1:T(8,128)(2,1)S(1)}, u32[]{:S(2)}, u32[]{:S(2)}) collective-permute-start(bf16[512,128]{0,1:T(8,128)(2,1)} %collective-permute-done.49), channel_id=1, source_target_pairs={{2,0},{4,2},{6,4},{7,6},{5,7},{3,5},{1,3},{0,1},{10,8},{12,10},{14... | collective-permute-start | bytes 393224 | tf_op jit(solution)/shard_map/ppermute | solution.py:63
  117.6 1.6 collective-permute-start.36
  121.2 1.6 collective-permute-start.53
  127.8 1.6 collective-permute-start.38
  131.4 1.6 collective-permute-start.55
  138.1 1.6 collective-permute-start.40
  141.7 1.6 collective-permute-start.57
  146.1 1.6 collective-permute-start.42
  148.6 1.6 collective-permute-start.59
  151.8 1.6 collective-permute-start.44
  154.3 1.6 collective-permute-start.61
  159.9 1.6 collective-permute-done.60
  169.6 1.8 %collective-permute-done.63 = bf16[256,128]{1,0:T(8,128)(2,1)S(1)} collective-permute-done((bf16[256,128]{1,0:T(8,128)(2,1)S(1)}, bf16[256,128]{1,0:T(8,128)(2,1)S(1)}, u32[]{:S(2)}, u32[]{:S(2)}) %collective-permute-start.63) | collective-permute-done | bytes 65568 | tf_op jit(solution)/shard_map/ppermute | solution.py:115
  (183 shorter events, 55.7 us)
Async XLA Ops:
  1.8 11.4 %collective-permute-start = (bf16[512,128]{1,0:T(8,128)(2,1)S(1)}, bf16[512,128]{1,0:T(8,128)(2,1)S(1)}, u32[]{:S(2)}, u32[]{:S(2)}) collective-permute-start(bf16[512,128]{1,0:T(8,128)(2,1)S(1)} %get-tuple-element.33), channel_id=1, source_target_pairs={{0,2},{2,4},{4,6},{6,7},{7,5},{5,3},{3,1},{1,0},{8,10},{10,12},{12... | collective-permute-start | bytes 393224 | tf_op jit(solution)/shard_map/ppermute | solution.py:62
  4.9 10.4 %collective-permute-start.1 = (bf16[512,128]{1,0:T(8,128)(2,1)S(1)}, bf16[512,128]{1,0:T(8,128)(2,1)S(1)}, u32[]{:S(2)}, u32[]{:S(2)}) collective-permute-start(bf16[512,128]{1,0:T(8,128)(2,1)S(1)} %get-tuple-element.30), channel_id=1, source_target_pairs={{2,0},{4,2},{6,4},{7,6},{5,7},{3,5},{1,3},{0,1},{10,8},{12,10},{14... | collective-permute-start | bytes 393224 | tf_op jit(solution)/shard_map/ppermute | solution.py:63
  4.9 10.4 %collective-permute-start.17 = (bf16[512,128]{1,0:T(8,128)(2,1)S(1)}, bf16[512,128]{1,0:T(8,128)(2,1)S(1)}, u32[]{:S(2)}, u32[]{:S(2)}) collective-permute-start(bf16[512,128]{1,0:T(8,128)(2,1)S(1)} %get-tuple-element.32), channel_id=1, source_target_pairs={{0,2},{2,4},{4,6},{6,7},{7,5},{5,3},{3,1},{1,0},{8,10},{10,12},{12... | collective-permute-start | bytes 393224 | tf_op jit(solution)/shard_map/ppermute | solution.py:62
  6.9 13.8 %collective-permute-start.18 = (bf16[512,128]{1,0:T(8,128)(2,1)S(1)}, bf16[512,128]{1,0:T(8,128)(2,1)S(1)}, u32[]{:S(2)}, u32[]{:S(2)}) collective-permute-start(bf16[512,128]{1,0:T(8,128)(2,1)S(1)} %get-tuple-element.31), channel_id=1, source_target_pairs={{2,0},{4,2},{6,4},{7,6},{5,7},{3,5},{1,3},{0,1},{10,8},{12,10},{14... | collective-permute-start | bytes 393224 | tf_op jit(solution)/shard_map/ppermute | solution.py:63
  13.2 11.1 %collective-permute-start.2 = (bf16[512,128]{1,0:T(8,128)(2,1)S(1)}, bf16[512,128]{1,0:T(8,128)(2,1)S(1)}, u32[]{:S(2)}, u32[]{:S(2)}) collective-permute-start(bf16[512,128]{1,0:T(8,128)(2,1)S(1)} %collective-permute-done), channel_id=1, source_target_pairs={{0,2},{2,4},{4,6},{6,7},{7,5},{5,3},{3,1},{1,0},{8,10},{10,12},{12... | collective-permute-start | bytes 393224 | tf_op jit(solution)/shard_map/ppermute | solution.py:62
  15.3 17.1 %collective-permute-start.3 = (bf16[512,128]{1,0:T(8,128)(2,1)S(1)}, bf16[512,128]{1,0:T(8,128)(2,1)S(1)}, u32[]{:S(2)}, u32[]{:S(2)}) collective-permute-start(bf16[512,128]{1,0:T(8,128)(2,1)S(1)} %collective-permute-done.1), channel_id=1, source_target_pairs={{2,0},{4,2},{6,4},{7,6},{5,7},{3,5},{1,3},{0,1},{10,8},{12,10},{14... | collective-permute-start | bytes 393224 | tf_op jit(solution)/shard_map/ppermute | solution.py:63
  15.3 17.5 %collective-permute-start.19 = (bf16[512,128]{1,0:T(8,128)(2,1)S(1)}, bf16[512,128]{1,0:T(8,128)(2,1)S(1)}, u32[]{:S(2)}, u32[]{:S(2)}) collective-permute-start(bf16[512,128]{1,0:T(8,128)(2,1)S(1)} %collective-permute-done.17), channel_id=1, source_target_pairs={{0,2},{2,4},{4,6},{6,7},{7,5},{5,3},{3,1},{1,0},{8,10},{10,12},{12... | collective-permute-start | bytes 393224 | tf_op jit(solution)/shard_map/ppermute | solution.py:62
  20.7 8.4 %collective-permute-start.20 = (bf16[512,128]{1,0:T(8,128)(2,1)S(1)}, bf16[512,128]{1,0:T(8,128)(2,1)S(1)}, u32[]{:S(2)}, u32[]{:S(2)}) collective-permute-start(bf16[512,128]{1,0:T(8,128)(2,1)S(1)} %collective-permute-done.18), channel_id=1, source_target_pairs={{2,0},{4,2},{6,4},{7,6},{5,7},{3,5},{1,3},{0,1},{10,8},{12,10},{14... | collective-permute-start | bytes 393224 | tf_op jit(solution)/shard_map/ppermute | solution.py:63
  24.3 12.2 %collective-permute-start.4 = (bf16[512,128]{1,0:T(8,128)(2,1)S(1)}, bf16[512,128]{1,0:T(8,128)(2,1)S(1)}, u32[]{:S(2)}, u32[]{:S(2)}) collective-permute-start(bf16[512,128]{1,0:T(8,128)(2,1)S(1)} %collective-permute-done.2), channel_id=1, source_target_pairs={{0,2},{2,4},{4,6},{6,7},{7,5},{5,3},{3,1},{1,0},{8,10},{10,12},{12... | collective-permute-start | bytes 393224 | tf_op jit(solution)/shard_map/ppermute | solution.py:62
  28.6 23.1 %collective-permute-start.7 = (s32[256]{0:T(256)S(1)}, s32[256]{0:T(256)S(1)}, u32[]{:S(2)}, u32[]{:S(2)}) collective-permute-start(s32[256]{0:T(256)S(1)} %get-tuple-element.40), channel_id=1, source_target_pairs={{0,8},{8,0},{16,24},{24,16},{1,9},{9,1},{17,25},{25,17},{2,10},{10... | collective-permute-start | bytes 3080 | tf_op jit(solution)/shard_map/ppermute | solution.py:93
  29.1 24.3 %collective-permute-start.8 = (s32[256]{0:T(256)S(1)}, s32[256]{0:T(256)S(1)}, u32[]{:S(2)}, u32[]{:S(2)}) collective-permute-start(s32[256]{0:T(256)S(1)} %get-tuple-element.39), channel_id=1, source_target_pairs={{0,16},{8,24},{16,0},{24,8},{1,17},{9,25},{17,1},{25,9},{2,18},{10... | collective-permute-start | bytes 3080 | tf_op jit(solution)/shard_map/ppermute | solution.py:93
  32.4 21.4 %collective-permute-start.9 = (s32[256]{0:T(256)S(1)}, s32[256]{0:T(256)S(1)}, u32[]{:S(2)}, u32[]{:S(2)}) collective-permute-start(s32[256]{0:T(256)S(1)} %get-tuple-element.38), channel_id=1, source_target_pairs={{0,24},{8,16},{16,8},{24,0},{1,25},{9,17},{17,9},{25,1},{2,26},{10... | collective-permute-start | bytes 3080 | tf_op jit(solution)/shard_map/ppermute | solution.py:93
  32.8 12.8 %collective-permute-start.5 = (bf16[512,128]{1,0:T(8,128)(2,1)S(1)}, bf16[512,128]{1,0:T(8,128)(2,1)S(1)}, u32[]{:S(2)}, u32[]{:S(2)}) collective-permute-start(bf16[512,128]{1,0:T(8,128)(2,1)S(1)} %collective-permute-done.3), channel_id=1, source_target_pairs={{2,0},{4,2},{6,4},{7,6},{5,7},{3,5},{1,3},{0,1},{10,8},{12,10},{14... | collective-permute-start | bytes 393224 | tf_op jit(solution)/shard_map/ppermute | solution.py:63
  36.5 5.6 %collective-permute-start.22 = (bf16[512,128]{1,0:T(8,128)(2,1)S(1)}, bf16[512,128]{1,0:T(8,128)(2,1)}, u32[]{:S(2)}, u32[]{:S(2)}) collective-permute-start(bf16[512,128]{1,0:T(8,128)(2,1)S(1)} %collective-permute-done.20), channel_id=1, source_target_pairs={{2,0},{4,2},{6,4},{7,6},{5,7},{3,5},{1,3},{0,1},{10,8},{12,10},{14... | collective-permute-start | bytes 393224 | tf_op jit(solution)/shard_map/ppermute | solution.py:63
  42.1 5.1 %collective-permute-start.21 = (bf16[512,128]{1,0:T(8,128)(2,1)S(1)}, bf16[512,128]{1,0:T(8,128)(2,1)}, u32[]{:S(2)}, u32[]{:S(2)}) collective-permute-start(bf16[512,128]{1,0:T(8,128)(2,1)S(1)} %collective-permute-done.19), channel_id=1, source_target_pairs={{0,2},{2,4},{4,6},{6,7},{7,5},{5,3},{3,1},{1,0},{8,10},{10,12},{12... | collective-permute-start | bytes 393224 | tf_op jit(solution)/shard_map/ppermute | solution.py:62
  45.6 8.2 %collective-permute-start.6 = (bf16[512,128]{1,0:T(8,128)(2,1)S(1)}, bf16[512,128]{1,0:T(8,128)(2,1)S(1)}, u32[]{:S(2)}, u32[]{:S(2)}) collective-permute-start(bf16[512,128]{1,0:T(8,128)(2,1)S(1)} %collective-permute-done.4), channel_id=1, source_target_pairs={{0,2},{2,4},{4,6},{6,7},{7,5},{5,3},{3,1},{1,0},{8,10},{10,12},{12... | collective-permute-start | bytes 393224 | tf_op jit(solution)/shard_map/ppermute | solution.py:62
  47.2 7.2 %collective-permute-start.10 = (bf16[512,128]{1,0:T(8,128)(2,1)S(1)}, bf16[512,128]{1,0:T(8,128)(2,1)S(1)}, u32[]{:S(2)}, u32[]{:S(2)}) collective-permute-start(bf16[512,128]{1,0:T(8,128)(2,1)S(1)} %collective-permute-done.5), channel_id=1, source_target_pairs={{2,0},{4,2},{6,4},{7,6},{5,7},{3,5},{1,3},{0,1},{10,8},{12,10},{14... | collective-permute-start | bytes 393224 | tf_op jit(solution)/shard_map/ppermute | solution.py:63
  51.8 6.5 %collective-permute-start.24 = (bf16[512,128]{1,0:T(8,128)(2,1)}, bf16[512,128]{1,0:T(8,128)(2,1)}, u32[]{:S(2)}, u32[]{:S(2)}) collective-permute-start(bf16[512,128]{1,0:T(8,128)(2,1)} %collective-permute-done.22), channel_id=1, source_target_pairs={{2,0},{4,2},{6,4},{7,6},{5,7},{3,5},{1,3},{0,1},{10,8},{12,10},{14... | collective-permute-start | bytes 393224 | tf_op jit(solution)/shard_map/ppermute | solution.py:63
  53.4 8.2 %collective-permute-start.23 = (bf16[512,128]{1,0:T(8,128)(2,1)}, bf16[512,128]{1,0:T(8,128)(2,1)}, u32[]{:S(2)}, u32[]{:S(2)}) collective-permute-start(bf16[512,128]{1,0:T(8,128)(2,1)} %collective-permute-done.21), channel_id=1, source_target_pairs={{0,2},{2,4},{4,6},{6,7},{7,5},{5,3},{3,1},{1,0},{8,10},{10,12},{12... | collective-permute-start | bytes 393224 | tf_op jit(solution)/shard_map/ppermute | solution.py:62
  54.4 11.1 %collective-permute-start.11 = (bf16[512,128]{1,0:T(8,128)(2,1)S(1)}, bf16[512,128]{1,0:T(8,128)(2,1)S(1)}, u32[]{:S(2)}, u32[]{:S(2)}) collective-permute-start(bf16[512,128]{1,0:T(8,128)(2,1)S(1)} %collective-permute-done.6), channel_id=1, source_target_pairs={{0,2},{2,4},{4,6},{6,7},{7,5},{5,3},{3,1},{1,0},{8,10},{10,12},{12... | collective-permute-start | bytes 393224 | tf_op jit(solution)/shard_map/ppermute | solution.py:62
  54.5 11.2 %collective-permute-start.12 = (bf16[512,128]{1,0:T(8,128)(2,1)S(1)}, bf16[512,128]{1,0:T(8,128)(2,1)S(1)}, u32[]{:S(2)}, u32[]{:S(2)}) collective-permute-start(bf16[512,128]{1,0:T(8,128)(2,1)S(1)} %collective-permute-done.10), channel_id=1, source_target_pairs={{2,0},{4,2},{6,4},{7,6},{5,7},{3,5},{1,3},{0,1},{10,8},{12,10},{14... | collective-permute-start | bytes 393224 | tf_op jit(solution)/shard_map/ppermute | solution.py:63
  58.2 11.1 %collective-permute-start.26 = (bf16[512,128]{1,0:T(8,128)(2,1)}, bf16[512,128]{1,0:T(8,128)(2,1)S(1)}, u32[]{:S(2)}, u32[]{:S(2)}) collective-permute-start(bf16[512,128]{1,0:T(8,128)(2,1)} %collective-permute-done.24), channel_id=1, source_target_pairs={{2,0},{4,2},{6,4},{7,6},{5,7},{3,5},{1,3},{0,1},{10,8},{12,10},{14... | collective-permute-start | bytes 393224 | tf_op jit(solution)/shard_map/ppermute | solution.py:63
  61.6 11.1 %collective-permute-start.25 = (bf16[512,128]{1,0:T(8,128)(2,1)}, bf16[512,128]{1,0:T(8,128)(2,1)S(1)}, u32[]{:S(2)}, u32[]{:S(2)}) collective-permute-start(bf16[512,128]{1,0:T(8,128)(2,1)} %collective-permute-done.23), channel_id=1, source_target_pairs={{0,2},{2,4},{4,6},{6,7},{7,5},{5,3},{3,1},{1,0},{8,10},{10,12},{12... | collective-permute-start | bytes 393224 | tf_op jit(solution)/shard_map/ppermute | solution.py:62
  65.5 11.1 %collective-permute-start.13 = (bf16[512,128]{1,0:T(8,128)(2,1)S(1)}, bf16[512,128]{1,0:T(8,128)(2,1)S(1)}, u32[]{:S(2)}, u32[]{:S(2)}) collective-permute-start(bf16[512,128]{1,0:T(8,128)(2,1)S(1)} %collective-permute-done.11), channel_id=1, source_target_pairs={{0,2},{2,4},{4,6},{6,7},{7,5},{5,3},{3,1},{1,0},{8,10},{10,12},{12... | collective-permute-start | bytes 393224 | tf_op jit(solution)/shard_map/ppermute | solution.py:62
  65.6 11.1 %collective-permute-start.14 = (bf16[512,128]{1,0:T(8,128)(2,1)S(1)}, bf16[512,128]{1,0:T(8,128)(2,1)S(1)}, u32[]{:S(2)}, u32[]{:S(2)}) collective-permute-start(bf16[512,128]{1,0:T(8,128)(2,1)S(1)} %collective-permute-done.12), channel_id=1, source_target_pairs={{2,0},{4,2},{6,4},{7,6},{5,7},{3,5},{1,3},{0,1},{10,8},{12,10},{14... | collective-permute-start | bytes 393224 | tf_op jit(solution)/shard_map/ppermute | solution.py:63
  69.3 11.1 %collective-permute-start.28 = (bf16[512,128]{1,0:T(8,128)(2,1)S(1)}, bf16[512,128]{1,0:T(8,128)(2,1)S(1)}, u32[]{:S(2)}, u32[]{:S(2)}) collective-permute-start(bf16[512,128]{1,0:T(8,128)(2,1)S(1)} %collective-permute-done.26), channel_id=1, source_target_pairs={{2,0},{4,2},{6,4},{7,6},{5,7},{3,5},{1,3},{0,1},{10,8},{12,10},{14... | collective-permute-start | bytes 393224 | tf_op jit(solution)/shard_map/ppermute | solution.py:63
  72.7 11.1 %collective-permute-start.27 = (bf16[512,128]{1,0:T(8,128)(2,1)S(1)}, bf16[512,128]{1,0:T(8,128)(2,1)S(1)}, u32[]{:S(2)}, u32[]{:S(2)}) collective-permute-start(bf16[512,128]{1,0:T(8,128)(2,1)S(1)} %collective-permute-done.25), channel_id=1, source_target_pairs={{0,2},{2,4},{4,6},{6,7},{7,5},{5,3},{3,1},{1,0},{8,10},{10,12},{12... | collective-permute-start | bytes 393224 | tf_op jit(solution)/shard_map/ppermute | solution.py:62
  76.6 11.3 %collective-permute-start.15 = (bf16[512,128]{1,0:T(8,128)(2,1)S(1)}, bf16[512,128]{1,0:T(8,128)(2,1)S(1)}, u32[]{:S(2)}, u32[]{:S(2)}) collective-permute-start(bf16[512,128]{1,0:T(8,128)(2,1)S(1)} %collective-permute-done.13), channel_id=1, source_target_pairs={{0,2},{2,4},{4,6},{6,7},{7,5},{5,3},{3,1},{1,0},{8,10},{10,12},{12... | collective-permute-start | bytes 393224 | tf_op jit(solution)/shard_map/ppermute | solution.py:62
  76.8 16.3 %collective-permute-start.16 = (bf16[512,128]{1,0:T(8,128)(2,1)S(1)}, bf16[512,128]{1,0:T(8,128)(2,1)S(1)}, u32[]{:S(2)}, u32[]{:S(2)}) collective-permute-start(bf16[512,128]{1,0:T(8,128)(2,1)S(1)} %collective-permute-done.14), channel_id=1, source_target_pairs={{2,0},{4,2},{6,4},{7,6},{5,7},{3,5},{1,3},{0,1},{10,8},{12,10},{14... | collective-permute-start | bytes 393224 | tf_op jit(solution)/shard_map/ppermute | solution.py:63
  80.4 10.9 %collective-permute-start.30 = (bf16[512,128]{1,0:T(8,128)(2,1)S(1)}, bf16[512,128]{1,0:T(8,128)(2,1)S(1)}, u32[]{:S(2)}, u32[]{:S(2)}) collective-permute-start(bf16[512,128]{1,0:T(8,128)(2,1)S(1)} %collective-permute-done.28), channel_id=1, source_target_pairs={{2,0},{4,2},{6,4},{7,6},{5,7},{3,5},{1,3},{0,1},{10,8},{12,10},{14... | collective-permute-start | bytes 393224 | tf_op jit(solution)/shard_map/ppermute | solution.py:63
  83.8 11.7 %collective-permute-start.29 = (bf16[512,128]{1,0:T(8,128)(2,1)S(1)}, bf16[512,128]{1,0:T(8,128)(2,1)S(1)}, u32[]{:S(2)}, u32[]{:S(2)}) collective-permute-start(bf16[512,128]{1,0:T(8,128)(2,1)S(1)} %collective-permute-done.27), channel_id=1, source_target_pairs={{0,2},{2,4},{4,6},{6,7},{7,5},{5,3},{3,1},{1,0},{8,10},{10,12},{12... | collective-permute-start | bytes 393224 | tf_op jit(solution)/shard_map/ppermute | solution.py:62
  97.9 9.3 %collective-permute-start.31 = (bf16[512,128]{0,1:T(8,128)(2,1)S(1)}, bf16[512,128]{0,1:T(8,128)(2,1)S(1)}, u32[]{:S(2)}, u32[]{:S(2)}) collective-permute-start(bf16[512,128]{0,1:T(8,128)(2,1)S(1)} %get-tuple-element.34), channel_id=1, source_target_pairs={{0,2},{2,4},{4,6},{6,7},{7,5},{5,3},{3,1},{1,0},{8,10},{10,12},{12... | collective-permute-start | bytes 393224 | tf_op jit(solution)/shard_map/ppermute | solution.py:62
  100.0 8.8 %collective-permute-start.32 = (bf16[512,128]{0,1:T(8,128)(2,1)}, bf16[512,128]{0,1:T(8,128)(2,1)}, u32[]{:S(2)}, u32[]{:S(2)}) collective-permute-start(bf16[512,128]{0,1:T(8,128)(2,1)} %get-tuple-element.35), channel_id=1, source_target_pairs={{2,0},{4,2},{6,4},{7,6},{5,7},{3,5},{1,3},{0,1},{10,8},{12,10},{14... | collective-permute-start | bytes 393224 | tf_op jit(solution)/shard_map/ppermute | solution.py:63
  102.0 10.3 %collective-permute-start.48 = (bf16[512,128]{0,1:T(8,128)(2,1)}, bf16[512,128]{0,1:T(8,128)(2,1)S(1)}, u32[]{:S(2)}, u32[]{:S(2)}) collective-permute-start(bf16[512,128]{0,1:T(8,128)(2,1)} %get-tuple-element.36), channel_id=1, source_target_pairs={{0,2},{2,4},{4,6},{6,7},{7,5},{5,3},{3,1},{1,0},{8,10},{10,12},{12... | collective-permute-start | bytes 393224 | tf_op jit(solution)/shard_map/ppermute | solution.py:62
  102.1 11.9 %collective-permute-start.49 = (bf16[512,128]{0,1:T(8,128)(2,1)}, bf16[512,128]{0,1:T(8,128)(2,1)}, u32[]{:S(2)}, u32[]{:S(2)}) collective-permute-start(bf16[512,128]{0,1:T(8,128)(2,1)} %get-tuple-element.37), channel_id=1, source_target_pairs={{2,0},{4,2},{6,4},{7,6},{5,7},{3,5},{1,3},{0,1},{10,8},{12,10},{14... | collective-permute-start | bytes 393224 | tf_op jit(solution)/shard_map/ppermute | solution.py:63
  107.2 12.0 %collective-permute-start.33 = (bf16[512,128]{0,1:T(8,128)(2,1)S(1)}, bf16[512,128]{0,1:T(8,128)(2,1)S(1)}, u32[]{:S(2)}, u32[]{:S(2)}) collective-permute-start(bf16[512,128]{0,1:T(8,128)(2,1)S(1)} %collective-permute-done.31), channel_id=1, source_target_pairs={{0,2},{2,4},{4,6},{6,7},{7,5},{5,3},{3,1},{1,0},{8,10},{10,12},{12... | collective-permute-start | bytes 393224 | tf_op jit(solution)/shard_map/ppermute | solution.py:62
  108.9 8.7 %collective-permute-start.34 = (bf16[512,128]{0,1:T(8,128)(2,1)}, bf16[512,128]{0,1:T(8,128)(2,1)S(1)}, u32[]{:S(2)}, u32[]{:S(2)}) collective-permute-start(bf16[512,128]{0,1:T(8,128)(2,1)} %collective-permute-done.32), channel_id=1, source_target_pairs={{2,0},{4,2},{6,4},{7,6},{5,7},{3,5},{1,3},{0,1},{10,8},{12,10},{14... | collective-permute-start | bytes 393224 | tf_op jit(solution)/shard_map/ppermute | solution.py:63
  112.4 11.9 %collective-permute-start.50 = (bf16[512,128]{0,1:T(8,128)(2,1)S(1)}, bf16[512,128]{0,1:T(8,128)(2,1)S(1)}, u32[]{:S(2)}, u32[]{:S(2)}) collective-permute-start(bf16[512,128]{0,1:T(8,128)(2,1)S(1)} %collective-permute-done.48), channel_id=1, source_target_pairs={{0,2},{2,4},{4,6},{6,7},{7,5},{5,3},{3,1},{1,0},{8,10},{10,12},{12... | collective-permute-start | bytes 393224 | tf_op jit(solution)/shard_map/ppermute | solution.py:62
  114.0 7.1 %collective-permute-start.51 = (bf16[512,128]{0,1:T(8,128)(2,1)}, bf16[512,128]{0,1:T(8,128)(2,1)S(1)}, u32[]{:S(2)}, u32[]{:S(2)}) collective-permute-start(bf16[512,128]{0,1:T(8,128)(2,1)} %collective-permute-done.49), channel_id=1, source_target_pairs={{2,0},{4,2},{6,4},{7,6},{5,7},{3,5},{1,3},{0,1},{10,8},{12,10},{14... | collective-permute-start | bytes 393224 | tf_op jit(solution)/shard_map/ppermute | solution.py:63
  117.6 10.3 %collective-permute-start.36 = (bf16[512,128]{0,1:T(8,128)(2,1)S(1)}, bf16[512,128]{0,1:T(8,128)(2,1)S(1)}, u32[]{:S(2)}, u32[]{:S(2)}) collective-permute-start(bf16[512,128]{0,1:T(8,128)(2,1)S(1)} %collective-permute-done.34), channel_id=1, source_target_pairs={{2,0},{4,2},{6,4},{7,6},{5,7},{3,5},{1,3},{0,1},{10,8},{12,10},{14... | collective-permute-start | bytes 393224 | tf_op jit(solution)/shard_map/ppermute | solution.py:63
  119.2 10.3 %collective-permute-start.35 = (bf16[512,128]{0,1:T(8,128)(2,1)S(1)}, bf16[512,128]{0,1:T(8,128)(2,1)S(1)}, u32[]{:S(2)}, u32[]{:S(2)}) collective-permute-start(bf16[512,128]{0,1:T(8,128)(2,1)S(1)} %collective-permute-done.33), channel_id=1, source_target_pairs={{0,2},{2,4},{4,6},{6,7},{7,5},{5,3},{3,1},{1,0},{8,10},{10,12},{12... | collective-permute-start | bytes 393224 | tf_op jit(solution)/shard_map/ppermute | solution.py:62
  121.2 10.3 %collective-permute-start.53 = (bf16[512,128]{0,1:T(8,128)(2,1)S(1)}, bf16[512,128]{0,1:T(8,128)(2,1)S(1)}, u32[]{:S(2)}, u32[]{:S(2)}) collective-permute-start(bf16[512,128]{0,1:T(8,128)(2,1)S(1)} %collective-permute-done.51), channel_id=1, source_target_pairs={{2,0},{4,2},{6,4},{7,6},{5,7},{3,5},{1,3},{0,1},{10,8},{12,10},{14... | collective-permute-start | bytes 393224 | tf_op jit(solution)/shard_map/ppermute | solution.py:63
  124.3 10.3 %collective-permute-start.52 = (bf16[512,128]{0,1:T(8,128)(2,1)S(1)}, bf16[512,128]{0,1:T(8,128)(2,1)S(1)}, u32[]{:S(2)}, u32[]{:S(2)}) collective-permute-start(bf16[512,128]{0,1:T(8,128)(2,1)S(1)} %collective-permute-done.50), channel_id=1, source_target_pairs={{0,2},{2,4},{4,6},{6,7},{7,5},{5,3},{3,1},{1,0},{8,10},{10,12},{12... | collective-permute-start | bytes 393224 | tf_op jit(solution)/shard_map/ppermute | solution.py:62
  127.8 10.2 %collective-permute-start.38 = (bf16[512,128]{0,1:T(8,128)(2,1)S(1)}, bf16[512,128]{0,1:T(8,128)(2,1)S(1)}, u32[]{:S(2)}, u32[]{:S(2)}) collective-permute-start(bf16[512,128]{0,1:T(8,128)(2,1)S(1)} %collective-permute-done.36), channel_id=1, source_target_pairs={{2,0},{4,2},{6,4},{7,6},{5,7},{3,5},{1,3},{0,1},{10,8},{12,10},{14... | collective-permute-start | bytes 393224 | tf_op jit(solution)/shard_map/ppermute | solution.py:63
  129.5 10.2 %collective-permute-start.37 = (bf16[512,128]{0,1:T(8,128)(2,1)S(1)}, bf16[512,128]{0,1:T(8,128)(2,1)S(1)}, u32[]{:S(2)}, u32[]{:S(2)}) collective-permute-start(bf16[512,128]{0,1:T(8,128)(2,1)S(1)} %collective-permute-done.35), channel_id=1, source_target_pairs={{0,2},{2,4},{4,6},{6,7},{7,5},{5,3},{3,1},{1,0},{8,10},{10,12},{12... | collective-permute-start | bytes 393224 | tf_op jit(solution)/shard_map/ppermute | solution.py:62
  131.4 10.2 %collective-permute-start.55 = (bf16[512,128]{0,1:T(8,128)(2,1)S(1)}, bf16[512,128]{0,1:T(8,128)(2,1)S(1)}, u32[]{:S(2)}, u32[]{:S(2)}) collective-permute-start(bf16[512,128]{0,1:T(8,128)(2,1)S(1)} %collective-permute-done.53), channel_id=1, source_target_pairs={{2,0},{4,2},{6,4},{7,6},{5,7},{3,5},{1,3},{0,1},{10,8},{12,10},{14... | collective-permute-start | bytes 393224 | tf_op jit(solution)/shard_map/ppermute | solution.py:63
  134.6 10.2 %collective-permute-start.54 = (bf16[512,128]{0,1:T(8,128)(2,1)S(1)}, bf16[512,128]{0,1:T(8,128)(2,1)S(1)}, u32[]{:S(2)}, u32[]{:S(2)}) collective-permute-start(bf16[512,128]{0,1:T(8,128)(2,1)S(1)} %collective-permute-done.52), channel_id=1, source_target_pairs={{0,2},{2,4},{4,6},{6,7},{7,5},{5,3},{3,1},{1,0},{8,10},{10,12},{12... | collective-permute-start | bytes 393224 | tf_op jit(solution)/shard_map/ppermute | solution.py:62
  138.1 8.0 %collective-permute-start.40 = (bf16[512,128]{0,1:T(8,128)(2,1)S(1)}, bf16[512,128]{0,1:T(8,128)(2,1)S(1)}, u32[]{:S(2)}, u32[]{:S(2)}) collective-permute-start(bf16[512,128]{0,1:T(8,128)(2,1)S(1)} %collective-permute-done.38), channel_id=1, source_target_pairs={{2,0},{4,2},{6,4},{7,6},{5,7},{3,5},{1,3},{0,1},{10,8},{12,10},{14... | collective-permute-start | bytes 393224 | tf_op jit(solution)/shard_map/ppermute | solution.py:63
  139.7 8.0 %collective-permute-start.39 = (bf16[512,128]{0,1:T(8,128)(2,1)S(1)}, bf16[512,128]{0,1:T(8,128)(2,1)S(1)}, u32[]{:S(2)}, u32[]{:S(2)}) collective-permute-start(bf16[512,128]{0,1:T(8,128)(2,1)S(1)} %collective-permute-done.37), channel_id=1, source_target_pairs={{0,2},{2,4},{4,6},{6,7},{7,5},{5,3},{3,1},{1,0},{8,10},{10,12},{12... | collective-permute-start | bytes 393224 | tf_op jit(solution)/shard_map/ppermute | solution.py:62
  141.7 6.9 %collective-permute-start.57 = (bf16[512,128]{0,1:T(8,128)(2,1)S(1)}, bf16[512,128]{0,1:T(8,128)(2,1)S(1)}, u32[]{:S(2)}, u32[]{:S(2)}) collective-permute-start(bf16[512,128]{0,1:T(8,128)(2,1)S(1)} %collective-permute-done.55), channel_id=1, source_target_pairs={{2,0},{4,2},{6,4},{7,6},{5,7},{3,5},{1,3},{0,1},{10,8},{12,10},{14... | collective-permute-start | bytes 393224 | tf_op jit(solution)/shard_map/ppermute | solution.py:63
  144.8 5.8 %collective-permute-start.56 = (bf16[512,128]{0,1:T(8,128)(2,1)S(1)}, bf16[512,128]{0,1:T(8,128)(2,1)S(1)}, u32[]{:S(2)}, u32[]{:S(2)}) collective-permute-start(bf16[512,128]{0,1:T(8,128)(2,1)S(1)} %collective-permute-done.54), channel_id=1, source_target_pairs={{0,2},{2,4},{4,6},{6,7},{7,5},{5,3},{3,1},{1,0},{8,10},{10,12},{12... | collective-permute-start | bytes 393224 | tf_op jit(solution)/shard_map/ppermute | solution.py:62
  146.1 5.7 %collective-permute-start.42 = (bf16[512,128]{0,1:T(8,128)(2,1)S(1)}, bf16[512,128]{0,1:T(8,128)(2,1)S(1)}, u32[]{:S(2)}, u32[]{:S(2)}) collective-permute-start(bf16[512,128]{0,1:T(8,128)(2,1)S(1)} %collective-permute-done.40), channel_id=1, source_target_pairs={{2,0},{4,2},{6,4},{7,6},{5,7},{3,5},{1,3},{0,1},{10,8},{12,10},{14... | collective-permute-start | bytes 393224 | tf_op jit(solution)/shard_map/ppermute | solution.py:63
  147.7 5.7 %collective-permute-start.41 = (bf16[512,128]{0,1:T(8,128)(2,1)S(1)}, bf16[512,128]{0,1:T(8,128)(2,1)S(1)}, u32[]{:S(2)}, u32[]{:S(2)}) collective-permute-start(bf16[512,128]{0,1:T(8,128)(2,1)S(1)} %collective-permute-done.39), channel_id=1, source_target_pairs={{0,2},{2,4},{4,6},{6,7},{7,5},{5,3},{3,1},{1,0},{8,10},{10,12},{12... | collective-permute-start | bytes 393224 | tf_op jit(solution)/shard_map/ppermute | solution.py:62
  148.6 5.7 %collective-permute-start.59 = (bf16[512,128]{0,1:T(8,128)(2,1)S(1)}, bf16[512,128]{0,1:T(8,128)(2,1)S(1)}, u32[]{:S(2)}, u32[]{:S(2)}) collective-permute-start(bf16[512,128]{0,1:T(8,128)(2,1)S(1)} %collective-permute-done.57), channel_id=1, source_target_pairs={{2,0},{4,2},{6,4},{7,6},{5,7},{3,5},{1,3},{0,1},{10,8},{12,10},{14... | collective-permute-start | bytes 393224 | tf_op jit(solution)/shard_map/ppermute | solution.py:63
  150.6 5.7 %collective-permute-start.58 = (bf16[512,128]{0,1:T(8,128)(2,1)S(1)}, bf16[512,128]{0,1:T(8,128)(2,1)S(1)}, u32[]{:S(2)}, u32[]{:S(2)}) collective-permute-start(bf16[512,128]{0,1:T(8,128)(2,1)S(1)} %collective-permute-done.56), channel_id=1, source_target_pairs={{0,2},{2,4},{4,6},{6,7},{7,5},{5,3},{3,1},{1,0},{8,10},{10,12},{12... | collective-permute-start | bytes 393224 | tf_op jit(solution)/shard_map/ppermute | solution.py:62
  151.8 5.9 %collective-permute-start.44 = (bf16[512,128]{0,1:T(8,128)(2,1)S(1)}, bf16[512,128]{0,1:T(8,128)(2,1)S(1)}, u32[]{:S(2)}, u32[]{:S(2)}) collective-permute-start(bf16[512,128]{0,1:T(8,128)(2,1)S(1)} %collective-permute-done.42), channel_id=1, source_target_pairs={{2,0},{4,2},{6,4},{7,6},{5,7},{3,5},{1,3},{0,1},{10,8},{12,10},{14... | collective-permute-start | bytes 393224 | tf_op jit(solution)/shard_map/ppermute | solution.py:63
  153.5 5.0 %collective-permute-start.43 = (bf16[512,128]{0,1:T(8,128)(2,1)S(1)}, bf16[512,128]{0,1:T(8,128)(2,1)S(1)}, u32[]{:S(2)}, u32[]{:S(2)}) collective-permute-start(bf16[512,128]{0,1:T(8,128)(2,1)S(1)} %collective-permute-done.41), channel_id=1, source_target_pairs={{0,2},{2,4},{4,6},{6,7},{7,5},{5,3},{3,1},{1,0},{8,10},{10,12},{12... | collective-permute-start | bytes 393224 | tf_op jit(solution)/shard_map/ppermute | solution.py:62
  154.3 5.3 %collective-permute-start.61 = (bf16[512,128]{0,1:T(8,128)(2,1)S(1)}, bf16[512,128]{0,1:T(8,128)(2,1)S(1)}, u32[]{:S(2)}, u32[]{:S(2)}) collective-permute-start(bf16[512,128]{0,1:T(8,128)(2,1)S(1)} %collective-permute-done.59), channel_id=1, source_target_pairs={{2,0},{4,2},{6,4},{7,6},{5,7},{3,5},{1,3},{0,1},{10,8},{12,10},{14... | collective-permute-start | bytes 393224 | tf_op jit(solution)/shard_map/ppermute | solution.py:63
  156.3 5.2 %collective-permute-start.60 = (bf16[512,128]{0,1:T(8,128)(2,1)S(1)}, bf16[512,128]{0,1:T(8,128)(2,1)S(1)}, u32[]{:S(2)}, u32[]{:S(2)}) collective-permute-start(bf16[512,128]{0,1:T(8,128)(2,1)S(1)} %collective-permute-done.58), channel_id=1, source_target_pairs={{0,2},{2,4},{4,6},{6,7},{7,5},{5,3},{3,1},{1,0},{8,10},{10,12},{12... | collective-permute-start | bytes 393224 | tf_op jit(solution)/shard_map/ppermute | solution.py:62
  163.3 4.3 %collective-permute-start.46 = (bf16[256,128]{1,0:T(8,128)(2,1)S(1)}, bf16[256,128]{1,0:T(8,128)(2,1)S(1)}, u32[]{:S(2)}, u32[]{:S(2)}) collective-permute-start(bf16[256,128]{1,0:T(8,128)(2,1)S(1)} %convolution_convert_fusion.5), channel_id=1, source_target_pairs={{0,16},{8,24},{16,0},{24,8},{1,17},{9,25},{17,1},{25,9},{2,18},{10... | collective-permute-start | bytes 196616 | tf_op jit(solution)/shard_map/ppermute | solution.py:115
  165.1 4.2 %collective-permute-start.45 = (bf16[256,128]{1,0:T(8,128)(2,1)S(1)}, bf16[256,128]{1,0:T(8,128)(2,1)S(1)}, u32[]{:S(2)}, u32[]{:S(2)}) collective-permute-start(bf16[256,128]{1,0:T(8,128)(2,1)S(1)} %convolution_convert_fusion.6), channel_id=1, source_target_pairs={{0,8},{8,0},{16,24},{24,16},{1,9},{9,1},{17,25},{25,17},{2,10},{10... | collective-permute-start | bytes 196616 | tf_op jit(solution)/shard_map/ppermute | solution.py:115
  165.9 6.5 %collective-permute-start.62 = (bf16[256,128]{1,0:T(8,128)(2,1)S(1)}, bf16[256,128]{1,0:T(8,128)(2,1)S(1)}, u32[]{:S(2)}, u32[]{:S(2)}) collective-permute-start(bf16[256,128]{1,0:T(8,128)(2,1)S(1)} %convolution_convert_fusion.2), channel_id=1, source_target_pairs={{0,8},{8,0},{16,24},{24,16},{1,9},{9,1},{17,25},{25,17},{2,10},{10... | collective-permute-start | bytes 196616 | tf_op jit(solution)/shard_map/ppermute | solution.py:115
  165.9 5.5 %collective-permute-start.63 = (bf16[256,128]{1,0:T(8,128)(2,1)S(1)}, bf16[256,128]{1,0:T(8,128)(2,1)S(1)}, u32[]{:S(2)}, u32[]{:S(2)}) collective-permute-start(bf16[256,128]{1,0:T(8,128)(2,1)S(1)} %convolution_convert_fusion.1), channel_id=1, source_target_pairs={{0,16},{8,24},{16,0},{24,8},{1,17},{9,25},{17,1},{25,9},{2,18},{10... | collective-permute-start | bytes 196616 | tf_op jit(solution)/shard_map/ppermute | solution.py:115
  167.7 4.5 %collective-permute-start.64 = (bf16[256,128]{1,0:T(8,128)(2,1)S(1)}, bf16[256,128]{1,0:T(8,128)(2,1)S(1)}, u32[]{:S(2)}, u32[]{:S(2)}) collective-permute-start(bf16[256,128]{1,0:T(8,128)(2,1)S(1)} %convolution_convert_fusion), channel_id=1, source_target_pairs={{0,24},{8,16},{16,8},{24,0},{1,25},{9,17},{17,9},{25,1},{2,26},{10... | collective-permute-start | bytes 196616 | tf_op jit(solution)/shard_map/ppermute | solution.py:115
  (10 other events, 210.2 us)
where the time goes:
time: 176 us; the launch traced here: 174 us
  matrix products  86.7 us (49%)
  starting transfers between devices  69.9 us (40%)
  local copies, waits for them, and re-layouts  6.9 us (4%)
  waiting for transfers between devices  6 us (3%)
  other arithmetic  2.2 us (1%)
  between operations  1.9 us (1%)
    dot_general x74, matrix products, dot(): return jnp.dot(a, b, preferred_element_type=jnp.float32)  86.7 us
    ppermute x28, starting transfers between devices, ring_products(): second = lax.ppermute(second, 'wide', backward)  41.7 us
    ppermute x28, starting transfers between devices, ring_products(): first = lax.ppermute(first, 'wide', onward)  22.3 us
    ppermute x6, starting transfers between devices, body(): lax.ppermute(values_out[delta], 'front', swaps[delta])  3.9 us
    unnamed x24, local copies, waits for them, and re-layouts  3.78 us
    ppermute x6, waiting for transfers between devices, body(): lax.ppermute(values_out[delta], 'front', swaps[delta])  3.58 us
  transfers between devices with their start and end apart: 65, of which 7 were waited for; matrix products, arithmetic and copies ran while one was open for 51% of the time, Pallas kernels for 0%

commit v1 on v0

--- a/solution.py
+++ b/solution.py
@@ -1,6 +1,9 @@
 import jax
 import jax.numpy as jnp
 from jax import lax
+from jax.experimental import pallas as pl
+from jax.experimental.layout import Layout, with_layout_constraint
+from jax.experimental.pallas import tpu as pltpu
 from jax.sharding import PartitionSpec as P
 
 CAPACITY = 2
@@ -27,8 +30,31 @@
     return result
 
 
+def row_major(array):
+    return with_layout_constraint(array, Layout(major_to_minor=tuple(range(array.ndim))))
+
+
 def dot(a, b):
-    return jnp.dot(a, b, preferred_element_type=jnp.float32)
+    return row_major(jnp.dot(a, b, preferred_element_type=jnp.float32))
+
+
+def held(matrix):
+    def kernel(source, target, semaphore):
+        copy = pltpu.make_async_copy(source, target, semaphore)
+        copy.start()
+        copy.wait()
+
+    return pl.pallas_call(
+        kernel,
+        out_shape=pltpu.VMEM(matrix.shape, matrix.dtype),
+        in_specs=[pl.BlockSpec(memory_space=pl.ANY)],
+        out_specs=pl.BlockSpec(memory_space=pltpu.VMEM),
+        scratch_shapes=[pltpu.SemaphoreType.DMA],
+        compiler_params=pltpu.CompilerParams(vmem_limit_bytes=2 << 20),
+        cost_estimate=pl.CostEstimate(
+            flops=0, bytes_accessed=2 * matrix.size * matrix.dtype.itemsize, transcendentals=0
+        ),
+    )(matrix)
 
 
 def body(inv_diag, below, rhs, tile_count, tile_owner, tile_rows, parent_rhs):
@@ -55,7 +81,7 @@
 
     def ring_products(matrix, blocks, aside=None):
         travelling = [(block[:half], block[half:]) for block in blocks]
-        totals = [part(matrix, wide_index, 0, block) for block in blocks]
+        total = part(matrix, wide_index, 0, jnp.concatenate(blocks, axis=1))
         extra = None
         for step in range(1, wide):
             for column, (first, second) in enumerate(travelling):
@@ -66,9 +92,17 @@
                 if aside and column == 0 and step == ROUTING_STEPS[1]:
                     first, extra = lax.optimization_barrier((first, extra))
                 travelling[column] = (first, second)
-                totals[column] = totals[column] + part(matrix, from_left[step], 0, first)
-                totals[column] = totals[column] + part(matrix, from_right[step], half, second)
-        return [total.astype(jnp.bfloat16) for total in totals], extra
+            if step < wide - 1:
+                firsts, seconds = [jnp.concatenate(pieces, axis=1) for pieces in zip(*travelling)]
+                total = total + part(matrix, from_left[step], 0, firsts)
+                total = total + part(matrix, from_right[step], half, seconds)
+        results = []
+        for column, (first, second) in enumerate(travelling):
+            piece = total[:, column * LANES:(column + 1) * LANES]
+            piece = piece + part(matrix, from_left[wide - 1], 0, first)
+            piece = piece + part(matrix, from_right[wide - 1], half, second)
+            results.append(piece.astype(jnp.bfloat16))
+        return results, extra
 
     swaps = [[(i, i ^ delta) for i in range(fronts)] for delta in range(fronts)]
 
@@ -102,11 +136,11 @@
 
     cuts = range(0, width, LANES)
     solved, (rows_in, picker, alive_rows) = ring_products(
-        inv_diag[0], [rhs[0][:, c:c + LANES] for c in cuts], routing
+        held(inv_diag[0]), [rhs[0][:, c:c + LANES] for c in cuts], routing
     )
     numbers = jnp.arange(parent_height, dtype=jnp.int32)[:, None]
 
-    updates, _ = ring_products(below[0], solved)
+    updates, _ = ring_products(held(below[0]), solved)
     results = []
     for c, update in zip(cuts, updates):
         update = jnp.where(alive_rows, update, jnp.zeros_like(update))

time: 176 us -> 159 us (0.903)
  matrix products: 86.7 us -> 39.4 us
  waiting for transfers between devices: 6 us -> 23.8 us
  local copies, waits for them, and re-layouts: 6.9 us -> 22.6 us
  starting transfers between devices: 69.9 us -> 65 us
  Pallas kernels: 0 us -> 2 us
    dot_general x74 -> x48, matrix products: 86.7 us -> 39.4 us  [dot(): return row_major(jnp.dot(a, b, preferred_element_type=jnp.float32))]
    ppermute x28, starting transfers between devices: 41.7 us -> 17.1 us  [ring_products(): second = lax.ppermute(second, 'wide', backward)]
    ppermute x28, starting transfers between devices: 22.3 us -> 43.4 us  [ring_products(): first = lax.ppermute(first, 'wide', onward)]
    unnamed x24 -> x33, local copies, waits for them, and re-layouts: 3.78 us -> 20.9 us
    ppermute x28, waiting for transfers between devices: 0.47 us -> 13.9 us  [ring_products(): second = lax.ppermute(second, 'wide', backward)]
    ppermute x28, waiting for transfers between devices: 1.95 us -> 5.26 us  [ring_products(): first = lax.ppermute(first, 'wide', onward)]
    pallas_call x0 -> x2, Pallas kernels: none -> 2 us  [held(): pl.pallas_call(kernel, out_shape=pltpu.VMEM(matrix.shape, matrix.dtype),...]
  transfers between devices with their start and end apart: 65 -> 65, of which waited for: 7 -> 23; matrix products, arithmetic and copies ran while one was open for 51% -> 24% of each run, Pallas kernels for 0% -> 1%
where the time goes in v1:
time: 159 us; the launch traced here: 158 us
  starting transfers between devices  65 us (41%)
  matrix products  39.4 us (25%)
  waiting for transfers between devices  23.8 us (15%)
  local copies, waits for them, and re-layouts  22.6 us (14%)
  other arithmetic  3.81 us (2%)
  Pallas kernels  2 us (1%)
  between operations  1.65 us (1%)
    ppermute x28, starting transfers between devices, ring_products(): first = lax.ppermute(first, 'wide', onward)  43.4 us
    dot_general x48, matrix products, dot(): return row_major(jnp.dot(a, b, preferred_element_type=jnp.float32))  39.4 us
    unnamed x33, local copies, waits for them, and re-layouts  20.9 us
    ppermute x28, starting transfers between devices, ring_products(): second = lax.ppermute(second, 'wide', backward)  17.1 us
    ppermute x28, waiting for transfers between devices, ring_products(): second = lax.ppermute(second, 'wide', backward)  13.9 us
    ppermute x28, waiting for transfers between devices, ring_products(): first = lax.ppermute(first, 'wide', onward)  5.26 us
    ppermute x6, waiting for transfers between devices, body(): lax.ppermute(values_out[delta], 'front', swaps[delta])  4.71 us
  transfers between devices with their start and end apart: 65, of which 23 were waited for; matrix products, arithmetic and copies ran while one was open for 24% of the time, Pallas kernels for 1%

profile of v1, /device:TPU:0, one launch (start us, length us, event | category | flops | bytes accessed | tf_op | source)
XLA Modules:
  0.0 158.3 jit_solution(4484349025953497620)
XLA Ops:
  0.6 1.1 fusion.240
  1.8 3.1 %collective-permute-start = (bf16[512,128]{1,0:T(8,128)(2,1)S(1)}, bf16[512,128]{1,0:T(8,128)(2,1)S(1)}, u32[]{:S(2)}, u32[]{:S(2)}) collective-permute-start(bf16[512,128]{1,0:T(8,128)(2,1)S(1)} %get-tuple-element.26), channel_id=1, source_target_pairs={{0,2},{2,4},{4,6},{6,7},{7,5},{5,3},{3,1},{1,0},{8,10},{10,12},{12... | collective-permute-start | bytes 393224 | tf_op jit(solution)/shard_map/ppermute | solution.py:88
  4.8 1.6 collective-permute-start.1
  6.9 5.8 %copy-done.2 = bf16[1,1024,8192]{2,1,0:T(8,128)(2,1)S(1)} copy-done((bf16[1,1024,8192]{2,1,0:T(8,128)(2,1)S(1)}, bf16[1,1024,8192]{2,1,0:T(8,128)(2,1)}, u32[]{:S(2)}) %copy-start.2) | copy-done | bytes 16777240
  12.7 1.2 shard_map.86
  13.8 5.8 %copy-done = bf16[1024,8192]{1,0:T(8,128)(2,1)} copy-done((bf16[1024,8192]{1,0:T(8,128)(2,1)}, bf16[1024,8192]{1,0:T(8,128)(2,1)S(1)}, u32[]{:S(2)}) %copy-start) | copy-done | bytes 16777240
  19.6 2.3 %fusion = f32[1024,256]{1,0:T(8,128)S(1)} fusion(bf16[1024,8192]{1,0:T(8,128)(2,1)} %copy-done, s32[]{:T(128)S(6)} %select_n.346, bf16[1,1024,256]{2,1,0:T(8,128)(2,1)S(1)} %copy-done.4), kind=kOutput, calls=%fused_computation.1 | convolution fusion | flops 536870912 | bytes 3670020 | tf_op jit(solution)/shard_map/dot_general | solution.py:38
  22.2 4.6 %copy-done.3 = bf16[1,768,8192]{2,1,0:T(8,128)(2,1)S(1)} copy-done((bf16[1,768,8192]{2,1,0:T(8,128)(2,1)S(1)}, bf16[1,768,8192]{2,1,0:T(8,128)(2,1)}, u32[]{:S(2)}) %copy-start.3) | copy-done | bytes 12582936
  27.7 4.6 %copy-done.1 = bf16[768,8192]{1,0:T(8,128)(2,1)} copy-done((bf16[768,8192]{1,0:T(8,128)(2,1)}, bf16[768,8192]{1,0:T(8,128)(2,1)S(1)}, u32[]{:S(2)}) %copy-start.1) | copy-done | bytes 12582936
  32.3 2.0 %collective-permute-start.4 = (bf16[512,128]{1,0:T(8,128)(2,1)S(1)}, bf16[512,128]{1,0:T(8,128)(2,1)S(1)}, u32[]{:S(2)}, u32[]{:S(2)}) collective-permute-start(bf16[512,128]{1,0:T(8,128)(2,1)S(1)} %collective-permute-done), channel_id=1, source_target_pairs={{0,2},{2,4},{4,6},{6,7},{7,5},{5,3},{3,1},{1,0},{8,10},{10,12},{12... | collective-permute-start | bytes 393224 | tf_op jit(solution)/shard_map/ppermute | solution.py:88
  34.3 1.9 %collective-permute-start.7 = (bf16[512,128]{1,0:T(8,128)(2,1)S(1)}, bf16[512,128]{1,0:T(8,128)(2,1)S(1)}, u32[]{:S(2)}, u32[]{:S(2)}) collective-permute-start(bf16[512,128]{1,0:T(8,128)(2,1)S(1)} %collective-permute-done.3), channel_id=1, source_target_pairs={{2,0},{4,2},{6,4},{7,6},{5,7},{3,5},{1,3},{0,1},{10,8},{12,10},{14... | collective-permute-start | bytes 393224 | tf_op jit(solution)/shard_map/ppermute | solution.py:89
  36.4 1.7 %convolution_add_fusion.6 = f32[1024,256]{1,0:T(8,128)S(1)} fusion(f32[1024,256]{1,0:T(8,128)S(1)} %fusion, bf16[1024,8192]{1,0:T(8,128)(2,1)} %copy-done, s32[]{:T(128)S(6)} %select_n.362, bf16[512,128]{1,0:T(8,128)(2,1)S(1)} %collective-permute-done.1, bf16[512,128]{1,0:T(8,128)(2,1)S(1)} %collective-permute-done), kind=kOutput, calls=%fused_computation.16 | convolution fusion | flops 269221888 | bytes 3407876 | tf_op jit(solution)/shard_map/dot_general | solution.py:38
  38.0 1.7 %convolution_add_fusion.5 = f32[1024,256]{1,0:T(8,128)S(1)} fusion(f32[1024,256]{1,0:T(8,128)S(1)} %convolution_add_fusion.6, bf16[1024,8192]{1,0:T(8,128)(2,1)} %copy-done, s32[]{:T(128)S(6)} %select_n.371, bf16[512,128]{1,0:T(8,128)(2,1)S(1)} %collective-permute-done.3, bf16[512,128]{1,0:T(8,128)(2,1)S(1)} %collective-permute-done.2), kind=kOutput, calls=%fused_computation.15 | convolution fusion | flops 269221888 | bytes 3407876 | tf_op jit(solution)/shard_map/dot_general | solution.py:38
  42.0 1.9 %collective-permute-start.14 = (s32[256]{0:T(256)S(1)}, s32[256]{0:T(256)S(1)}, u32[]{:S(2)}, u32[]{:S(2)}) collective-permute-start(s32[256]{0:T(256)S(1)} %get-tuple-element.35), channel_id=1, source_target_pairs={{0,16},{8,24},{16,0},{24,8},{1,17},{9,25},{17,1},{25,9},{2,18},{10... | collective-permute-start | bytes 3080 | tf_op jit(solution)/shard_map/ppermute | solution.py:127
  44.3 1.6 %collective-permute-start.8 = (bf16[512,128]{1,0:T(8,128)(2,1)S(1)}, bf16[512,128]{1,0:T(8,128)(2,1)S(1)}, u32[]{:S(2)}, u32[]{:S(2)}) collective-permute-start(bf16[512,128]{1,0:T(8,128)(2,1)S(1)} %collective-permute-done.4), channel_id=1, source_target_pairs={{0,2},{2,4},{4,6},{6,7},{7,5},{5,3},{3,1},{1,0},{8,10},{10,12},{12... | collective-permute-start | bytes 393224 | tf_op jit(solution)/shard_map/ppermute | solution.py:88
  46.4 1.7 %fusion.39 = f32[1024,256]{1,0:T(8,128)S(1)} fusion(bf16[1024,8192]{1,0:T(8,128)(2,1)} %copy-done, s32[]{:T(128)S(6)} %select_n.389, bf16[512,128]{1,0:T(8,128)(2,1)S(1)} %collective-permute-done.7, bf16[512,128]{1,0:T(8,128)(2,1)S(1)} %collective-permute-done.6), kind=kOutput, calls=%fused_computation.70 | convolution fusion | flops 268959744 | bytes 2359300 | tf_op jit(solution)/shard_map/dot_general | solution.py:38
  48.1 1.6 collective-permute-start.11
  49.7 1.7 %fusion.8 = f32[1024,256]{1,0:T(8,128)S(1)} fusion(f32[1024,256]{1,0:T(8,128)S(1)} %fusion.39, f32[1024,256]{1,0:T(8,128)S(1)} %convolution_add_fusion.5, bf16[1024,8192]{1,0:T(8,128)(2,1)} %copy-done, s32[]{:T(128)S(6)} %select_n.380, bf16[512,128]{1,0:T(8,128)(2,1)S(1)} %collective-permute-done.5, bf16[512,128]{1,0:T(8,128)(2,1)S(1)} %collective-permute-done.4), kind=kOutput, calls=%fused_computation.14 | convolution fusion | flops 269484032 | bytes 4456452 | tf_op jit(solution)/shard_map/dot_general | solution.py:38
  52.3 1.9 %collective-permute-done.11 = bf16[512,128]{1,0:T(8,128)(2,1)S(1)} collective-permute-done((bf16[512,128]{1,0:T(8,128)(2,1)S(1)}, bf16[512,128]{1,0:T(8,128)(2,1)S(1)}, u32[]{:S(2)}, u32[]{:S(2)}) %collective-permute-start.11) | collective-permute-done | bytes 131104 | tf_op jit(solution)/shard_map/ppermute | solution.py:89
  54.1 1.6 collective-permute-start.9
  55.7 1.7 %fusion.36 = f32[1024,256]{1,0:T(8,128)S(1)} fusion(bf16[1024,8192]{1,0:T(8,128)(2,1)} %copy-done, s32[]{:T(128)S(6)} %select_n.407, bf16[512,128]{1,0:T(8,128)(2,1)S(1)} %collective-permute-done.11, bf16[512,128]{1,0:T(8,128)(2,1)S(1)} %collective-permute-done.10), kind=kOutput, calls=%fused_computation.67 | convolution fusion | flops 268959744 | bytes 2359300 | tf_op jit(solution)/shard_map/dot_general | solution.py:38
  59.1 1.6 collective-permute-start.12
  60.7 1.7 %fusion.7 = f32[1024,256]{1,0:T(8,128)S(1)} fusion(f32[1024,256]{1,0:T(8,128)S(1)} %fusion.36, f32[1024,256]{1,0:T(8,128)S(1)} %fusion.8, bf16[1024,8192]{1,0:T(8,128)(2,1)} %copy-done, s32[]{:T(128)S(6)} %select_n.398, bf16[512,128]{1,0:T(8,128)(2,1)S(1)} %collective-permute-done.9, bf16[512,128]{1,0:T(8,128)(2,1)S(1)} %collective-permute-done.8), kind=kOutput, calls=%fused_computation.12 | convolution fusion | flops 269484032 | bytes 4456452 | tf_op jit(solution)/shard_map/dot_general | solution.py:38
  62.4 1.6 %collective-permute-start.16 = (bf16[512,128]{1,0:T(8,128)(2,1)S(1)}, bf16[512,128]{1,0:T(8,128)(2,1)S(1)}, u32[]{:S(2)}, u32[]{:S(2)}) collective-permute-start(bf16[512,128]{1,0:T(8,128)(2,1)S(1)} %collective-permute-done.9), channel_id=1, source_target_pairs={{0,2},{2,4},{4,6},{6,7},{7,5},{5,3},{3,1},{1,0},{8,10},{10,12},{12... | collective-permute-start | bytes 393224 | tf_op jit(solution)/shard_map/ppermute | solution.py:88
  64.0 1.4 collective-permute-done.12
  65.4 1.6 collective-permute-start.19
  68.4 1.7 %fusion.33 = f32[1024,256]{1,0:T(8,128)S(1)} fusion(bf16[1024,8192]{1,0:T(8,128)(2,1)} %copy-done, s32[]{:T(128)S(6)} %select_n.420, bf16[512,128]{1,0:T(8,128)(2,1)S(1)} %collective-permute-done.18, bf16[512,128]{1,0:T(8,128)(2,1)S(1)} %collective-permute-done.17), kind=kOutput, calls=%fused_computation.64 | convolution fusion | flops 268959744 | bytes 2359300 | tf_op jit(solution)/shard_map/dot_general | solution.py:38
  70.1 1.7 %fusion.6 = f32[1024,256]{1,0:T(8,128)S(1)} fusion(f32[1024,256]{1,0:T(8,128)S(1)} %fusion.33, f32[1024,256]{1,0:T(8,128)S(1)} %fusion.7, bf16[1024,8192]{1,0:T(8,128)(2,1)} %copy-done, s32[]{:T(128)S(6)} %select_n.416, bf16[512,128]{1,0:T(8,128)(2,1)S(1)} %collective-permute-done.16, bf16[512,128]{1,0:T(8,128)(2,1)S(1)} %collective-permute-done.12), kind=kOutput, calls=%fused_computation.10 | convolution fusion | flops 269484032 | bytes 4456452 | tf_op jit(solution)/shard_map/dot_general | solution.py:38
  71.8 1.1 collective-permute-start.20
  72.9 1.6 collective-permute-start.23
  75.9 1.7 %fusion.30 = f32[1024,256]{1,0:T(8,128)S(1)} fusion(bf16[1024,8192]{1,0:T(8,128)(2,1)} %copy-done, s32[]{:T(128)S(6)} %select_n.422, bf16[512,128]{1,0:T(8,128)(2,1)S(1)} %collective-permute-done.22, bf16[512,128]{1,0:T(8,128)(2,1)S(1)} %collective-permute-done.21), kind=kOutput, calls=%fused_computation.61 | convolution fusion | flops 268959744 | bytes 2359300 | tf_op jit(solution)/shard_map/dot_general | solution.py:38
  77.6 1.3 collective-permute-start.24
  78.9 1.7 %fusion.5 = f32[1024,256]{1,0:T(8,128)S(1)} fusion(f32[1024,256]{1,0:T(8,128)S(1)} %fusion.30, f32[1024,256]{1,0:T(8,128)S(1)} %fusion.6, bf16[1024,8192]{1,0:T(8,128)(2,1)} %copy-done, s32[]{:T(128)S(6)} %select_n.421, bf16[512,128]{1,0:T(8,128)(2,1)S(1)} %collective-permute-done.20, bf16[512,128]{1,0:T(8,128)(2,1)S(1)} %collective-permute-done.19), kind=kOutput, calls=%fused_computation.8 | convolution fusion | flops 269484032 | bytes 4456452 | tf_op jit(solution)/shard_map/dot_general | solution.py:38
  80.6 1.6 %collective-permute-start.27 = (bf16[512,128]{1,0:T(8,128)(2,1)S(1)}, bf16[512,128]{1,0:T(8,128)(2,1)S(1)}, u32[]{:S(2)}, u32[]{:S(2)}) collective-permute-start(bf16[512,128]{1,0:T(8,128)(2,1)S(1)} %collective-permute-done.23), channel_id=1, source_target_pairs={{0,2},{2,4},{4,6},{6,7},{7,5},{5,3},{3,1},{1,0},{8,10},{10,12},{12... | collective-permute-start | bytes 393224 | tf_op jit(solution)/shard_map/ppermute | solution.py:88
  83.5 1.7 %fusion.27 = f32[1024,256]{1,0:T(8,128)S(1)} fusion(bf16[1024,8192]{1,0:T(8,128)(2,1)} %copy-done, s32[]{:T(128)S(6)} %select_n.424, bf16[512,128]{1,0:T(8,128)(2,1)S(1)} %collective-permute-done.26, bf16[512,128]{1,0:T(8,128)(2,1)S(1)} %collective-permute-done.25), kind=kOutput, calls=%fused_computation.58 | convolution fusion | flops 268959744 | bytes 2359300 | tf_op jit(solution)/shard_map/dot_general | solution.py:38
  85.1 1.5 collective-permute-start.29
  86.6 1.7 %fusion.4 = f32[1024,256]{1,0:T(8,128)S(1)} fusion(f32[1024,256]{1,0:T(8,128)S(1)} %fusion.27, f32[1024,256]{1,0:T(8,128)S(1)} %fusion.5, bf16[1024,8192]{1,0:T(8,128)(2,1)} %copy-done, s32[]{:T(128)S(6)} %select_n.423, bf16[512,128]{1,0:T(8,128)(2,1)S(1)} %collective-permute-done.24, bf16[512,128]{1,0:T(8,128)(2,1)S(1)} %collective-permute-done.23), kind=kOutput, calls=%fused_computation.6 | convolution fusion | flops 269484032 | bytes 4456452 | tf_op jit(solution)/shard_map/dot_general | solution.py:38
  88.3 1.7 %fusion.48 = f32[1024,128]{1,0:T(8,128)S(1)} fusion(bf16[512,128]{1,0:T(8,128)(2,1)S(1)} %collective-permute-done.27, bf16[1024,8192]{1,0:T(8,128)(2,1)} %copy-done, s32[]{:T(128)S(6)} %select_n.425), kind=kOutput, calls=%fused_computation.79 | convolution fusion | flops 134217728 | bytes 1703940 | tf_op jit(solution)/shard_map/dot_general | solution.py:38
  90.0 1.8 %fusion.44 = f32[1024,128]{1,0:T(8,128)S(1)} fusion(bf16[512,128]{1,0:T(8,128)(2,1)S(1)} %collective-permute-done.30, bf16[1024,8192]{1,0:T(8,128)(2,1)} %copy-done, s32[]{:T(128)S(6)} %select_n.426), kind=kOutput, calls=%fused_computation.75 | convolution fusion | flops 134217728 | bytes 1703940 | tf_op jit(solution)/shard_map/dot_general | solution.py:38
  91.8 1.7 %fusion.16 = bf16[1024,128]{1,0:T(8,128)(2,1)S(1)} fusion(bf16[512,128]{1,0:T(8,128)(2,1)S(1)} %collective-permute-done.28, bf16[1024,8192]{1,0:T(8,128)(2,1)} %copy-done, s32[]{:T(128)S(6)} %select_n.426, f32[1024,128]{1,0:T(8,128)S(1)} %fusion.48, f32[1024,256]{1,0:T(8,128)S(1)} %fusion.4), kind=kOutput, calls=%fused_computation.33 | convolution fusion | flops 134610944 | bytes 2490372 | tf_op jit(solution)/shard_map/dot_general | solution.py:38
  93.5 1.7 %fusion.15 = bf16[1024,128]{1,0:T(8,128)(2,1)S(1)} fusion(f32[1024,128]{1,0:T(8,128)S(1)} %fusion.44, bf16[512,128]{1,0:T(8,128)(2,1)S(1)} %collective-permute-done.29, bf16[1024,8192]{1,0:T(8,128)(2,1)} %copy-done, s32[]{:T(128)S(6)} %select_n.425, f32[1024,256]{1,0:T(8,128)S(1)} %fusion.4), kind=kOutput, calls=%fused_computation.32 | convolution fusion | flops 134610944 | bytes 2490372 | tf_op jit(solution)/shard_map/dot_general | solution.py:38
  96.0 1.9 %collective-permute-start.31 = (bf16[512,128]{1,0:T(8,128)(2,1)S(1)}, bf16[512,128]{1,0:T(8,128)(2,1)S(1)}, u32[]{:S(2)}, u32[]{:S(2)}) collective-permute-start(bf16[512,128]{1,0:T(8,128)(2,1)S(1)} %get-tuple-element.30), channel_id=1, source_target_pairs={{0,2},{2,4},{4,6},{6,7},{7,5},{5,3},{3,1},{1,0},{8,10},{10,12},{12... | collective-permute-start | bytes 393224 | tf_op jit(solution)/shard_map/ppermute | solution.py:88
  98.0 2.0 %collective-permute-start.32 = (bf16[512,128]{1,0:T(8,128)(2,1)S(1)}, bf16[512,128]{1,0:T(8,128)(2,1)S(1)}, u32[]{:S(2)}, u32[]{:S(2)}) collective-permute-start(bf16[512,128]{1,0:T(8,128)(2,1)S(1)} %get-tuple-element.32), channel_id=1, source_target_pairs={{0,2},{2,4},{4,6},{6,7},{7,5},{5,3},{3,1},{1,0},{8,10},{10,12},{12... | collective-permute-start | bytes 393224 | tf_op jit(solution)/shard_map/ppermute | solution.py:88
  101.0 1.9 %collective-permute-start.35 = (bf16[512,128]{1,0:T(8,128)(2,1)S(1)}, bf16[512,128]{1,0:T(8,128)(2,1)S(1)}, u32[]{:S(2)}, u32[]{:S(2)}) collective-permute-start(bf16[512,128]{1,0:T(8,128)(2,1)S(1)} %collective-permute-done.31), channel_id=1, source_target_pairs={{0,2},{2,4},{4,6},{6,7},{7,5},{5,3},{3,1},{1,0},{8,10},{10,12},{12... | collective-permute-start | bytes 393224 | tf_op jit(solution)/shard_map/ppermute | solution.py:88
  102.9 2.0 %collective-permute-start.36 = (bf16[512,128]{1,0:T(8,128)(2,1)S(1)}, bf16[512,128]{1,0:T(8,128)(2,1)S(1)}, u32[]{:S(2)}, u32[]{:S(2)}) collective-permute-start(bf16[512,128]{1,0:T(8,128)(2,1)S(1)} %collective-permute-done.32), channel_id=1, source_target_pairs={{0,2},{2,4},{4,6},{6,7},{7,5},{5,3},{3,1},{1,0},{8,10},{10,12},{12... | collective-permute-start | bytes 393224 | tf_op jit(solution)/shard_map/ppermute | solution.py:88
  106.2 2.8 %collective-permute-done.34 = bf16[512,128]{1,0:T(8,128)(2,1)S(1)} collective-permute-done((bf16[512,128]{1,0:T(8,128)(2,1)S(1)}, bf16[512,128]{1,0:T(8,128)(2,1)S(1)}, u32[]{:S(2)}, u32[]{:S(2)}) %collective-permute-start.34) | collective-permute-done | bytes 131104 | tf_op jit(solution)/shard_map/ppermute | solution.py:89
  109.4 2.7 %collective-permute-done.37 = bf16[512,128]{1,0:T(8,128)(2,1)S(1)} collective-permute-done((bf16[512,128]{1,0:T(8,128)(2,1)S(1)}, bf16[512,128]{1,0:T(8,128)(2,1)S(1)}, u32[]{:S(2)}, u32[]{:S(2)}) %collective-permute-start.37) | collective-permute-done | bytes 131104 | tf_op jit(solution)/shard_map/ppermute | solution.py:89
  112.6 2.3 %collective-permute-done.38 = bf16[512,128]{1,0:T(8,128)(2,1)S(1)} collective-permute-done((bf16[512,128]{1,0:T(8,128)(2,1)S(1)}, bf16[512,128]{1,0:T(8,128)(2,1)S(1)}, u32[]{:S(2)}, u32[]{:S(2)}) %collective-permute-start.38) | collective-permute-done | bytes 131104 | tf_op jit(solution)/shard_map/ppermute | solution.py:89
  115.3 1.6 %collective-permute-start.39 = (bf16[512,128]{1,0:T(8,128)(2,1)S(1)}, bf16[512,128]{1,0:T(8,128)(2,1)S(1)}, u32[]{:S(2)}, u32[]{:S(2)}) collective-permute-start(bf16[512,128]{1,0:T(8,128)(2,1)S(1)} %collective-permute-done.35), channel_id=1, source_target_pairs={{0,2},{2,4},{4,6},{6,7},{7,5},{5,3},{3,1},{1,0},{8,10},{10,12},{12... | collective-permute-start | bytes 393224 | tf_op jit(solution)/shard_map/ppermute | solution.py:88
  118.5 1.3 collective-permute-start.45
  119.8 1.5 collective-permute-done.42
  121.8 1.5 collective-permute-start.43
  124.9 1.3 collective-permute-start.49
  126.5 1.3 collective-permute-start.50
  128.2 1.4 collective-permute-start.47
  131.0 1.4 collective-permute-start.48
  134.0 1.5 collective-permute-start.51
  136.0 1.4 collective-permute-start.52
  139.0 1.5 collective-permute-start.55
  141.4 1.6 collective-permute-start.60
  148.9 2.1 %collective-permute-start.59 = (bf16[256,128]{1,0:T(8,128)(2,1)S(1)}, bf16[256,128]{1,0:T(8,128)(2,1)S(1)}, u32[]{:S(2)}, u32[]{:S(2)}) collective-permute-start(bf16[256,128]{1,0:T(8,128)(2,1)S(1)} %convolution_convert_fusion.4), channel_id=1, source_target_pairs={{0,24},{8,16},{16,8},{24,0},{1,25},{9,17},{17,9},{25,1},{2,26},{10... | collective-permute-start | bytes 196616 | tf_op jit(solution)/shard_map/ppermute | solution.py:149
  151.3 2.0 %collective-permute-done.58 = bf16[256,128]{1,0:T(8,128)(2,1)S(1)} collective-permute-done((bf16[256,128]{1,0:T(8,128)(2,1)S(1)}, bf16[256,128]{1,0:T(8,128)(2,1)S(1)}, u32[]{:S(2)}, u32[]{:S(2)}) %collective-permute-start.58) | collective-permute-done | bytes 65568 | tf_op jit(solution)/shard_map/ppermute | solution.py:149
  154.1 1.5 collective-permute-done.63
  155.8 1.2 collective-permute-done.64
  (168 shorter events, 34.6 us)
Async XLA Ops:
  1.8 30.5 %collective-permute-start = (bf16[512,128]{1,0:T(8,128)(2,1)S(1)}, bf16[512,128]{1,0:T(8,128)(2,1)S(1)}, u32[]{:S(2)}, u32[]{:S(2)}) collective-permute-start(bf16[512,128]{1,0:T(8,128)(2,1)S(1)} %get-tuple-element.26), channel_id=1, source_target_pairs={{0,2},{2,4},{4,6},{6,7},{7,5},{5,3},{3,1},{1,0},{8,10},{10,12},{12... | collective-permute-start | bytes 393224 | tf_op jit(solution)/shard_map/ppermute | solution.py:88
  4.8 31.4 %collective-permute-start.1 = (bf16[512,128]{1,0:T(8,128)(2,1)S(1)}, bf16[512,128]{1,0:T(8,128)(2,1)S(1)}, u32[]{:S(2)}, u32[]{:S(2)}) collective-permute-start(bf16[512,128]{1,0:T(8,128)(2,1)S(1)} %get-tuple-element.28), channel_id=1, source_target_pairs={{0,2},{2,4},{4,6},{6,7},{7,5},{5,3},{3,1},{1,0},{8,10},{10,12},{12... | collective-permute-start | bytes 393224 | tf_op jit(solution)/shard_map/ppermute | solution.py:88
  6.4 27.8 %collective-permute-start.2 = (bf16[512,128]{1,0:T(8,128)(2,1)S(1)}, bf16[512,128]{1,0:T(8,128)(2,1)S(1)}, u32[]{:S(2)}, u32[]{:S(2)}) collective-permute-start(bf16[512,128]{1,0:T(8,128)(2,1)S(1)} %get-tuple-element.27), channel_id=1, source_target_pairs={{2,0},{4,2},{6,4},{7,6},{5,7},{3,5},{1,3},{0,1},{10,8},{12,10},{14... | collective-permute-start | bytes 393224 | tf_op jit(solution)/shard_map/ppermute | solution.py:89
  6.9 27.4 %collective-permute-start.3 = (bf16[512,128]{1,0:T(8,128)(2,1)S(1)}, bf16[512,128]{1,0:T(8,128)(2,1)S(1)}, u32[]{:S(2)}, u32[]{:S(2)}) collective-permute-start(bf16[512,128]{1,0:T(8,128)(2,1)S(1)} %get-tuple-element.29), channel_id=1, source_target_pairs={{2,0},{4,2},{6,4},{7,6},{5,7},{3,5},{1,3},{0,1},{10,8},{12,10},{14... | collective-permute-start | bytes 393224 | tf_op jit(solution)/shard_map/ppermute | solution.py:89
  32.3 7.4 %collective-permute-start.4 = (bf16[512,128]{1,0:T(8,128)(2,1)S(1)}, bf16[512,128]{1,0:T(8,128)(2,1)S(1)}, u32[]{:S(2)}, u32[]{:S(2)}) collective-permute-start(bf16[512,128]{1,0:T(8,128)(2,1)S(1)} %collective-permute-done), channel_id=1, source_target_pairs={{0,2},{2,4},{4,6},{6,7},{7,5},{5,3},{3,1},{1,0},{8,10},{10,12},{12... | collective-permute-start | bytes 393224 | tf_op jit(solution)/shard_map/ppermute | solution.py:88
  34.3 10.1 %collective-permute-start.6 = (bf16[512,128]{1,0:T(8,128)(2,1)S(1)}, bf16[512,128]{1,0:T(8,128)(2,1)S(1)}, u32[]{:S(2)}, u32[]{:S(2)}) collective-permute-start(bf16[512,128]{1,0:T(8,128)(2,1)S(1)} %collective-permute-done.2), channel_id=1, source_target_pairs={{2,0},{4,2},{6,4},{7,6},{5,7},{3,5},{1,3},{0,1},{10,8},{12,10},{14... | collective-permute-start | bytes 393224 | tf_op jit(solution)/shard_map/ppermute | solution.py:89
  34.3 11.7 %collective-permute-start.7 = (bf16[512,128]{1,0:T(8,128)(2,1)S(1)}, bf16[512,128]{1,0:T(8,128)(2,1)S(1)}, u32[]{:S(2)}, u32[]{:S(2)}) collective-permute-start(bf16[512,128]{1,0:T(8,128)(2,1)S(1)} %collective-permute-done.3), channel_id=1, source_target_pairs={{2,0},{4,2},{6,4},{7,6},{5,7},{3,5},{1,3},{0,1},{10,8},{12,10},{14... | collective-permute-start | bytes 393224 | tf_op jit(solution)/shard_map/ppermute | solution.py:89
  36.2 11.8 %collective-permute-start.5 = (bf16[512,128]{1,0:T(8,128)(2,1)S(1)}, bf16[512,128]{1,0:T(8,128)(2,1)S(1)}, u32[]{:S(2)}, u32[]{:S(2)}) collective-permute-start(bf16[512,128]{1,0:T(8,128)(2,1)S(1)} %collective-permute-done.1), channel_id=1, source_target_pairs={{0,2},{2,4},{4,6},{6,7},{7,5},{5,3},{3,1},{1,0},{8,10},{10,12},{12... | collective-permute-start | bytes 393224 | tf_op jit(solution)/shard_map/ppermute | solution.py:88
  42.0 15.4 %collective-permute-start.13 = (s32[256]{0:T(256)S(1)}, s32[256]{0:T(256)S(1)}, u32[]{:S(2)}, u32[]{:S(2)}) collective-permute-start(s32[256]{0:T(256)S(1)} %get-tuple-element.36), channel_id=1, source_target_pairs={{0,8},{8,0},{16,24},{24,16},{1,9},{9,1},{17,25},{25,17},{2,10},{10... | collective-permute-start | bytes 3080 | tf_op jit(solution)/shard_map/ppermute | solution.py:127
  42.0 20.3 %collective-permute-start.14 = (s32[256]{0:T(256)S(1)}, s32[256]{0:T(256)S(1)}, u32[]{:S(2)}, u32[]{:S(2)}) collective-permute-start(s32[256]{0:T(256)S(1)} %get-tuple-element.35), channel_id=1, source_target_pairs={{0,16},{8,24},{16,0},{24,8},{1,17},{9,25},{17,1},{25,9},{2,18},{10... | collective-permute-start | bytes 3080 | tf_op jit(solution)/shard_map/ppermute | solution.py:127
  44.3 13.6 %collective-permute-start.8 = (bf16[512,128]{1,0:T(8,128)(2,1)S(1)}, bf16[512,128]{1,0:T(8,128)(2,1)S(1)}, u32[]{:S(2)}, u32[]{:S(2)}) collective-permute-start(bf16[512,128]{1,0:T(8,128)(2,1)S(1)} %collective-permute-done.4), channel_id=1, source_target_pairs={{0,2},{2,4},{4,6},{6,7},{7,5},{5,3},{3,1},{1,0},{8,10},{10,12},{12... | collective-permute-start | bytes 393224 | tf_op jit(solution)/shard_map/ppermute | solution.py:88
  46.0 6.3 %collective-permute-start.10 = (bf16[512,128]{1,0:T(8,128)(2,1)S(1)}, bf16[512,128]{1,0:T(8,128)(2,1)S(1)}, u32[]{:S(2)}, u32[]{:S(2)}) collective-permute-start(bf16[512,128]{1,0:T(8,128)(2,1)S(1)} %collective-permute-done.6), channel_id=1, source_target_pairs={{2,0},{4,2},{6,4},{7,6},{5,7},{3,5},{1,3},{0,1},{10,8},{12,10},{14... | collective-permute-start | bytes 393224 | tf_op jit(solution)/shard_map/ppermute | solution.py:89
  48.1 6.0 %collective-permute-start.11 = (bf16[512,128]{1,0:T(8,128)(2,1)S(1)}, bf16[512,128]{1,0:T(8,128)(2,1)S(1)}, u32[]{:S(2)}, u32[]{:S(2)}) collective-permute-start(bf16[512,128]{1,0:T(8,128)(2,1)S(1)} %collective-permute-done.7), channel_id=1, source_target_pairs={{2,0},{4,2},{6,4},{7,6},{5,7},{3,5},{1,3},{0,1},{10,8},{12,10},{14... | collective-permute-start | bytes 393224 | tf_op jit(solution)/shard_map/ppermute | solution.py:89
  52.3 11.7 %collective-permute-start.15 = (s32[256]{0:T(256)S(1)}, s32[256]{0:T(256)S(1)}, u32[]{:S(2)}, u32[]{:S(2)}) collective-permute-start(s32[256]{0:T(256)S(1)} %get-tuple-element.34), channel_id=1, source_target_pairs={{0,24},{8,16},{16,8},{24,0},{1,25},{9,17},{17,9},{25,1},{2,26},{10... | collective-permute-start | bytes 3080 | tf_op jit(solution)/shard_map/ppermute | solution.py:127
  54.1 5.0 %collective-permute-start.9 = (bf16[512,128]{1,0:T(8,128)(2,1)S(1)}, bf16[512,128]{1,0:T(8,128)(2,1)S(1)}, u32[]{:S(2)}, u32[]{:S(2)}) collective-permute-start(bf16[512,128]{1,0:T(8,128)(2,1)S(1)} %collective-permute-done.5), channel_id=1, source_target_pairs={{0,2},{2,4},{4,6},{6,7},{7,5},{5,3},{3,1},{1,0},{8,10},{10,12},{12... | collective-permute-start | bytes 393224 | tf_op jit(solution)/shard_map/ppermute | solution.py:88
  57.4 9.6 %collective-permute-start.17 = (bf16[512,128]{1,0:T(8,128)(2,1)S(1)}, bf16[512,128]{1,0:T(8,128)(2,1)S(1)}, u32[]{:S(2)}, u32[]{:S(2)}) collective-permute-start(bf16[512,128]{1,0:T(8,128)(2,1)S(1)} %collective-permute-done.10), channel_id=1, source_target_pairs={{2,0},{4,2},{6,4},{7,6},{5,7},{3,5},{1,3},{0,1},{10,8},{12,10},{14... | collective-permute-start | bytes 393224 | tf_op jit(solution)/shard_map/ppermute | solution.py:89
  57.9 9.5 %collective-permute-start.18 = (bf16[512,128]{1,0:T(8,128)(2,1)S(1)}, bf16[512,128]{1,0:T(8,128)(2,1)S(1)}, u32[]{:S(2)}, u32[]{:S(2)}) collective-permute-start(bf16[512,128]{1,0:T(8,128)(2,1)S(1)} %collective-permute-done.11), channel_id=1, source_target_pairs={{2,0},{4,2},{6,4},{7,6},{5,7},{3,5},{1,3},{0,1},{10,8},{12,10},{14... | collective-permute-start | bytes 393224 | tf_op jit(solution)/shard_map/ppermute | solution.py:89
  59.1 6.3 %collective-permute-start.12 = (bf16[512,128]{1,0:T(8,128)(2,1)S(1)}, bf16[512,128]{1,0:T(8,128)(2,1)S(1)}, u32[]{:S(2)}, u32[]{:S(2)}) collective-permute-start(bf16[512,128]{1,0:T(8,128)(2,1)S(1)} %collective-permute-done.8), channel_id=1, source_target_pairs={{0,2},{2,4},{4,6},{6,7},{7,5},{5,3},{3,1},{1,0},{8,10},{10,12},{12... | collective-permute-start | bytes 393224 | tf_op jit(solution)/shard_map/ppermute | solution.py:88
  62.4 7.7 %collective-permute-start.16 = (bf16[512,128]{1,0:T(8,128)(2,1)S(1)}, bf16[512,128]{1,0:T(8,128)(2,1)S(1)}, u32[]{:S(2)}, u32[]{:S(2)}) collective-permute-start(bf16[512,128]{1,0:T(8,128)(2,1)S(1)} %collective-permute-done.9), channel_id=1, source_target_pairs={{0,2},{2,4},{4,6},{6,7},{7,5},{5,3},{3,1},{1,0},{8,10},{10,12},{12... | collective-permute-start | bytes 393224 | tf_op jit(solution)/shard_map/ppermute | solution.py:88
  65.4 7.5 %collective-permute-start.19 = (bf16[512,128]{1,0:T(8,128)(2,1)S(1)}, bf16[512,128]{1,0:T(8,128)(2,1)S(1)}, u32[]{:S(2)}, u32[]{:S(2)}) collective-permute-start(bf16[512,128]{1,0:T(8,128)(2,1)S(1)} %collective-permute-done.12), channel_id=1, source_target_pairs={{0,2},{2,4},{4,6},{6,7},{7,5},{5,3},{3,1},{1,0},{8,10},{10,12},{12... | collective-permute-start | bytes 393224 | tf_op jit(solution)/shard_map/ppermute | solution.py:88
  67.0 7.5 %collective-permute-start.21 = (bf16[512,128]{1,0:T(8,128)(2,1)S(1)}, bf16[512,128]{1,0:T(8,128)(2,1)S(1)}, u32[]{:S(2)}, u32[]{:S(2)}) collective-permute-start(bf16[512,128]{1,0:T(8,128)(2,1)S(1)} %collective-permute-done.17), channel_id=1, source_target_pairs={{2,0},{4,2},{6,4},{7,6},{5,7},{3,5},{1,3},{0,1},{10,8},{12,10},{14... | collective-permute-start | bytes 393224 | tf_op jit(solution)/shard_map/ppermute | solution.py:89
  67.4 7.5 %collective-permute-start.22 = (bf16[512,128]{1,0:T(8,128)(2,1)S(1)}, bf16[512,128]{1,0:T(8,128)(2,1)S(1)}, u32[]{:S(2)}, u32[]{:S(2)}) collective-permute-start(bf16[512,128]{1,0:T(8,128)(2,1)S(1)} %collective-permute-done.18), channel_id=1, source_target_pairs={{2,0},{4,2},{6,4},{7,6},{5,7},{3,5},{1,3},{0,1},{10,8},{12,10},{14... | collective-permute-start | bytes 393224 | tf_op jit(solution)/shard_map/ppermute | solution.py:89
  71.8 5.8 %collective-permute-start.20 = (bf16[512,128]{1,0:T(8,128)(2,1)S(1)}, bf16[512,128]{1,0:T(8,128)(2,1)S(1)}, u32[]{:S(2)}, u32[]{:S(2)}) collective-permute-start(bf16[512,128]{1,0:T(8,128)(2,1)S(1)} %collective-permute-done.16), channel_id=1, source_target_pairs={{0,2},{2,4},{4,6},{6,7},{7,5},{5,3},{3,1},{1,0},{8,10},{10,12},{12... | collective-permute-start | bytes 393224 | tf_op jit(solution)/shard_map/ppermute | solution.py:88
  72.9 7.7 %collective-permute-start.23 = (bf16[512,128]{1,0:T(8,128)(2,1)S(1)}, bf16[512,128]{1,0:T(8,128)(2,1)S(1)}, u32[]{:S(2)}, u32[]{:S(2)}) collective-permute-start(bf16[512,128]{1,0:T(8,128)(2,1)S(1)} %collective-permute-done.19), channel_id=1, source_target_pairs={{0,2},{2,4},{4,6},{6,7},{7,5},{5,3},{3,1},{1,0},{8,10},{10,12},{12... | collective-permute-start | bytes 393224 | tf_op jit(solution)/shard_map/ppermute | solution.py:88
  74.5 7.7 %collective-permute-start.25 = (bf16[512,128]{1,0:T(8,128)(2,1)S(1)}, bf16[512,128]{1,0:T(8,128)(2,1)S(1)}, u32[]{:S(2)}, u32[]{:S(2)}) collective-permute-start(bf16[512,128]{1,0:T(8,128)(2,1)S(1)} %collective-permute-done.21), channel_id=1, source_target_pairs={{2,0},{4,2},{6,4},{7,6},{5,7},{3,5},{1,3},{0,1},{10,8},{12,10},{14... | collective-permute-start | bytes 393224 | tf_op jit(solution)/shard_map/ppermute | solution.py:89
  74.9 7.9 %collective-permute-start.26 = (bf16[512,128]{1,0:T(8,128)(2,1)S(1)}, bf16[512,128]{1,0:T(8,128)(2,1)S(1)}, u32[]{:S(2)}, u32[]{:S(2)}) collective-permute-start(bf16[512,128]{1,0:T(8,128)(2,1)S(1)} %collective-permute-done.22), channel_id=1, source_target_pairs={{2,0},{4,2},{6,4},{7,6},{5,7},{3,5},{1,3},{0,1},{10,8},{12,10},{14... | collective-permute-start | bytes 393224 | tf_op jit(solution)/shard_map/ppermute | solution.py:89
  77.6 7.5 %collective-permute-start.24 = (bf16[512,128]{1,0:T(8,128)(2,1)S(1)}, bf16[512,128]{1,0:T(8,128)(2,1)S(1)}, u32[]{:S(2)}, u32[]{:S(2)}) collective-permute-start(bf16[512,128]{1,0:T(8,128)(2,1)S(1)} %collective-permute-done.20), channel_id=1, source_target_pairs={{0,2},{2,4},{4,6},{6,7},{7,5},{5,3},{3,1},{1,0},{8,10},{10,12},{12... | collective-permute-start | bytes 393224 | tf_op jit(solution)/shard_map/ppermute | solution.py:88
  80.6 7.7 %collective-permute-start.27 = (bf16[512,128]{1,0:T(8,128)(2,1)S(1)}, bf16[512,128]{1,0:T(8,128)(2,1)S(1)}, u32[]{:S(2)}, u32[]{:S(2)}) collective-permute-start(bf16[512,128]{1,0:T(8,128)(2,1)S(1)} %collective-permute-done.23), channel_id=1, source_target_pairs={{0,2},{2,4},{4,6},{6,7},{7,5},{5,3},{3,1},{1,0},{8,10},{10,12},{12... | collective-permute-start | bytes 393224 | tf_op jit(solution)/shard_map/ppermute | solution.py:88
  82.2 9.6 %collective-permute-start.28 = (bf16[512,128]{1,0:T(8,128)(2,1)S(1)}, bf16[512,128]{1,0:T(8,128)(2,1)S(1)}, u32[]{:S(2)}, u32[]{:S(2)}) collective-permute-start(bf16[512,128]{1,0:T(8,128)(2,1)S(1)} %collective-permute-done.25), channel_id=1, source_target_pairs={{2,0},{4,2},{6,4},{7,6},{5,7},{3,5},{1,3},{0,1},{10,8},{12,10},{14... | collective-permute-start | bytes 393224 | tf_op jit(solution)/shard_map/ppermute | solution.py:89
  82.9 7.1 %collective-permute-start.30 = (bf16[512,128]{1,0:T(8,128)(2,1)S(1)}, bf16[512,128]{1,0:T(8,128)(2,1)S(1)}, u32[]{:S(2)}, u32[]{:S(2)}) collective-permute-start(bf16[512,128]{1,0:T(8,128)(2,1)S(1)} %collective-permute-done.26), channel_id=1, source_target_pairs={{2,0},{4,2},{6,4},{7,6},{5,7},{3,5},{1,3},{0,1},{10,8},{12,10},{14... | collective-permute-start | bytes 393224 | tf_op jit(solution)/shard_map/ppermute | solution.py:89
  85.1 8.4 %collective-permute-start.29 = (bf16[512,128]{1,0:T(8,128)(2,1)S(1)}, bf16[512,128]{1,0:T(8,128)(2,1)S(1)}, u32[]{:S(2)}, u32[]{:S(2)}) collective-permute-start(bf16[512,128]{1,0:T(8,128)(2,1)S(1)} %collective-permute-done.24), channel_id=1, source_target_pairs={{0,2},{2,4},{4,6},{6,7},{7,5},{5,3},{3,1},{1,0},{8,10},{10,12},{12... | collective-permute-start | bytes 393224 | tf_op jit(solution)/shard_map/ppermute | solution.py:88
  96.0 5.0 %collective-permute-start.31 = (bf16[512,128]{1,0:T(8,128)(2,1)S(1)}, bf16[512,128]{1,0:T(8,128)(2,1)S(1)}, u32[]{:S(2)}, u32[]{:S(2)}) collective-permute-start(bf16[512,128]{1,0:T(8,128)(2,1)S(1)} %get-tuple-element.30), channel_id=1, source_target_pairs={{0,2},{2,4},{4,6},{6,7},{7,5},{5,3},{3,1},{1,0},{8,10},{10,12},{12... | collective-permute-start | bytes 393224 | tf_op jit(solution)/shard_map/ppermute | solution.py:88
  98.0 5.0 %collective-permute-start.32 = (bf16[512,128]{1,0:T(8,128)(2,1)S(1)}, bf16[512,128]{1,0:T(8,128)(2,1)S(1)}, u32[]{:S(2)}, u32[]{:S(2)}) collective-permute-start(bf16[512,128]{1,0:T(8,128)(2,1)S(1)} %get-tuple-element.32), channel_id=1, source_target_pairs={{0,2},{2,4},{4,6},{6,7},{7,5},{5,3},{3,1},{1,0},{8,10},{10,12},{12... | collective-permute-start | bytes 393224 | tf_op jit(solution)/shard_map/ppermute | solution.py:88
  100.0 6.2 %collective-permute-start.33 = (bf16[512,128]{1,0:T(8,128)(2,1)S(1)}, bf16[512,128]{1,0:T(8,128)(2,1)S(1)}, u32[]{:S(2)}, u32[]{:S(2)}) collective-permute-start(bf16[512,128]{1,0:T(8,128)(2,1)S(1)} %get-tuple-element.31), channel_id=1, source_target_pairs={{2,0},{4,2},{6,4},{7,6},{5,7},{3,5},{1,3},{0,1},{10,8},{12,10},{14... | collective-permute-start | bytes 393224 | tf_op jit(solution)/shard_map/ppermute | solution.py:89
  100.0 9.0 %collective-permute-start.34 = (bf16[512,128]{1,0:T(8,128)(2,1)S(1)}, bf16[512,128]{1,0:T(8,128)(2,1)S(1)}, u32[]{:S(2)}, u32[]{:S(2)}) collective-permute-start(bf16[512,128]{1,0:T(8,128)(2,1)S(1)} %get-tuple-element.33), channel_id=1, source_target_pairs={{2,0},{4,2},{6,4},{7,6},{5,7},{3,5},{1,3},{0,1},{10,8},{12,10},{14... | collective-permute-start | bytes 393224 | tf_op jit(solution)/shard_map/ppermute | solution.py:89
  101.0 14.3 %collective-permute-start.35 = (bf16[512,128]{1,0:T(8,128)(2,1)S(1)}, bf16[512,128]{1,0:T(8,128)(2,1)S(1)}, u32[]{:S(2)}, u32[]{:S(2)}) collective-permute-start(bf16[512,128]{1,0:T(8,128)(2,1)S(1)} %collective-permute-done.31), channel_id=1, source_target_pairs={{0,2},{2,4},{4,6},{6,7},{7,5},{5,3},{3,1},{1,0},{8,10},{10,12},{12... | collective-permute-start | bytes 393224 | tf_op jit(solution)/shard_map/ppermute | solution.py:88
  102.9 14.3 %collective-permute-start.36 = (bf16[512,128]{1,0:T(8,128)(2,1)S(1)}, bf16[512,128]{1,0:T(8,128)(2,1)S(1)}, u32[]{:S(2)}, u32[]{:S(2)}) collective-permute-start(bf16[512,128]{1,0:T(8,128)(2,1)S(1)} %collective-permute-done.32), channel_id=1, source_target_pairs={{0,2},{2,4},{4,6},{6,7},{7,5},{5,3},{3,1},{1,0},{8,10},{10,12},{12... | collective-permute-start | bytes 393224 | tf_op jit(solution)/shard_map/ppermute | solution.py:88
  106.2 6.0 %collective-permute-start.37 = (bf16[512,128]{1,0:T(8,128)(2,1)S(1)}, bf16[512,128]{1,0:T(8,128)(2,1)S(1)}, u32[]{:S(2)}, u32[]{:S(2)}) collective-permute-start(bf16[512,128]{1,0:T(8,128)(2,1)S(1)} %collective-permute-done.33), channel_id=1, source_target_pairs={{2,0},{4,2},{6,4},{7,6},{5,7},{3,5},{1,3},{0,1},{10,8},{12,10},{14... | collective-permute-start | bytes 393224 | tf_op jit(solution)/shard_map/ppermute | solution.py:89
  109.0 5.9 %collective-permute-start.38 = (bf16[512,128]{1,0:T(8,128)(2,1)S(1)}, bf16[512,128]{1,0:T(8,128)(2,1)S(1)}, u32[]{:S(2)}, u32[]{:S(2)}) collective-permute-start(bf16[512,128]{1,0:T(8,128)(2,1)S(1)} %collective-permute-done.34), channel_id=1, source_target_pairs={{2,0},{4,2},{6,4},{7,6},{5,7},{3,5},{1,3},{0,1},{10,8},{12,10},{14... | collective-permute-start | bytes 393224 | tf_op jit(solution)/shard_map/ppermute | solution.py:89
  112.1 6.3 %collective-permute-start.41 = (bf16[512,128]{1,0:T(8,128)(2,1)S(1)}, bf16[512,128]{1,0:T(8,128)(2,1)S(1)}, u32[]{:S(2)}, u32[]{:S(2)}) collective-permute-start(bf16[512,128]{1,0:T(8,128)(2,1)S(1)} %collective-permute-done.37), channel_id=1, source_target_pairs={{2,0},{4,2},{6,4},{7,6},{5,7},{3,5},{1,3},{0,1},{10,8},{12,10},{14... | collective-permute-start | bytes 393224 | tf_op jit(solution)/shard_map/ppermute | solution.py:89
  114.9 6.4 %collective-permute-start.42 = (bf16[512,128]{1,0:T(8,128)(2,1)S(1)}, bf16[512,128]{1,0:T(8,128)(2,1)S(1)}, u32[]{:S(2)}, u32[]{:S(2)}) collective-permute-start(bf16[512,128]{1,0:T(8,128)(2,1)S(1)} %collective-permute-done.38), channel_id=1, source_target_pairs={{2,0},{4,2},{6,4},{7,6},{5,7},{3,5},{1,3},{0,1},{10,8},{12,10},{14... | collective-permute-start | bytes 393224 | tf_op jit(solution)/shard_map/ppermute | solution.py:89
  115.3 6.5 %collective-permute-start.39 = (bf16[512,128]{1,0:T(8,128)(2,1)S(1)}, bf16[512,128]{1,0:T(8,128)(2,1)S(1)}, u32[]{:S(2)}, u32[]{:S(2)}) collective-permute-start(bf16[512,128]{1,0:T(8,128)(2,1)S(1)} %collective-permute-done.35), channel_id=1, source_target_pairs={{0,2},{2,4},{4,6},{6,7},{7,5},{5,3},{3,1},{1,0},{8,10},{10,12},{12... | collective-permute-start | bytes 393224 | tf_op jit(solution)/shard_map/ppermute | solution.py:88
  117.3 6.4 %collective-permute-start.40 = (bf16[512,128]{1,0:T(8,128)(2,1)S(1)}, bf16[512,128]{1,0:T(8,128)(2,1)S(1)}, u32[]{:S(2)}, u32[]{:S(2)}) collective-permute-start(bf16[512,128]{1,0:T(8,128)(2,1)S(1)} %collective-permute-done.36), channel_id=1, source_target_pairs={{0,2},{2,4},{4,6},{6,7},{7,5},{5,3},{3,1},{1,0},{8,10},{10,12},{12... | collective-permute-start | bytes 393224 | tf_op jit(solution)/shard_map/ppermute | solution.py:88
  118.5 6.5 %collective-permute-start.45 = (bf16[512,128]{1,0:T(8,128)(2,1)S(1)}, bf16[512,128]{1,0:T(8,128)(2,1)S(1)}, u32[]{:S(2)}, u32[]{:S(2)}) collective-permute-start(bf16[512,128]{1,0:T(8,128)(2,1)S(1)} %collective-permute-done.41), channel_id=1, source_target_pairs={{2,0},{4,2},{6,4},{7,6},{5,7},{3,5},{1,3},{0,1},{10,8},{12,10},{14... | collective-permute-start | bytes 393224 | tf_op jit(solution)/shard_map/ppermute | solution.py:89
  121.3 5.2 %collective-permute-start.46 = (bf16[512,128]{1,0:T(8,128)(2,1)S(1)}, bf16[512,128]{1,0:T(8,128)(2,1)S(1)}, u32[]{:S(2)}, u32[]{:S(2)}) collective-permute-start(bf16[512,128]{1,0:T(8,128)(2,1)S(1)} %collective-permute-done.42), channel_id=1, source_target_pairs={{2,0},{4,2},{6,4},{7,6},{5,7},{3,5},{1,3},{0,1},{10,8},{12,10},{14... | collective-permute-start | bytes 393224 | tf_op jit(solution)/shard_map/ppermute | solution.py:89
  121.8 6.4 %collective-permute-start.43 = (bf16[512,128]{1,0:T(8,128)(2,1)S(1)}, bf16[512,128]{1,0:T(8,128)(2,1)S(1)}, u32[]{:S(2)}, u32[]{:S(2)}) collective-permute-start(bf16[512,128]{1,0:T(8,128)(2,1)S(1)} %collective-permute-done.39), channel_id=1, source_target_pairs={{0,2},{2,4},{4,6},{6,7},{7,5},{5,3},{3,1},{1,0},{8,10},{10,12},{12... | collective-permute-start | bytes 393224 | tf_op jit(solution)/shard_map/ppermute | solution.py:88
  123.7 7.3 %collective-permute-start.44 = (bf16[512,128]{1,0:T(8,128)(2,1)S(1)}, bf16[512,128]{1,0:T(8,128)(2,1)S(1)}, u32[]{:S(2)}, u32[]{:S(2)}) collective-permute-start(bf16[512,128]{1,0:T(8,128)(2,1)S(1)} %collective-permute-done.40), channel_id=1, source_target_pairs={{0,2},{2,4},{4,6},{6,7},{7,5},{5,3},{3,1},{1,0},{8,10},{10,12},{12... | collective-permute-start | bytes 393224 | tf_op jit(solution)/shard_map/ppermute | solution.py:88
  124.9 7.8 %collective-permute-start.49 = (bf16[512,128]{1,0:T(8,128)(2,1)S(1)}, bf16[512,128]{1,0:T(8,128)(2,1)S(1)}, u32[]{:S(2)}, u32[]{:S(2)}) collective-permute-start(bf16[512,128]{1,0:T(8,128)(2,1)S(1)} %collective-permute-done.45), channel_id=1, source_target_pairs={{2,0},{4,2},{6,4},{7,6},{5,7},{3,5},{1,3},{0,1},{10,8},{12,10},{14... | collective-permute-start | bytes 393224 | tf_op jit(solution)/shard_map/ppermute | solution.py:89
  126.5 7.0 %collective-permute-start.50 = (bf16[512,128]{1,0:T(8,128)(2,1)S(1)}, bf16[512,128]{1,0:T(8,128)(2,1)S(1)}, u32[]{:S(2)}, u32[]{:S(2)}) collective-permute-start(bf16[512,128]{1,0:T(8,128)(2,1)S(1)} %collective-permute-done.46), channel_id=1, source_target_pairs={{2,0},{4,2},{6,4},{7,6},{5,7},{3,5},{1,3},{0,1},{10,8},{12,10},{14... | collective-permute-start | bytes 393224 | tf_op jit(solution)/shard_map/ppermute | solution.py:89
  128.2 5.8 %collective-permute-start.47 = (bf16[512,128]{1,0:T(8,128)(2,1)S(1)}, bf16[512,128]{1,0:T(8,128)(2,1)S(1)}, u32[]{:S(2)}, u32[]{:S(2)}) collective-permute-start(bf16[512,128]{1,0:T(8,128)(2,1)S(1)} %collective-permute-done.43), channel_id=1, source_target_pairs={{0,2},{2,4},{4,6},{6,7},{7,5},{5,3},{3,1},{1,0},{8,10},{10,12},{12... | collective-permute-start | bytes 393224 | tf_op jit(solution)/shard_map/ppermute | solution.py:88
  131.0 5.0 %collective-permute-start.48 = (bf16[512,128]{1,0:T(8,128)(2,1)S(1)}, bf16[512,128]{1,0:T(8,128)(2,1)S(1)}, u32[]{:S(2)}, u32[]{:S(2)}) collective-permute-start(bf16[512,128]{1,0:T(8,128)(2,1)S(1)} %collective-permute-done.44), channel_id=1, source_target_pairs={{0,2},{2,4},{4,6},{6,7},{7,5},{5,3},{3,1},{1,0},{8,10},{10,12},{12... | collective-permute-start | bytes 393224 | tf_op jit(solution)/shard_map/ppermute | solution.py:88
  132.8 5.0 %collective-permute-start.53 = (bf16[512,128]{1,0:T(8,128)(2,1)S(1)}, bf16[512,128]{1,0:T(8,128)(2,1)S(1)}, u32[]{:S(2)}, u32[]{:S(2)}) collective-permute-start(bf16[512,128]{1,0:T(8,128)(2,1)S(1)} %collective-permute-done.49), channel_id=1, source_target_pairs={{2,0},{4,2},{6,4},{7,6},{5,7},{3,5},{1,3},{0,1},{10,8},{12,10},{14... | collective-permute-start | bytes 393224 | tf_op jit(solution)/shard_map/ppermute | solution.py:89
  133.5 7.0 %collective-permute-start.54 = (bf16[512,128]{1,0:T(8,128)(2,1)S(1)}, bf16[512,128]{1,0:T(8,128)(2,1)S(1)}, u32[]{:S(2)}, u32[]{:S(2)}) collective-permute-start(bf16[512,128]{1,0:T(8,128)(2,1)S(1)} %collective-permute-done.50), channel_id=1, source_target_pairs={{2,0},{4,2},{6,4},{7,6},{5,7},{3,5},{1,3},{0,1},{10,8},{12,10},{14... | collective-permute-start | bytes 393224 | tf_op jit(solution)/shard_map/ppermute | solution.py:89
  134.0 5.0 %collective-permute-start.51 = (bf16[512,128]{1,0:T(8,128)(2,1)S(1)}, bf16[512,128]{1,0:T(8,128)(2,1)S(1)}, u32[]{:S(2)}, u32[]{:S(2)}) collective-permute-start(bf16[512,128]{1,0:T(8,128)(2,1)S(1)} %collective-permute-done.47), channel_id=1, source_target_pairs={{0,2},{2,4},{4,6},{6,7},{7,5},{5,3},{3,1},{1,0},{8,10},{10,12},{12... | collective-permute-start | bytes 393224 | tf_op jit(solution)/shard_map/ppermute | solution.py:88
  136.0 5.4 %collective-permute-start.52 = (bf16[512,128]{1,0:T(8,128)(2,1)S(1)}, bf16[512,128]{1,0:T(8,128)(2,1)S(1)}, u32[]{:S(2)}, u32[]{:S(2)}) collective-permute-start(bf16[512,128]{1,0:T(8,128)(2,1)S(1)} %collective-permute-done.48), channel_id=1, source_target_pairs={{0,2},{2,4},{4,6},{6,7},{7,5},{5,3},{3,1},{1,0},{8,10},{10,12},{12... | collective-permute-start | bytes 393224 | tf_op jit(solution)/shard_map/ppermute | solution.py:88
  137.8 5.5 %collective-permute-start.56 = (bf16[512,128]{1,0:T(8,128)(2,1)S(1)}, bf16[512,128]{1,0:T(8,128)(2,1)S(1)}, u32[]{:S(2)}, u32[]{:S(2)}) collective-permute-start(bf16[512,128]{1,0:T(8,128)(2,1)S(1)} %collective-permute-done.53), channel_id=1, source_target_pairs={{2,0},{4,2},{6,4},{7,6},{5,7},{3,5},{1,3},{0,1},{10,8},{12,10},{14... | collective-permute-start | bytes 393224 | tf_op jit(solution)/shard_map/ppermute | solution.py:89
  139.0 5.0 %collective-permute-start.55 = (bf16[512,128]{1,0:T(8,128)(2,1)S(1)}, bf16[512,128]{1,0:T(8,128)(2,1)S(1)}, u32[]{:S(2)}, u32[]{:S(2)}) collective-permute-start(bf16[512,128]{1,0:T(8,128)(2,1)S(1)} %collective-permute-done.51), channel_id=1, source_target_pairs={{0,2},{2,4},{4,6},{6,7},{7,5},{5,3},{3,1},{1,0},{8,10},{10,12},{12... | collective-permute-start | bytes 393224 | tf_op jit(solution)/shard_map/ppermute | solution.py:88
  140.5 5.0 %collective-permute-start.61 = (bf16[512,128]{1,0:T(8,128)(2,1)S(1)}, bf16[512,128]{1,0:T(8,128)(2,1)S(1)}, u32[]{:S(2)}, u32[]{:S(2)}) collective-permute-start(bf16[512,128]{1,0:T(8,128)(2,1)S(1)} %collective-permute-done.54), channel_id=1, source_target_pairs={{2,0},{4,2},{6,4},{7,6},{5,7},{3,5},{1,3},{0,1},{10,8},{12,10},{14... | collective-permute-start | bytes 393224 | tf_op jit(solution)/shard_map/ppermute | solution.py:89
  141.4 5.0 %collective-permute-start.60 = (bf16[512,128]{1,0:T(8,128)(2,1)S(1)}, bf16[512,128]{1,0:T(8,128)(2,1)S(1)}, u32[]{:S(2)}, u32[]{:S(2)}) collective-permute-start(bf16[512,128]{1,0:T(8,128)(2,1)S(1)} %collective-permute-done.52), channel_id=1, source_target_pairs={{0,2},{2,4},{4,6},{6,7},{7,5},{5,3},{3,1},{1,0},{8,10},{10,12},{12... | collective-permute-start | bytes 393224 | tf_op jit(solution)/shard_map/ppermute | solution.py:88
  148.4 4.9 %collective-permute-start.58 = (bf16[256,128]{1,0:T(8,128)(2,1)S(1)}, bf16[256,128]{1,0:T(8,128)(2,1)S(1)}, u32[]{:S(2)}, u32[]{:S(2)}) collective-permute-start(bf16[256,128]{1,0:T(8,128)(2,1)S(1)} %convolution_convert_fusion.5), channel_id=1, source_target_pairs={{0,16},{8,24},{16,0},{24,8},{1,17},{9,25},{17,1},{25,9},{2,18},{10... | collective-permute-start | bytes 196616 | tf_op jit(solution)/shard_map/ppermute | solution.py:149
  148.8 5.0 %collective-permute-start.57 = (bf16[256,128]{1,0:T(8,128)(2,1)S(1)}, bf16[256,128]{1,0:T(8,128)(2,1)S(1)}, u32[]{:S(2)}, u32[]{:S(2)}) collective-permute-start(bf16[256,128]{1,0:T(8,128)(2,1)S(1)} %convolution_convert_fusion.6), channel_id=1, source_target_pairs={{0,8},{8,0},{16,24},{24,16},{1,9},{9,1},{17,25},{25,17},{2,10},{10... | collective-permute-start | bytes 196616 | tf_op jit(solution)/shard_map/ppermute | solution.py:149
  148.9 4.7 %collective-permute-start.59 = (bf16[256,128]{1,0:T(8,128)(2,1)S(1)}, bf16[256,128]{1,0:T(8,128)(2,1)S(1)}, u32[]{:S(2)}, u32[]{:S(2)}) collective-permute-start(bf16[256,128]{1,0:T(8,128)(2,1)S(1)} %convolution_convert_fusion.4), channel_id=1, source_target_pairs={{0,24},{8,16},{16,8},{24,0},{1,25},{9,17},{17,9},{25,1},{2,26},{10... | collective-permute-start | bytes 196616 | tf_op jit(solution)/shard_map/ppermute | solution.py:149
  151.0 6.3 %collective-permute-start.62 = (bf16[256,128]{1,0:T(8,128)(2,1)S(1)}, bf16[256,128]{1,0:T(8,128)(2,1)S(1)}, u32[]{:S(2)}, u32[]{:S(2)}) collective-permute-start(bf16[256,128]{1,0:T(8,128)(2,1)S(1)} %convolution_convert_fusion.2), channel_id=1, source_target_pairs={{0,8},{8,0},{16,24},{24,16},{1,9},{9,1},{17,25},{25,17},{2,10},{10... | collective-permute-start | bytes 196616 | tf_op jit(solution)/shard_map/ppermute | solution.py:149
  151.0 4.5 %collective-permute-start.63 = (bf16[256,128]{1,0:T(8,128)(2,1)S(1)}, bf16[256,128]{1,0:T(8,128)(2,1)S(1)}, u32[]{:S(2)}, u32[]{:S(2)}) collective-permute-start(bf16[256,128]{1,0:T(8,128)(2,1)S(1)} %convolution_convert_fusion.1), channel_id=1, source_target_pairs={{0,16},{8,24},{16,0},{24,8},{1,17},{9,25},{17,1},{25,9},{2,18},{10... | collective-permute-start | bytes 196616 | tf_op jit(solution)/shard_map/ppermute | solution.py:149
  (16 other events, 201.9 us)

commit v2 on v0

--- a/solution.py
+++ b/solution.py
@@ -1,6 +1,9 @@
 import jax
 import jax.numpy as jnp
 from jax import lax
+from jax.experimental import pallas as pl
+from jax.experimental.layout import Layout, with_layout_constraint
+from jax.experimental.pallas import tpu as pltpu
 from jax.sharding import PartitionSpec as P
 
 CAPACITY = 2
@@ -27,8 +30,79 @@
     return result
 
 
+def row_major(array):
+    return with_layout_constraint(array, Layout(major_to_minor=tuple(range(array.ndim))))
+
+
 def dot(a, b):
-    return jnp.dot(a, b, preferred_element_type=jnp.float32)
+    return row_major(jnp.dot(a, b, preferred_element_type=jnp.float32))
+
+
+def streamed_product(matrix, total, firsts, seconds, order, step):
+    count = len(order)
+    height = matrix.shape[0]
+    half = firsts[0].shape[0]
+    pieces = len(firsts)
+    chunk = 256 if height % 256 == 0 else height
+    chunks = height // chunk
+    given = 0 if total is None else 1
+
+    def kernel(source, *refs):
+        first_refs = refs[given:given + pieces]
+        second_refs = refs[given + pieces:given + 2 * pieces]
+        out, buffers, semaphores = refs[given + 2 * pieces:]
+        place = lookup([order.index(i) for i in range(count)], lax.axis_index("wide"))
+        columns = [
+            2 * half * lookup(order, lax.rem(place + count - step, count)),
+            2 * half * lookup(order, lax.rem(place + step, count)) + half,
+        ]
+        copies = []
+        for number in range(chunks):
+            part = pl.ds(number * chunk, chunk)
+            for side in range(2):
+                start = pl.multiple_of(columns[side], half)
+                copies.append(
+                    pltpu.make_async_copy(
+                        source.at[part, pl.ds(start, half)],
+                        buffers.at[side, part],
+                        semaphores.at[side, number],
+                    )
+                )
+                copies[-1].start()
+        values = [
+            jnp.concatenate([ref[...] for ref in refs_], axis=1)
+            for refs_ in (first_refs, second_refs)
+        ]
+        for number in range(chunks):
+            part = pl.ds(number * chunk, chunk)
+            result = refs[0][part, :] if given else 0.0
+            for side in range(2):
+                copies[2 * number + side].wait()
+                result = result + jnp.dot(
+                    buffers[side, part], values[side], preferred_element_type=jnp.float32
+                )
+            out[part, :] = result
+
+    width = sum(piece.shape[1] for piece in firsts)
+    blocks = [pl.BlockSpec(memory_space=pltpu.VMEM)] * (given + 2 * pieces)
+    inputs = ([total] if given else []) + list(firsts) + list(seconds)
+    return pl.pallas_call(
+        kernel,
+        out_shape=pltpu.VMEM((height, width), jnp.float32),
+        in_specs=[pl.BlockSpec(memory_space=pltpu.HBM)] + blocks,
+        out_specs=pl.BlockSpec(memory_space=pltpu.VMEM),
+        scratch_shapes=[
+            pltpu.VMEM((2, height, half), matrix.dtype),
+            pltpu.SemaphoreType.DMA((2, chunks)),
+        ],
+        input_output_aliases={1: 0} if given else {},
+        compiler_params=pltpu.CompilerParams(vmem_limit_bytes=16 << 20),
+        cost_estimate=pl.CostEstimate(
+            flops=4 * height * half * width,
+            bytes_accessed=4 * height * half + 8 * height * width,
+            transcendentals=0,
+        ),
+    )(pltpu.with_memory_space_constraint(matrix, pltpu.HBM), *inputs)
 
 
 def body(inv_diag, below, rhs, tile_count, tile_owner, tile_rows, parent_rhs):
@@ -46,18 +120,16 @@
     place = lookup([order.index(i) for i in range(wide)], wide_index)
     onward = [(order[i], order[(i + 1) % wide]) for i in range(wide)]
     backward = [(b, a) for a, b in onward]
-    from_left = [lookup(order, (place + wide - step) % wide) for step in range(wide)]
-    from_right = [lookup(order, (place + step) % wide) for step in range(wide)]
-
-    def part(matrix, index, offset, values):
-        columns = lax.dynamic_slice_in_dim(matrix, index * rows + offset, values.shape[0], 1)
-        return dot(columns, values)
-
     def ring_products(matrix, blocks, aside=None):
         travelling = [(block[:half], block[half:]) for block in blocks]
-        totals = [part(matrix, wide_index, 0, block) for block in blocks]
+        total = None
         extra = None
         for step in range(1, wide):
+            arrived = list(travelling)
+            if step > 1:
+                first, second = travelling[0]
+                first, total = lax.optimization_barrier((first, total))
+                travelling[0] = (first, second)
             for column, (first, second) in enumerate(travelling):
                 first = lax.ppermute(first, "wide", onward)
                 second = lax.ppermute(second, "wide", backward)
@@ -66,9 +138,14 @@
                 if aside and column == 0 and step == ROUTING_STEPS[1]:
                     first, extra = lax.optimization_barrier((first, extra))
                 travelling[column] = (first, second)
-                totals[column] = totals[column] + part(matrix, from_left[step], 0, first)
-                totals[column] = totals[column] + part(matrix, from_right[step], half, second)
-        return [total.astype(jnp.bfloat16) for total in totals], extra
+            firsts, seconds = zip(*arrived)
+            total = streamed_product(matrix, total, firsts, seconds, order, step - 1)
+        results = []
+        for column, (first, second) in enumerate(travelling):
+            piece = total[:, column * LANES:(column + 1) * LANES]
+            piece = streamed_product(matrix, piece, [first], [second], order, wide - 1)
+            results.append(piece.astype(jnp.bfloat16))
+        return results, extra
 
     swaps = [[(i, i ^ delta) for i in range(fronts)] for delta in range(fronts)]
 

time: 176 us -> 133 us (0.76)
  matrix products: 86.7 us -> 3.99 us
  Pallas kernels: 0 us -> 47.7 us
  local copies, waits for them, and re-layouts: 6.9 us -> 1.41 us
  starting transfers between devices: 69.9 us -> 64.7 us
  other arithmetic: 2.2 us -> 5.22 us
  waiting for transfers between devices: 6 us -> 8.08 us
    dot_general x74 -> x14, matrix products: 86.7 us -> 3.99 us  [dot(): return row_major(jnp.dot(a, b, preferred_element_type=jnp.float32))]
    pallas_call x0 -> x18, Pallas kernels: none -> 47.7 us  [streamed_product(): pl.pallas_call(kernel, out_shape=pltpu.VMEM((height, width), jnp.float32)...]
    ppermute x28, starting transfers between devices: 41.7 us -> 18.1 us  [ring_products(): second = lax.ppermute(second, 'wide', backward)]
    ppermute x28, starting transfers between devices: 22.3 us -> 41.2 us  [ring_products(): first = lax.ppermute(first, 'wide', onward)]
    unnamed x24 -> x13, local copies, waits for them, and re-layouts: 3.78 us -> 0.11 us
    ppermute x28, waiting for transfers between devices: 0.47 us -> 4.07 us  [ring_products(): second = lax.ppermute(second, 'wide', backward)]
    ppermute x28, waiting for transfers between devices: 1.95 us -> 0.07 us  [ring_products(): first = lax.ppermute(first, 'wide', onward)]
  transfers between devices with their start and end apart: 65 -> 65, of which waited for: 7 -> 11; matrix products, arithmetic and copies ran while one was open for 51% -> 4% of each run, Pallas kernels for 0% -> 32%
where the time goes in v2:
time: 133 us; the launch traced here: 132 us
  starting transfers between devices  64.7 us (49%)
  Pallas kernels  47.7 us (36%)
  waiting for transfers between devices  8.08 us (6%)
  other arithmetic  5.22 us (4%)
  matrix products  3.99 us (3%)
  local copies, waits for them, and re-layouts  1.41 us (1%)
    pallas_call x18, Pallas kernels, streamed_product(): pl.pallas_call(kernel, out_shape=pltpu.VMEM((height, width), jnp.float32)...  47.7 us
    ppermute x28, starting transfers between devices, ring_products(): first = lax.ppermute(first, 'wide', onward)  41.2 us
    ppermute x28, starting transfers between devices, ring_products(): second = lax.ppermute(second, 'wide', backward)  18.1 us
    ppermute x28, waiting for transfers between devices, ring_products(): second = lax.ppermute(second, 'wide', backward)  4.07 us
    dot_general x14, matrix products, dot(): return row_major(jnp.dot(a, b, preferred_element_type=jnp.float32))  3.99 us
    ppermute x6, waiting for transfers between devices, body(): lax.ppermute(values_out[delta], 'front', swaps[delta])  3.82 us
    ppermute x6, starting transfers between devices, body(): lax.ppermute(values_out[delta], 'front', swaps[delta])  3.76 us
  transfers between devices with their start and end apart: 65, of which 11 were waited for; matrix products, arithmetic and copies ran while one was open for 4% of the time, Pallas kernels for 32%

profile of v2, /device:TPU:0, one launch (start us, length us, event | category | flops | bytes accessed | tf_op | source)
XLA Modules:
  0.0 132.4 jit_solution(2127782321900037598)
XLA Ops:
  0.6 1.1 fusion.40
  1.8 3.1 %collective-permute-start = (bf16[512,128]{1,0:T(8,128)(2,1)S(1)}, bf16[512,128]{1,0:T(8,128)(2,1)S(1)}, u32[]{:S(2)}, u32[]{:S(2)}) collective-permute-start(bf16[512,128]{1,0:T(8,128)(2,1)S(1)} %get-tuple-element.81.refs_0_), channel_id=1, source_target_pairs={{0,2},{2,4},{4,6},{6,7},{7,5},{5,3},{3,1},{1,0},{8,10},{10,12},{12... | collective-permute-start | bytes 393224 | tf_op jit(solution)/shard_map/ppermute | solution.py:134
  4.8 1.6 %collective-permute-start.2 = (bf16[512,128]{1,0:T(8,128)(2,1)S(1)}, bf16[512,128]{1,0:T(8,128)(2,1)S(1)}, u32[]{:S(2)}, u32[]{:S(2)}) collective-permute-start(bf16[512,128]{1,0:T(8,128)(2,1)S(1)} %get-tuple-element.80.refs_1_), channel_id=1, source_target_pairs={{0,2},{2,4},{4,6},{6,7},{7,5},{5,3},{3,1},{1,0},{8,10},{10,12},{12... | collective-permute-start | bytes 393224 | tf_op jit(solution)/shard_map/ppermute | solution.py:134
  6.9 2.8 %shard_map.86.refs_0_ = f32[1024,256]{1,0:T(8,128)S(1)} custom-call(bf16[1024,8192]{1,0:T(8,128)(2,1)} %bitcast.67, bf16[512,128]{1,0:T(8,128)(2,1)S(1)} %get-tuple-element.81.refs_0_, bf16[512,128]{1,0:T(8,128)(2,1)S(1)} %get-tuple-element.80.refs_1_, bf16[512,128]{1,0:T(8,128)(2,1)S(1)} %get-tuple-element.79.refs_2_, ...), custom_call_target="tpu_custom_call" | custom-call | flops 536870912 | bytes 4194304 | tf_op jit(solution)/shard_map/pallas_call | solution.py:89
  9.8 2.0 %collective-permute-start.1 = (bf16[512,128]{1,0:T(8,128)(2,1)S(1)}, bf16[512,128]{1,0:T(8,128)(2,1)S(1)}, u32[]{:S(2)}, u32[]{:S(2)}) collective-permute-start(bf16[512,128]{1,0:T(8,128)(2,1)S(1)} %collective-permute-done.refs_1_), channel_id=1, source_target_pairs={{0,2},{2,4},{4,6},{6,7},{7,5},{5,3},{3,1},{1,0},{8,10},{10,12},{12... | collective-permute-start | bytes 393224 | tf_op jit(solution)/shard_map/ppermute | solution.py:134
  11.8 1.6 %collective-permute-start.6 = (bf16[512,128]{1,0:T(8,128)(2,1)S(1)}, bf16[512,128]{1,0:T(8,128)(2,1)S(1)}, u32[]{:S(2)}, u32[]{:S(2)}) collective-permute-start(bf16[512,128]{1,0:T(8,128)(2,1)S(1)} %collective-permute-done.2.refs_2_), channel_id=1, source_target_pairs={{0,2},{2,4},{4,6},{6,7},{7,5},{5,3},{3,1},{1,0},{8,10},{10,12},{12... | collective-permute-start | bytes 393224 | tf_op jit(solution)/shard_map/ppermute | solution.py:134
  13.9 0.9 collective-permute-start.8
  14.9 2.9 %shard_map.87.refs_0_ = f32[1024,256]{1,0:T(8,128)S(1)} custom-call(bf16[1024,8192]{1,0:T(8,128)(2,1)} %bitcast.68, f32[1024,256]{1,0:T(8,128)S(1)} %shard_map.86.refs_0_, bf16[512,128]{1,0:T(8,128)(2,1)S(1)} %collective-permute-done.refs_1_, bf16[512,128]{1,0:T(8,128)(2,1)S(1)} %collective-permute-done.2.refs_2_, ...), custom_call_target="tpu_custom_call", output_to_operand_aliasing={{}: (1, {})} | custom-call | flops 536870912 | bytes 4194304 | tf_op jit(solution)/shard_map/pallas_call | solution.py:89
  17.8 1.1 collective-permute-start.5
  20.7 1.6 %collective-permute-start.13 = (bf16[512,128]{1,0:T(8,128)(2,1)S(1)}, bf16[512,128]{1,0:T(8,128)(2,1)S(1)}, u32[]{:S(2)}, u32[]{:S(2)}) collective-permute-start(bf16[512,128]{1,0:T(8,128)(2,1)S(1)} %collective-permute-done.6.refs_2_), channel_id=1, source_target_pairs={{0,2},{2,4},{4,6},{6,7},{7,5},{5,3},{3,1},{1,0},{8,10},{10,12},{12... | collective-permute-start | bytes 393224 | tf_op jit(solution)/shard_map/ppermute | solution.py:134
  22.9 0.9 collective-permute-start.15
  23.8 1.5 %compare_convert_fusion = bf16[4,256,768]{2,1,0:T(8,128)(2,1)} fusion(s32[768]{0:T(1024)S(1)} %add_bitcast_fusion, s32[4,256]{1,0:T(4,128)S(1)} %multiply_add_fusion), kind=kLoop, calls=%fused_computation | loop fusion | flops 1572864 | bytes 1580032 | tf_op jit(solution)/shard_map/convert_element_type | solution.py:175
  25.3 2.9 %shard_map.88.refs_0_ = f32[1024,256]{1,0:T(8,128)S(1)} custom-call(bf16[1024,8192]{1,0:T(8,128)(2,1)} %bitcast.69, f32[1024,256]{1,0:T(8,128)S(1)} %shard_map.87.refs_0_, bf16[512,128]{1,0:T(8,128)(2,1)S(1)} %collective-permute-done.1.refs_1_, bf16[512,128]{1,0:T(8,128)(2,1)S(1)} %collective-permute-done.6.refs_2_, ...), custom_call_target="tpu_custom_call", output_to_operand_aliasing={{}: (1, {})} | custom-call | flops 536870912 | bytes 4194304 | tf_op jit(solution)/shard_map/pallas_call | solution.py:89
  28.2 1.6 %collective-permute-start.11 = (s32[256]{0:T(256)S(1)}, s32[256]{0:T(256)S(1)}, u32[]{:S(2)}, u32[]{:S(2)}) collective-permute-start(s32[256]{0:T(256)S(1)} %get-tuple-element.87), channel_id=1, source_target_pairs={{0,16},{8,24},{16,0},{24,8},{1,17},{9,25},{17,1},{25,9},{2,18},{10... | collective-permute-start | bytes 3080 | tf_op jit(solution)/shard_map/ppermute | solution.py:170
  29.8 1.1 collective-permute-start.9
  30.9 1.6 %collective-permute-start.17 = (bf16[512,128]{1,0:T(8,128)(2,1)S(1)}, bf16[512,128]{1,0:T(8,128)(2,1)S(1)}, u32[]{:S(2)}, u32[]{:S(2)}) collective-permute-start(bf16[512,128]{1,0:T(8,128)(2,1)S(1)} %collective-permute-done.13.refs_2_), channel_id=1, source_target_pairs={{0,2},{2,4},{4,6},{6,7},{7,5},{5,3},{3,1},{1,0},{8,10},{10,12},{12... | collective-permute-start | bytes 393224 | tf_op jit(solution)/shard_map/ppermute | solution.py:134
  32.9 0.9 collective-permute-start.19
  34.0 2.9 %shard_map.89.refs_0_ = f32[1024,256]{1,0:T(8,128)S(1)} custom-call(bf16[1024,8192]{1,0:T(8,128)(2,1)} %bitcast.70, f32[1024,256]{1,0:T(8,128)S(1)} %shard_map.88.refs_0_, bf16[512,128]{1,0:T(8,128)(2,1)S(1)} %collective-permute-done.5.refs_1_, bf16[512,128]{1,0:T(8,128)(2,1)S(1)} %collective-permute-done.13.refs_2_, ...), custom_call_target="tpu_custom_call", output_to_operand_aliasing={{}: (1, {})} | custom-call | flops 536870912 | bytes 4194304 | tf_op jit(solution)/shard_map/pallas_call | solution.py:89
  37.0 1.1 collective-permute-start.16
  38.1 0.9 collective-permute-start.22
  39.0 1.1 collective-permute-start.21
  40.1 0.9 collective-permute-start.23
  41.1 2.9 %shard_map.90.refs_0_ = f32[1024,256]{1,0:T(8,128)S(1)} custom-call(bf16[1024,8192]{1,0:T(8,128)(2,1)} %bitcast.71, f32[1024,256]{1,0:T(8,128)S(1)} %shard_map.89.refs_0_, bf16[512,128]{1,0:T(8,128)(2,1)S(1)} %collective-permute-done.9.refs_1_, bf16[512,128]{1,0:T(8,128)(2,1)S(1)} %collective-permute-done.17.refs_2_, ...), custom_call_target="tpu_custom_call", output_to_operand_aliasing={{}: (1, {})} | custom-call | flops 536870912 | bytes 4194304 | tf_op jit(solution)/shard_map/pallas_call | solution.py:89
  44.0 1.1 collective-permute-start.20
  45.1 0.9 collective-permute-start.25
  46.0 1.1 collective-permute-start.24
  47.1 0.9 collective-permute-start.26
  48.1 2.9 %shard_map.91.refs_0_ = f32[1024,256]{1,0:T(8,128)S(1)} custom-call(bf16[1024,8192]{1,0:T(8,128)(2,1)} %bitcast.72, f32[1024,256]{1,0:T(8,128)S(1)} %shard_map.90.refs_0_, bf16[512,128]{1,0:T(8,128)(2,1)S(1)} %collective-permute-done.16.refs_1_, bf16[512,128]{1,0:T(8,128)(2,1)S(1)} %collective-permute-done.21.refs_2_, ...), custom_call_target="tpu_custom_call", output_to_operand_aliasing={{}: (1, {})} | custom-call | flops 536870912 | bytes 4194304 | tf_op jit(solution)/shard_map/pallas_call | solution.py:89
  51.0 1.1 collective-permute-start.27
  52.1 0.9 collective-permute-start.28
  53.0 1.1 collective-permute-start.29
  54.1 0.9 collective-permute-start.30
  55.1 2.9 %shard_map.92 = f32[1024,256]{1,0:T(8,128)S(1)} custom-call(bf16[1024,8192]{1,0:T(8,128)(2,1)} %bitcast.73, f32[1024,256]{1,0:T(8,128)S(1)} %shard_map.91.refs_0_, bf16[512,128]{1,0:T(8,128)(2,1)S(1)} %collective-permute-done.20.refs_1_, bf16[512,128]{1,0:T(8,128)(2,1)S(1)} %collective-permute-done.24.refs_2_, ...), custom_call_target="tpu_custom_call", output_to_operand_aliasing={{}: (1, {})} | custom-call | flops 536870912 | bytes 4194304 | tf_op jit(solution)/shard_map/pallas_call | solution.py:89
  58.0 2.8 %shard_map.93 = f32[1024,128]{1,0:T(8,128)S(1)} custom-call(bf16[1024,8192]{1,0:T(8,128)(2,1)} %bitcast.74, f32[1024,128]{1,0:T(8,128)S(1)} %get-tuple-element.74.refs_0_, bf16[512,128]{1,0:T(8,128)(2,1)S(1)} %collective-permute-done.27.refs_1_, bf16[512,128]{1,0:T(8,128)(2,1)S(1)} %collective-permute-done.28.refs_2_), custom_call_target="tpu_custom_call", output_to_operand_aliasing={{}: (1, {})} | custom-call | flops 268435456 | bytes 3145728 | tf_op jit(solution)/shard_map/pallas_call | solution.py:89
  60.9 2.8 %shard_map.94 = f32[1024,128]{1,0:T(8,128)S(1)} custom-call(bf16[1024,8192]{1,0:T(8,128)(2,1)} %bitcast.75, f32[1024,128]{1,0:T(8,128)S(1)} %get-tuple-element.75.refs_0_, bf16[512,128]{1,0:T(8,128)(2,1)S(1)} %collective-permute-done.29.refs_1_, bf16[512,128]{1,0:T(8,128)(2,1)S(1)} %collective-permute-done.30.refs_2_), custom_call_target="tpu_custom_call", output_to_operand_aliasing={{}: (1, {})} | custom-call | flops 268435456 | bytes 3145728 | tf_op jit(solution)/shard_map/pallas_call | solution.py:89
  63.8 1.3 %collective-permute-start.31 = (bf16[512,128]{1,0:T(8,128)(2,1)S(1)}, bf16[512,128]{1,0:T(8,128)(2,1)S(1)}, u32[]{:S(2)}, u32[]{:S(2)}) collective-permute-start(bf16[512,128]{1,0:T(8,128)(2,1)S(1)} %get-tuple-element.92.refs_0_), channel_id=1, source_target_pairs={{0,2},{2,4},{4,6},{6,7},{7,5},{5,3},{3,1},{1,0},{8,10},{10,12},{12... | collective-permute-start | bytes 393224 | tf_op jit(solution)/shard_map/ppermute | solution.py:134
  65.1 1.6 %collective-permute-start.33 = (bf16[512,128]{1,0:T(8,128)(2,1)S(1)}, bf16[512,128]{1,0:T(8,128)(2,1)S(1)}, u32[]{:S(2)}, u32[]{:S(2)}) collective-permute-start(bf16[512,128]{1,0:T(8,128)(2,1)S(1)} %get-tuple-element.83.refs_1_), channel_id=1, source_target_pairs={{0,2},{2,4},{4,6},{6,7},{7,5},{5,3},{3,1},{1,0},{8,10},{10,12},{12... | collective-permute-start | bytes 393224 | tf_op jit(solution)/shard_map/ppermute | solution.py:134
  67.9 2.3 %shard_map.95.refs_0_ = f32[768,256]{1,0:T(8,128)S(1)} custom-call(bf16[768,8192]{1,0:T(8,128)(2,1)} %bitcast.76, bf16[512,128]{1,0:T(8,128)(2,1)S(1)} %get-tuple-element.92.refs_0_, bf16[512,128]{1,0:T(8,128)(2,1)S(1)} %get-tuple-element.83.refs_1_, bf16[512,128]{1,0:T(8,128)(2,1)S(1)} %get-tuple-element.93.refs_2_, ...), custom_call_target="tpu_custom_call" | custom-call | flops 402653184 | bytes 3145728 | tf_op jit(solution)/shard_map/pallas_call | solution.py:89
  70.2 1.3 %collective-permute-start.32 = (bf16[512,128]{1,0:T(8,128)(2,1)S(1)}, bf16[512,128]{1,0:T(8,128)(2,1)S(1)}, u32[]{:S(2)}, u32[]{:S(2)}) collective-permute-start(bf16[512,128]{1,0:T(8,128)(2,1)S(1)} %collective-permute-done.31.refs_1_), channel_id=1, source_target_pairs={{0,2},{2,4},{4,6},{6,7},{7,5},{5,3},{3,1},{1,0},{8,10},{10,12},{12... | collective-permute-start | bytes 393224 | tf_op jit(solution)/shard_map/ppermute | solution.py:134
  71.5 1.6 %collective-permute-start.37 = (bf16[512,128]{1,0:T(8,128)(2,1)S(1)}, bf16[512,128]{1,0:T(8,128)(2,1)S(1)}, u32[]{:S(2)}, u32[]{:S(2)}) collective-permute-start(bf16[512,128]{1,0:T(8,128)(2,1)S(1)} %collective-permute-done.33.refs_2_), channel_id=1, source_target_pairs={{0,2},{2,4},{4,6},{6,7},{7,5},{5,3},{3,1},{1,0},{8,10},{10,12},{12... | collective-permute-start | bytes 393224 | tf_op jit(solution)/shard_map/ppermute | solution.py:134
  74.8 2.5 %shard_map.96.refs_0_ = f32[768,256]{1,0:T(8,128)S(1)} custom-call(bf16[768,8192]{1,0:T(8,128)(2,1)} %bitcast.77, f32[768,256]{1,0:T(8,128)S(1)} %shard_map.95.refs_0_, bf16[512,128]{1,0:T(8,128)(2,1)S(1)} %collective-permute-done.31.refs_1_, bf16[512,128]{1,0:T(8,128)(2,1)S(1)} %collective-permute-done.33.refs_2_, ...), custom_call_target="tpu_custom_call", output_to_operand_aliasing={{}: (1, {})} | custom-call | flops 402653184 | bytes 3145728 | tf_op jit(solution)/shard_map/pallas_call | solution.py:89
  77.3 1.6 %collective-permute-start.36 = (bf16[512,128]{1,0:T(8,128)(2,1)S(1)}, bf16[512,128]{1,0:T(8,128)(2,1)S(1)}, u32[]{:S(2)}, u32[]{:S(2)}) collective-permute-start(bf16[512,128]{1,0:T(8,128)(2,1)S(1)} %collective-permute-done.32.refs_1_), channel_id=1, source_target_pairs={{0,2},{2,4},{4,6},{6,7},{7,5},{5,3},{3,1},{1,0},{8,10},{10,12},{12... | collective-permute-start | bytes 393224 | tf_op jit(solution)/shard_map/ppermute | solution.py:134
  78.9 1.5 %collective-permute-start.41 = (bf16[512,128]{1,0:T(8,128)(2,1)S(1)}, bf16[512,128]{1,0:T(8,128)(2,1)S(1)}, u32[]{:S(2)}, u32[]{:S(2)}) collective-permute-start(bf16[512,128]{1,0:T(8,128)(2,1)S(1)} %collective-permute-done.37.refs_2_), channel_id=1, source_target_pairs={{0,2},{2,4},{4,6},{6,7},{7,5},{5,3},{3,1},{1,0},{8,10},{10,12},{12... | collective-permute-start | bytes 393224 | tf_op jit(solution)/shard_map/ppermute | solution.py:134
  82.1 2.5 %shard_map.97.refs_0_ = f32[768,256]{1,0:T(8,128)S(1)} custom-call(bf16[768,8192]{1,0:T(8,128)(2,1)} %bitcast.78, f32[768,256]{1,0:T(8,128)S(1)} %shard_map.96.refs_0_, bf16[512,128]{1,0:T(8,128)(2,1)S(1)} %collective-permute-done.32.refs_1_, bf16[512,128]{1,0:T(8,128)(2,1)S(1)} %collective-permute-done.37.refs_2_, ...), custom_call_target="tpu_custom_call", output_to_operand_aliasing={{}: (1, {})} | custom-call | flops 402653184 | bytes 3145728 | tf_op jit(solution)/shard_map/pallas_call | solution.py:89
  84.6 1.6 %collective-permute-start.40 = (bf16[512,128]{1,0:T(8,128)(2,1)S(1)}, bf16[512,128]{1,0:T(8,128)(2,1)S(1)}, u32[]{:S(2)}, u32[]{:S(2)}) collective-permute-start(bf16[512,128]{1,0:T(8,128)(2,1)S(1)} %collective-permute-done.36.refs_1_), channel_id=1, source_target_pairs={{0,2},{2,4},{4,6},{6,7},{7,5},{5,3},{3,1},{1,0},{8,10},{10,12},{12... | collective-permute-start | bytes 393224 | tf_op jit(solution)/shard_map/ppermute | solution.py:134
  86.3 1.5 %collective-permute-start.45 = (bf16[512,128]{1,0:T(8,128)(2,1)S(1)}, bf16[512,128]{1,0:T(8,128)(2,1)S(1)}, u32[]{:S(2)}, u32[]{:S(2)}) collective-permute-start(bf16[512,128]{1,0:T(8,128)(2,1)S(1)} %collective-permute-done.41.refs_2_), channel_id=1, source_target_pairs={{0,2},{2,4},{4,6},{6,7},{7,5},{5,3},{3,1},{1,0},{8,10},{10,12},{12... | collective-permute-start | bytes 393224 | tf_op jit(solution)/shard_map/ppermute | solution.py:134
  88.3 1.2 collective-permute-done.43.refs_4_
  90.0 2.5 %shard_map.98.refs_0_ = f32[768,256]{1,0:T(8,128)S(1)} custom-call(bf16[768,8192]{1,0:T(8,128)(2,1)} %bitcast.79, f32[768,256]{1,0:T(8,128)S(1)} %shard_map.97.refs_0_, bf16[512,128]{1,0:T(8,128)(2,1)S(1)} %collective-permute-done.36.refs_1_, bf16[512,128]{1,0:T(8,128)(2,1)S(1)} %collective-permute-done.41.refs_2_, ...), custom_call_target="tpu_custom_call", output_to_operand_aliasing={{}: (1, {})} | custom-call | flops 402653184 | bytes 3145728 | tf_op jit(solution)/shard_map/pallas_call | solution.py:89
  92.5 1.6 %collective-permute-start.44 = (bf16[512,128]{1,0:T(8,128)(2,1)S(1)}, bf16[512,128]{1,0:T(8,128)(2,1)S(1)}, u32[]{:S(2)}, u32[]{:S(2)}) collective-permute-start(bf16[512,128]{1,0:T(8,128)(2,1)S(1)} %collective-permute-done.40.refs_1_), channel_id=1, source_target_pairs={{0,2},{2,4},{4,6},{6,7},{7,5},{5,3},{3,1},{1,0},{8,10},{10,12},{12... | collective-permute-start | bytes 393224 | tf_op jit(solution)/shard_map/ppermute | solution.py:134
  94.1 1.3 collective-permute-start.49
  96.7 2.5 %shard_map.99.refs_0_ = f32[768,256]{1,0:T(8,128)S(1)} custom-call(bf16[768,8192]{1,0:T(8,128)(2,1)} %bitcast.80, f32[768,256]{1,0:T(8,128)S(1)} %shard_map.98.refs_0_, bf16[512,128]{1,0:T(8,128)(2,1)S(1)} %collective-permute-done.40.refs_1_, bf16[512,128]{1,0:T(8,128)(2,1)S(1)} %collective-permute-done.45.refs_2_, ...), custom_call_target="tpu_custom_call", output_to_operand_aliasing={{}: (1, {})} | custom-call | flops 402653184 | bytes 3145728 | tf_op jit(solution)/shard_map/pallas_call | solution.py:89
  99.2 1.6 %collective-permute-start.48 = (bf16[512,128]{1,0:T(8,128)(2,1)S(1)}, bf16[512,128]{1,0:T(8,128)(2,1)S(1)}, u32[]{:S(2)}, u32[]{:S(2)}) collective-permute-start(bf16[512,128]{1,0:T(8,128)(2,1)S(1)} %collective-permute-done.44.refs_1_), channel_id=1, source_target_pairs={{0,2},{2,4},{4,6},{6,7},{7,5},{5,3},{3,1},{1,0},{8,10},{10,12},{12... | collective-permute-start | bytes 393224 | tf_op jit(solution)/shard_map/ppermute | solution.py:134
  100.8 1.5 %collective-permute-start.52 = (bf16[512,128]{1,0:T(8,128)(2,1)S(1)}, bf16[512,128]{1,0:T(8,128)(2,1)S(1)}, u32[]{:S(2)}, u32[]{:S(2)}) collective-permute-start(bf16[512,128]{1,0:T(8,128)(2,1)S(1)} %collective-permute-done.49.refs_2_), channel_id=1, source_target_pairs={{0,2},{2,4},{4,6},{6,7},{7,5},{5,3},{3,1},{1,0},{8,10},{10,12},{12... | collective-permute-start | bytes 393224 | tf_op jit(solution)/shard_map/ppermute | solution.py:134
  104.4 2.5 %shard_map.100.refs_0_ = f32[768,256]{1,0:T(8,128)S(1)} custom-call(bf16[768,8192]{1,0:T(8,128)(2,1)} %bitcast.81, f32[768,256]{1,0:T(8,128)S(1)} %shard_map.99.refs_0_, bf16[512,128]{1,0:T(8,128)(2,1)S(1)} %collective-permute-done.44.refs_1_, bf16[512,128]{1,0:T(8,128)(2,1)S(1)} %collective-permute-done.49.refs_2_, ...), custom_call_target="tpu_custom_call", output_to_operand_aliasing={{}: (1, {})} | custom-call | flops 402653184 | bytes 3145728 | tf_op jit(solution)/shard_map/pallas_call | solution.py:89
  106.9 1.5 %collective-permute-start.55 = (bf16[512,128]{1,0:T(8,128)(2,1)S(1)}, bf16[512,128]{1,0:T(8,128)(2,1)S(1)}, u32[]{:S(2)}, u32[]{:S(2)}) collective-permute-start(bf16[512,128]{1,0:T(8,128)(2,1)S(1)} %collective-permute-done.48.refs_1_), channel_id=1, source_target_pairs={{0,2},{2,4},{4,6},{6,7},{7,5},{5,3},{3,1},{1,0},{8,10},{10,12},{12... | collective-permute-start | bytes 393224 | tf_op jit(solution)/shard_map/ppermute | solution.py:134
  108.4 1.3 collective-permute-start.60
  111.2 2.5 %shard_map.101 = f32[768,256]{1,0:T(8,128)S(1)} custom-call(bf16[768,8192]{1,0:T(8,128)(2,1)} %bitcast.82, f32[768,256]{1,0:T(8,128)S(1)} %shard_map.100.refs_0_, bf16[512,128]{1,0:T(8,128)(2,1)S(1)} %collective-permute-done.48.refs_1_, bf16[512,128]{1,0:T(8,128)(2,1)S(1)} %collective-permute-done.52.refs_2_, ...), custom_call_target="tpu_custom_call", output_to_operand_aliasing={{}: (1, {})} | custom-call | flops 402653184 | bytes 3145728 | tf_op jit(solution)/shard_map/pallas_call | solution.py:89
  113.8 1.1 collective-permute-done.61.refs_2_
  114.9 2.3 %shard_map.103 = f32[768,128]{1,0:T(8,128)S(1)} custom-call(bf16[768,8192]{1,0:T(8,128)(2,1)} %bitcast.83, f32[768,128]{1,0:T(8,128)S(1)} %get-tuple-element.77.refs_0_, bf16[512,128]{1,0:T(8,128)(2,1)S(1)} %collective-permute-done.60.refs_1_, bf16[512,128]{1,0:T(8,128)(2,1)S(1)} %collective-permute-done.61.refs_2_), custom_call_target="tpu_custom_call", output_to_operand_aliasing={{}: (1, {})} | custom-call | flops 201326592 | bytes 2359296 | tf_op jit(solution)/shard_map/pallas_call | solution.py:89
  117.2 2.4 %shard_map.102 = f32[768,128]{1,0:T(8,128)S(1)} custom-call(bf16[768,8192]{1,0:T(8,128)(2,1)} %bitcast.84, f32[768,128]{1,0:T(8,128)S(1)} %get-tuple-element.76.refs_0_, bf16[512,128]{1,0:T(8,128)(2,1)S(1)} %collective-permute-done.55.refs_1_, bf16[512,128]{1,0:T(8,128)(2,1)S(1)} %collective-permute-done.56.refs_2_), custom_call_target="tpu_custom_call", output_to_operand_aliasing={{}: (1, {})} | custom-call | flops 201326592 | bytes 2359296 | tf_op jit(solution)/shard_map/pallas_call | solution.py:89
  122.3 1.4 %collective-permute-start.58 = (bf16[256,128]{1,0:T(8,128)(2,1)S(1)}, bf16[256,128]{1,0:T(8,128)(2,1)S(1)}, u32[]{:S(2)}, u32[]{:S(2)}) collective-permute-start(bf16[256,128]{1,0:T(8,128)(2,1)S(1)} %convolution_convert_fusion.5), channel_id=1, source_target_pairs={{0,16},{8,24},{16,0},{24,8},{1,17},{9,25},{17,1},{25,9},{2,18},{10... | collective-permute-start | bytes 196616 | tf_op jit(solution)/shard_map/ppermute | solution.py:192
  124.9 1.3 %collective-permute-start.63 = (bf16[256,128]{1,0:T(8,128)(2,1)S(1)}, bf16[256,128]{1,0:T(8,128)(2,1)S(1)}, u32[]{:S(2)}, u32[]{:S(2)}) collective-permute-start(bf16[256,128]{1,0:T(8,128)(2,1)S(1)} %convolution_convert_fusion.1), channel_id=1, source_target_pairs={{0,16},{8,24},{16,0},{24,8},{1,17},{9,25},{17,1},{25,9},{2,18},{10... | collective-permute-start | bytes 196616 | tf_op jit(solution)/shard_map/ppermute | solution.py:192
  126.9 1.0 collective-permute-done.59
  128.4 1.7 %collective-permute-done.63 = bf16[256,128]{1,0:T(8,128)(2,1)S(1)} collective-permute-done((bf16[256,128]{1,0:T(8,128)(2,1)S(1)}, bf16[256,128]{1,0:T(8,128)(2,1)S(1)}, u32[]{:S(2)}, u32[]{:S(2)}) %collective-permute-start.63) | collective-permute-done | bytes 65568 | tf_op jit(solution)/shard_map/ppermute | solution.py:192
  (133 shorter events, 21.9 us)
Async XLA Ops:
  1.8 8.0 %collective-permute-start = (bf16[512,128]{1,0:T(8,128)(2,1)S(1)}, bf16[512,128]{1,0:T(8,128)(2,1)S(1)}, u32[]{:S(2)}, u32[]{:S(2)}) collective-permute-start(bf16[512,128]{1,0:T(8,128)(2,1)S(1)} %get-tuple-element.81.refs_0_), channel_id=1, source_target_pairs={{0,2},{2,4},{4,6},{6,7},{7,5},{5,3},{3,1},{1,0},{8,10},{10,12},{12... | collective-permute-start | bytes 393224 | tf_op jit(solution)/shard_map/ppermute | solution.py:134
  4.8 7.0 %collective-permute-start.2 = (bf16[512,128]{1,0:T(8,128)(2,1)S(1)}, bf16[512,128]{1,0:T(8,128)(2,1)S(1)}, u32[]{:S(2)}, u32[]{:S(2)}) collective-permute-start(bf16[512,128]{1,0:T(8,128)(2,1)S(1)} %get-tuple-element.80.refs_1_), channel_id=1, source_target_pairs={{0,2},{2,4},{4,6},{6,7},{7,5},{5,3},{3,1},{1,0},{8,10},{10,12},{12... | collective-permute-start | bytes 393224 | tf_op jit(solution)/shard_map/ppermute | solution.py:134
  6.4 7.1 %collective-permute-start.3 = (bf16[512,128]{1,0:T(8,128)(2,1)S(1)}, bf16[512,128]{1,0:T(8,128)(2,1)S(1)}, u32[]{:S(2)}, u32[]{:S(2)}) collective-permute-start(bf16[512,128]{1,0:T(8,128)(2,1)S(1)} %get-tuple-element.79.refs_2_), channel_id=1, source_target_pairs={{2,0},{4,2},{6,4},{7,6},{5,7},{3,5},{1,3},{0,1},{10,8},{12,10},{14... | collective-permute-start | bytes 393224 | tf_op jit(solution)/shard_map/ppermute | solution.py:135
  6.9 7.1 %collective-permute-start.4 = (bf16[512,128]{1,0:T(8,128)(2,1)S(1)}, bf16[512,128]{1,0:T(8,128)(2,1)S(1)}, u32[]{:S(2)}, u32[]{:S(2)}) collective-permute-start(bf16[512,128]{1,0:T(8,128)(2,1)S(1)} %get-tuple-element.78.refs_3_), channel_id=1, source_target_pairs={{2,0},{4,2},{6,4},{7,6},{5,7},{3,5},{1,3},{0,1},{10,8},{12,10},{14... | collective-permute-start | bytes 393224 | tf_op jit(solution)/shard_map/ppermute | solution.py:135
  9.8 8.0 %collective-permute-start.1 = (bf16[512,128]{1,0:T(8,128)(2,1)S(1)}, bf16[512,128]{1,0:T(8,128)(2,1)S(1)}, u32[]{:S(2)}, u32[]{:S(2)}) collective-permute-start(bf16[512,128]{1,0:T(8,128)(2,1)S(1)} %collective-permute-done.refs_1_), channel_id=1, source_target_pairs={{0,2},{2,4},{4,6},{6,7},{7,5},{5,3},{3,1},{1,0},{8,10},{10,12},{12... | collective-permute-start | bytes 393224 | tf_op jit(solution)/shard_map/ppermute | solution.py:134
  11.8 8.9 %collective-permute-start.6 = (bf16[512,128]{1,0:T(8,128)(2,1)S(1)}, bf16[512,128]{1,0:T(8,128)(2,1)S(1)}, u32[]{:S(2)}, u32[]{:S(2)}) collective-permute-start(bf16[512,128]{1,0:T(8,128)(2,1)S(1)} %collective-permute-done.2.refs_2_), channel_id=1, source_target_pairs={{0,2},{2,4},{4,6},{6,7},{7,5},{5,3},{3,1},{1,0},{8,10},{10,12},{12... | collective-permute-start | bytes 393224 | tf_op jit(solution)/shard_map/ppermute | solution.py:134
  13.5 8.9 %collective-permute-start.7 = (bf16[512,128]{1,0:T(8,128)(2,1)S(1)}, bf16[512,128]{1,0:T(8,128)(2,1)S(1)}, u32[]{:S(2)}, u32[]{:S(2)}) collective-permute-start(bf16[512,128]{1,0:T(8,128)(2,1)S(1)} %collective-permute-done.3.refs_3_), channel_id=1, source_target_pairs={{2,0},{4,2},{6,4},{7,6},{5,7},{3,5},{1,3},{0,1},{10,8},{12,10},{14... | collective-permute-start | bytes 393224 | tf_op jit(solution)/shard_map/ppermute | solution.py:135
  13.9 9.0 %collective-permute-start.8 = (bf16[512,128]{1,0:T(8,128)(2,1)S(1)}, bf16[512,128]{1,0:T(8,128)(2,1)S(1)}, u32[]{:S(2)}, u32[]{:S(2)}) collective-permute-start(bf16[512,128]{1,0:T(8,128)(2,1)S(1)} %collective-permute-done.4.refs_4_), channel_id=1, source_target_pairs={{2,0},{4,2},{6,4},{7,6},{5,7},{3,5},{1,3},{0,1},{10,8},{12,10},{14... | collective-permute-start | bytes 393224 | tf_op jit(solution)/shard_map/ppermute | solution.py:135
  17.8 10.5 %collective-permute-start.5 = (bf16[512,128]{1,0:T(8,128)(2,1)S(1)}, bf16[512,128]{1,0:T(8,128)(2,1)S(1)}, u32[]{:S(2)}, u32[]{:S(2)}) collective-permute-start(bf16[512,128]{1,0:T(8,128)(2,1)S(1)} %collective-permute-done.1.refs_1_), channel_id=1, source_target_pairs={{0,2},{2,4},{4,6},{6,7},{7,5},{5,3},{3,1},{1,0},{8,10},{10,12},{12... | collective-permute-start | bytes 393224 | tf_op jit(solution)/shard_map/ppermute | solution.py:134
  20.6 9.1 %collective-permute-start.10 = (s32[256]{0:T(256)S(1)}, s32[256]{0:T(256)S(1)}, u32[]{:S(2)}, u32[]{:S(2)}) collective-permute-start(s32[256]{0:T(256)S(1)} %get-tuple-element.88), channel_id=1, source_target_pairs={{0,8},{8,0},{16,24},{24,16},{1,9},{9,1},{17,25},{25,17},{2,10},{10... | collective-permute-start | bytes 3080 | tf_op jit(solution)/shard_map/ppermute | solution.py:170
  20.7 10.1 %collective-permute-start.13 = (bf16[512,128]{1,0:T(8,128)(2,1)S(1)}, bf16[512,128]{1,0:T(8,128)(2,1)S(1)}, u32[]{:S(2)}, u32[]{:S(2)}) collective-permute-start(bf16[512,128]{1,0:T(8,128)(2,1)S(1)} %collective-permute-done.6.refs_2_), channel_id=1, source_target_pairs={{0,2},{2,4},{4,6},{6,7},{7,5},{5,3},{3,1},{1,0},{8,10},{10,12},{12... | collective-permute-start | bytes 393224 | tf_op jit(solution)/shard_map/ppermute | solution.py:134
  22.4 10.1 %collective-permute-start.14 = (bf16[512,128]{1,0:T(8,128)(2,1)S(1)}, bf16[512,128]{1,0:T(8,128)(2,1)S(1)}, u32[]{:S(2)}, u32[]{:S(2)}) collective-permute-start(bf16[512,128]{1,0:T(8,128)(2,1)S(1)} %collective-permute-done.7.refs_3_), channel_id=1, source_target_pairs={{2,0},{4,2},{6,4},{7,6},{5,7},{3,5},{1,3},{0,1},{10,8},{12,10},{14... | collective-permute-start | bytes 393224 | tf_op jit(solution)/shard_map/ppermute | solution.py:135
  22.9 10.0 %collective-permute-start.15 = (bf16[512,128]{1,0:T(8,128)(2,1)S(1)}, bf16[512,128]{1,0:T(8,128)(2,1)S(1)}, u32[]{:S(2)}, u32[]{:S(2)}) collective-permute-start(bf16[512,128]{1,0:T(8,128)(2,1)S(1)} %collective-permute-done.8.refs_4_), channel_id=1, source_target_pairs={{2,0},{4,2},{6,4},{7,6},{5,7},{3,5},{1,3},{0,1},{10,8},{12,10},{14... | collective-permute-start | bytes 393224 | tf_op jit(solution)/shard_map/ppermute | solution.py:135
  28.2 5.7 %collective-permute-start.11 = (s32[256]{0:T(256)S(1)}, s32[256]{0:T(256)S(1)}, u32[]{:S(2)}, u32[]{:S(2)}) collective-permute-start(s32[256]{0:T(256)S(1)} %get-tuple-element.87), channel_id=1, source_target_pairs={{0,16},{8,24},{16,0},{24,8},{1,17},{9,25},{17,1},{25,9},{2,18},{10... | collective-permute-start | bytes 3080 | tf_op jit(solution)/shard_map/ppermute | solution.py:170
  29.8 7.2 %collective-permute-start.9 = (bf16[512,128]{1,0:T(8,128)(2,1)S(1)}, bf16[512,128]{1,0:T(8,128)(2,1)S(1)}, u32[]{:S(2)}, u32[]{:S(2)}) collective-permute-start(bf16[512,128]{1,0:T(8,128)(2,1)S(1)} %collective-permute-done.5.refs_1_), channel_id=1, source_target_pairs={{0,2},{2,4},{4,6},{6,7},{7,5},{5,3},{3,1},{1,0},{8,10},{10,12},{12... | collective-permute-start | bytes 393224 | tf_op jit(solution)/shard_map/ppermute | solution.py:134
  30.9 8.2 %collective-permute-start.17 = (bf16[512,128]{1,0:T(8,128)(2,1)S(1)}, bf16[512,128]{1,0:T(8,128)(2,1)S(1)}, u32[]{:S(2)}, u32[]{:S(2)}) collective-permute-start(bf16[512,128]{1,0:T(8,128)(2,1)S(1)} %collective-permute-done.13.refs_2_), channel_id=1, source_target_pairs={{0,2},{2,4},{4,6},{6,7},{7,5},{5,3},{3,1},{1,0},{8,10},{10,12},{12... | collective-permute-start | bytes 393224 | tf_op jit(solution)/shard_map/ppermute | solution.py:134
  32.5 5.6 %collective-permute-start.18 = (bf16[512,128]{1,0:T(8,128)(2,1)S(1)}, bf16[512,128]{1,0:T(8,128)(2,1)S(1)}, u32[]{:S(2)}, u32[]{:S(2)}) collective-permute-start(bf16[512,128]{1,0:T(8,128)(2,1)S(1)} %collective-permute-done.14.refs_3_), channel_id=1, source_target_pairs={{2,0},{4,2},{6,4},{7,6},{5,7},{3,5},{1,3},{0,1},{10,8},{12,10},{14... | collective-permute-start | bytes 393224 | tf_op jit(solution)/shard_map/ppermute | solution.py:135
  32.9 7.2 %collective-permute-start.19 = (bf16[512,128]{1,0:T(8,128)(2,1)S(1)}, bf16[512,128]{1,0:T(8,128)(2,1)S(1)}, u32[]{:S(2)}, u32[]{:S(2)}) collective-permute-start(bf16[512,128]{1,0:T(8,128)(2,1)S(1)} %collective-permute-done.15.refs_4_), channel_id=1, source_target_pairs={{2,0},{4,2},{6,4},{7,6},{5,7},{3,5},{1,3},{0,1},{10,8},{12,10},{14... | collective-permute-start | bytes 393224 | tf_op jit(solution)/shard_map/ppermute | solution.py:135
  37.0 6.9 %collective-permute-start.16 = (bf16[512,128]{1,0:T(8,128)(2,1)S(1)}, bf16[512,128]{1,0:T(8,128)(2,1)S(1)}, u32[]{:S(2)}, u32[]{:S(2)}) collective-permute-start(bf16[512,128]{1,0:T(8,128)(2,1)S(1)} %collective-permute-done.9.refs_1_), channel_id=1, source_target_pairs={{0,2},{2,4},{4,6},{6,7},{7,5},{5,3},{3,1},{1,0},{8,10},{10,12},{12... | collective-permute-start | bytes 393224 | tf_op jit(solution)/shard_map/ppermute | solution.py:134
  38.1 7.0 %collective-permute-start.22 = (bf16[512,128]{1,0:T(8,128)(2,1)S(1)}, bf16[512,128]{1,0:T(8,128)(2,1)S(1)}, u32[]{:S(2)}, u32[]{:S(2)}) collective-permute-start(bf16[512,128]{1,0:T(8,128)(2,1)S(1)} %collective-permute-done.18.refs_3_), channel_id=1, source_target_pairs={{2,0},{4,2},{6,4},{7,6},{5,7},{3,5},{1,3},{0,1},{10,8},{12,10},{14... | collective-permute-start | bytes 393224 | tf_op jit(solution)/shard_map/ppermute | solution.py:135
  39.0 7.0 %collective-permute-start.21 = (bf16[512,128]{1,0:T(8,128)(2,1)S(1)}, bf16[512,128]{1,0:T(8,128)(2,1)S(1)}, u32[]{:S(2)}, u32[]{:S(2)}) collective-permute-start(bf16[512,128]{1,0:T(8,128)(2,1)S(1)} %collective-permute-done.17.refs_2_), channel_id=1, source_target_pairs={{0,2},{2,4},{4,6},{6,7},{7,5},{5,3},{3,1},{1,0},{8,10},{10,12},{12... | collective-permute-start | bytes 393224 | tf_op jit(solution)/shard_map/ppermute | solution.py:134
  40.1 7.0 %collective-permute-start.23 = (bf16[512,128]{1,0:T(8,128)(2,1)S(1)}, bf16[512,128]{1,0:T(8,128)(2,1)S(1)}, u32[]{:S(2)}, u32[]{:S(2)}) collective-permute-start(bf16[512,128]{1,0:T(8,128)(2,1)S(1)} %collective-permute-done.19.refs_4_), channel_id=1, source_target_pairs={{2,0},{4,2},{6,4},{7,6},{5,7},{3,5},{1,3},{0,1},{10,8},{12,10},{14... | collective-permute-start | bytes 393224 | tf_op jit(solution)/shard_map/ppermute | solution.py:135
  44.0 7.0 %collective-permute-start.20 = (bf16[512,128]{1,0:T(8,128)(2,1)S(1)}, bf16[512,128]{1,0:T(8,128)(2,1)S(1)}, u32[]{:S(2)}, u32[]{:S(2)}) collective-permute-start(bf16[512,128]{1,0:T(8,128)(2,1)S(1)} %collective-permute-done.16.refs_1_), channel_id=1, source_target_pairs={{0,2},{2,4},{4,6},{6,7},{7,5},{5,3},{3,1},{1,0},{8,10},{10,12},{12... | collective-permute-start | bytes 393224 | tf_op jit(solution)/shard_map/ppermute | solution.py:134
  45.1 7.0 %collective-permute-start.25 = (bf16[512,128]{1,0:T(8,128)(2,1)S(1)}, bf16[512,128]{1,0:T(8,128)(2,1)S(1)}, u32[]{:S(2)}, u32[]{:S(2)}) collective-permute-start(bf16[512,128]{1,0:T(8,128)(2,1)S(1)} %collective-permute-done.22.refs_3_), channel_id=1, source_target_pairs={{2,0},{4,2},{6,4},{7,6},{5,7},{3,5},{1,3},{0,1},{10,8},{12,10},{14... | collective-permute-start | bytes 393224 | tf_op jit(solution)/shard_map/ppermute | solution.py:135
  46.0 7.0 %collective-permute-start.24 = (bf16[512,128]{1,0:T(8,128)(2,1)S(1)}, bf16[512,128]{1,0:T(8,128)(2,1)S(1)}, u32[]{:S(2)}, u32[]{:S(2)}) collective-permute-start(bf16[512,128]{1,0:T(8,128)(2,1)S(1)} %collective-permute-done.21.refs_2_), channel_id=1, source_target_pairs={{0,2},{2,4},{4,6},{6,7},{7,5},{5,3},{3,1},{1,0},{8,10},{10,12},{12... | collective-permute-start | bytes 393224 | tf_op jit(solution)/shard_map/ppermute | solution.py:134
  47.1 7.0 %collective-permute-start.26 = (bf16[512,128]{1,0:T(8,128)(2,1)S(1)}, bf16[512,128]{1,0:T(8,128)(2,1)S(1)}, u32[]{:S(2)}, u32[]{:S(2)}) collective-permute-start(bf16[512,128]{1,0:T(8,128)(2,1)S(1)} %collective-permute-done.23.refs_4_), channel_id=1, source_target_pairs={{2,0},{4,2},{6,4},{7,6},{5,7},{3,5},{1,3},{0,1},{10,8},{12,10},{14... | collective-permute-start | bytes 393224 | tf_op jit(solution)/shard_map/ppermute | solution.py:135
  51.0 7.1 %collective-permute-start.27 = (bf16[512,128]{1,0:T(8,128)(2,1)S(1)}, bf16[512,128]{1,0:T(8,128)(2,1)S(1)}, u32[]{:S(2)}, u32[]{:S(2)}) collective-permute-start(bf16[512,128]{1,0:T(8,128)(2,1)S(1)} %collective-permute-done.20.refs_1_), channel_id=1, source_target_pairs={{0,2},{2,4},{4,6},{6,7},{7,5},{5,3},{3,1},{1,0},{8,10},{10,12},{12... | collective-permute-start | bytes 393224 | tf_op jit(solution)/shard_map/ppermute | solution.py:134
  52.1 5.9 %collective-permute-start.28 = (bf16[512,128]{1,0:T(8,128)(2,1)S(1)}, bf16[512,128]{1,0:T(8,128)(2,1)S(1)}, u32[]{:S(2)}, u32[]{:S(2)}) collective-permute-start(bf16[512,128]{1,0:T(8,128)(2,1)S(1)} %collective-permute-done.25.refs_3_), channel_id=1, source_target_pairs={{2,0},{4,2},{6,4},{7,6},{5,7},{3,5},{1,3},{0,1},{10,8},{12,10},{14... | collective-permute-start | bytes 393224 | tf_op jit(solution)/shard_map/ppermute | solution.py:135
  53.0 7.8 %collective-permute-start.29 = (bf16[512,128]{1,0:T(8,128)(2,1)S(1)}, bf16[512,128]{1,0:T(8,128)(2,1)S(1)}, u32[]{:S(2)}, u32[]{:S(2)}) collective-permute-start(bf16[512,128]{1,0:T(8,128)(2,1)S(1)} %collective-permute-done.24.refs_2_), channel_id=1, source_target_pairs={{0,2},{2,4},{4,6},{6,7},{7,5},{5,3},{3,1},{1,0},{8,10},{10,12},{12... | collective-permute-start | bytes 393224 | tf_op jit(solution)/shard_map/ppermute | solution.py:134
  54.1 6.8 %collective-permute-start.30 = (bf16[512,128]{1,0:T(8,128)(2,1)S(1)}, bf16[512,128]{1,0:T(8,128)(2,1)S(1)}, u32[]{:S(2)}, u32[]{:S(2)}) collective-permute-start(bf16[512,128]{1,0:T(8,128)(2,1)S(1)} %collective-permute-done.26.refs_4_), channel_id=1, source_target_pairs={{2,0},{4,2},{6,4},{7,6},{5,7},{3,5},{1,3},{0,1},{10,8},{12,10},{14... | collective-permute-start | bytes 393224 | tf_op jit(solution)/shard_map/ppermute | solution.py:135
  63.8 6.4 %collective-permute-start.31 = (bf16[512,128]{1,0:T(8,128)(2,1)S(1)}, bf16[512,128]{1,0:T(8,128)(2,1)S(1)}, u32[]{:S(2)}, u32[]{:S(2)}) collective-permute-start(bf16[512,128]{1,0:T(8,128)(2,1)S(1)} %get-tuple-element.92.refs_0_), channel_id=1, source_target_pairs={{0,2},{2,4},{4,6},{6,7},{7,5},{5,3},{3,1},{1,0},{8,10},{10,12},{12... | collective-permute-start | bytes 393224 | tf_op jit(solution)/shard_map/ppermute | solution.py:134
  65.1 6.4 %collective-permute-start.33 = (bf16[512,128]{1,0:T(8,128)(2,1)S(1)}, bf16[512,128]{1,0:T(8,128)(2,1)S(1)}, u32[]{:S(2)}, u32[]{:S(2)}) collective-permute-start(bf16[512,128]{1,0:T(8,128)(2,1)S(1)} %get-tuple-element.83.refs_1_), channel_id=1, source_target_pairs={{0,2},{2,4},{4,6},{6,7},{7,5},{5,3},{3,1},{1,0},{8,10},{10,12},{12... | collective-permute-start | bytes 393224 | tf_op jit(solution)/shard_map/ppermute | solution.py:134
  66.7 6.4 %collective-permute-start.34 = (bf16[512,128]{1,0:T(8,128)(2,1)S(1)}, bf16[512,128]{1,0:T(8,128)(2,1)S(1)}, u32[]{:S(2)}, u32[]{:S(2)}) collective-permute-start(bf16[512,128]{1,0:T(8,128)(2,1)S(1)} %get-tuple-element.93.refs_2_), channel_id=1, source_target_pairs={{2,0},{4,2},{6,4},{7,6},{5,7},{3,5},{1,3},{0,1},{10,8},{12,10},{14... | collective-permute-start | bytes 393224 | tf_op jit(solution)/shard_map/ppermute | solution.py:135
  67.1 7.2 %collective-permute-start.35 = (bf16[512,128]{1,0:T(8,128)(2,1)S(1)}, bf16[512,128]{1,0:T(8,128)(2,1)S(1)}, u32[]{:S(2)}, u32[]{:S(2)}) collective-permute-start(bf16[512,128]{1,0:T(8,128)(2,1)S(1)} %get-tuple-element.82.refs_3_), channel_id=1, source_target_pairs={{2,0},{4,2},{6,4},{7,6},{5,7},{3,5},{1,3},{0,1},{10,8},{12,10},{14... | collective-permute-start | bytes 393224 | tf_op jit(solution)/shard_map/ppermute | solution.py:135
  70.2 7.1 %collective-permute-start.32 = (bf16[512,128]{1,0:T(8,128)(2,1)S(1)}, bf16[512,128]{1,0:T(8,128)(2,1)S(1)}, u32[]{:S(2)}, u32[]{:S(2)}) collective-permute-start(bf16[512,128]{1,0:T(8,128)(2,1)S(1)} %collective-permute-done.31.refs_1_), channel_id=1, source_target_pairs={{0,2},{2,4},{4,6},{6,7},{7,5},{5,3},{3,1},{1,0},{8,10},{10,12},{12... | collective-permute-start | bytes 393224 | tf_op jit(solution)/shard_map/ppermute | solution.py:134
  71.5 7.4 %collective-permute-start.37 = (bf16[512,128]{1,0:T(8,128)(2,1)S(1)}, bf16[512,128]{1,0:T(8,128)(2,1)S(1)}, u32[]{:S(2)}, u32[]{:S(2)}) collective-permute-start(bf16[512,128]{1,0:T(8,128)(2,1)S(1)} %collective-permute-done.33.refs_2_), channel_id=1, source_target_pairs={{0,2},{2,4},{4,6},{6,7},{7,5},{5,3},{3,1},{1,0},{8,10},{10,12},{12... | collective-permute-start | bytes 393224 | tf_op jit(solution)/shard_map/ppermute | solution.py:134
  73.1 7.3 %collective-permute-start.38 = (bf16[512,128]{1,0:T(8,128)(2,1)S(1)}, bf16[512,128]{1,0:T(8,128)(2,1)S(1)}, u32[]{:S(2)}, u32[]{:S(2)}) collective-permute-start(bf16[512,128]{1,0:T(8,128)(2,1)S(1)} %collective-permute-done.34.refs_3_), channel_id=1, source_target_pairs={{2,0},{4,2},{6,4},{7,6},{5,7},{3,5},{1,3},{0,1},{10,8},{12,10},{14... | collective-permute-start | bytes 393224 | tf_op jit(solution)/shard_map/ppermute | solution.py:135
  74.3 7.3 %collective-permute-start.39 = (bf16[512,128]{1,0:T(8,128)(2,1)S(1)}, bf16[512,128]{1,0:T(8,128)(2,1)S(1)}, u32[]{:S(2)}, u32[]{:S(2)}) collective-permute-start(bf16[512,128]{1,0:T(8,128)(2,1)S(1)} %collective-permute-done.35.refs_4_), channel_id=1, source_target_pairs={{2,0},{4,2},{6,4},{7,6},{5,7},{3,5},{1,3},{0,1},{10,8},{12,10},{14... | collective-permute-start | bytes 393224 | tf_op jit(solution)/shard_map/ppermute | solution.py:135
  77.3 7.3 %collective-permute-start.36 = (bf16[512,128]{1,0:T(8,128)(2,1)S(1)}, bf16[512,128]{1,0:T(8,128)(2,1)S(1)}, u32[]{:S(2)}, u32[]{:S(2)}) collective-permute-start(bf16[512,128]{1,0:T(8,128)(2,1)S(1)} %collective-permute-done.32.refs_1_), channel_id=1, source_target_pairs={{0,2},{2,4},{4,6},{6,7},{7,5},{5,3},{3,1},{1,0},{8,10},{10,12},{12... | collective-permute-start | bytes 393224 | tf_op jit(solution)/shard_map/ppermute | solution.py:134
  78.9 7.3 %collective-permute-start.41 = (bf16[512,128]{1,0:T(8,128)(2,1)S(1)}, bf16[512,128]{1,0:T(8,128)(2,1)S(1)}, u32[]{:S(2)}, u32[]{:S(2)}) collective-permute-start(bf16[512,128]{1,0:T(8,128)(2,1)S(1)} %collective-permute-done.37.refs_2_), channel_id=1, source_target_pairs={{0,2},{2,4},{4,6},{6,7},{7,5},{5,3},{3,1},{1,0},{8,10},{10,12},{12... | collective-permute-start | bytes 393224 | tf_op jit(solution)/shard_map/ppermute | solution.py:134
  80.4 7.4 %collective-permute-start.42 = (bf16[512,128]{1,0:T(8,128)(2,1)S(1)}, bf16[512,128]{1,0:T(8,128)(2,1)S(1)}, u32[]{:S(2)}, u32[]{:S(2)}) collective-permute-start(bf16[512,128]{1,0:T(8,128)(2,1)S(1)} %collective-permute-done.38.refs_3_), channel_id=1, source_target_pairs={{2,0},{4,2},{6,4},{7,6},{5,7},{3,5},{1,3},{0,1},{10,8},{12,10},{14... | collective-permute-start | bytes 393224 | tf_op jit(solution)/shard_map/ppermute | solution.py:135
  81.7 7.8 %collective-permute-start.43 = (bf16[512,128]{1,0:T(8,128)(2,1)S(1)}, bf16[512,128]{1,0:T(8,128)(2,1)S(1)}, u32[]{:S(2)}, u32[]{:S(2)}) collective-permute-start(bf16[512,128]{1,0:T(8,128)(2,1)S(1)} %collective-permute-done.39.refs_4_), channel_id=1, source_target_pairs={{2,0},{4,2},{6,4},{7,6},{5,7},{3,5},{1,3},{0,1},{10,8},{12,10},{14... | collective-permute-start | bytes 393224 | tf_op jit(solution)/shard_map/ppermute | solution.py:135
  84.6 7.9 %collective-permute-start.40 = (bf16[512,128]{1,0:T(8,128)(2,1)S(1)}, bf16[512,128]{1,0:T(8,128)(2,1)S(1)}, u32[]{:S(2)}, u32[]{:S(2)}) collective-permute-start(bf16[512,128]{1,0:T(8,128)(2,1)S(1)} %collective-permute-done.36.refs_1_), channel_id=1, source_target_pairs={{0,2},{2,4},{4,6},{6,7},{7,5},{5,3},{3,1},{1,0},{8,10},{10,12},{12... | collective-permute-start | bytes 393224 | tf_op jit(solution)/shard_map/ppermute | solution.py:134
  86.3 7.8 %collective-permute-start.45 = (bf16[512,128]{1,0:T(8,128)(2,1)S(1)}, bf16[512,128]{1,0:T(8,128)(2,1)S(1)}, u32[]{:S(2)}, u32[]{:S(2)}) collective-permute-start(bf16[512,128]{1,0:T(8,128)(2,1)S(1)} %collective-permute-done.41.refs_2_), channel_id=1, source_target_pairs={{0,2},{2,4},{4,6},{6,7},{7,5},{5,3},{3,1},{1,0},{8,10},{10,12},{12... | collective-permute-start | bytes 393224 | tf_op jit(solution)/shard_map/ppermute | solution.py:134
  87.8 7.6 %collective-permute-start.46 = (bf16[512,128]{1,0:T(8,128)(2,1)S(1)}, bf16[512,128]{1,0:T(8,128)(2,1)S(1)}, u32[]{:S(2)}, u32[]{:S(2)}) collective-permute-start(bf16[512,128]{1,0:T(8,128)(2,1)S(1)} %collective-permute-done.42.refs_3_), channel_id=1, source_target_pairs={{2,0},{4,2},{6,4},{7,6},{5,7},{3,5},{1,3},{0,1},{10,8},{12,10},{14... | collective-permute-start | bytes 393224 | tf_op jit(solution)/shard_map/ppermute | solution.py:135
  89.5 6.7 %collective-permute-start.47 = (bf16[512,128]{1,0:T(8,128)(2,1)S(1)}, bf16[512,128]{1,0:T(8,128)(2,1)S(1)}, u32[]{:S(2)}, u32[]{:S(2)}) collective-permute-start(bf16[512,128]{1,0:T(8,128)(2,1)S(1)} %collective-permute-done.43.refs_4_), channel_id=1, source_target_pairs={{2,0},{4,2},{6,4},{7,6},{5,7},{3,5},{1,3},{0,1},{10,8},{12,10},{14... | collective-permute-start | bytes 393224 | tf_op jit(solution)/shard_map/ppermute | solution.py:135
  92.5 6.7 %collective-permute-start.44 = (bf16[512,128]{1,0:T(8,128)(2,1)S(1)}, bf16[512,128]{1,0:T(8,128)(2,1)S(1)}, u32[]{:S(2)}, u32[]{:S(2)}) collective-permute-start(bf16[512,128]{1,0:T(8,128)(2,1)S(1)} %collective-permute-done.40.refs_1_), channel_id=1, source_target_pairs={{0,2},{2,4},{4,6},{6,7},{7,5},{5,3},{3,1},{1,0},{8,10},{10,12},{12... | collective-permute-start | bytes 393224 | tf_op jit(solution)/shard_map/ppermute | solution.py:134
  94.1 6.7 %collective-permute-start.49 = (bf16[512,128]{1,0:T(8,128)(2,1)S(1)}, bf16[512,128]{1,0:T(8,128)(2,1)S(1)}, u32[]{:S(2)}, u32[]{:S(2)}) collective-permute-start(bf16[512,128]{1,0:T(8,128)(2,1)S(1)} %collective-permute-done.45.refs_2_), channel_id=1, source_target_pairs={{0,2},{2,4},{4,6},{6,7},{7,5},{5,3},{3,1},{1,0},{8,10},{10,12},{12... | collective-permute-start | bytes 393224 | tf_op jit(solution)/shard_map/ppermute | solution.py:134
  95.4 6.8 %collective-permute-start.50 = (bf16[512,128]{1,0:T(8,128)(2,1)S(1)}, bf16[512,128]{1,0:T(8,128)(2,1)S(1)}, u32[]{:S(2)}, u32[]{:S(2)}) collective-permute-start(bf16[512,128]{1,0:T(8,128)(2,1)S(1)} %collective-permute-done.46.refs_3_), channel_id=1, source_target_pairs={{2,0},{4,2},{6,4},{7,6},{5,7},{3,5},{1,3},{0,1},{10,8},{12,10},{14... | collective-permute-start | bytes 393224 | tf_op jit(solution)/shard_map/ppermute | solution.py:135
  96.2 6.8 %collective-permute-start.51 = (bf16[512,128]{1,0:T(8,128)(2,1)S(1)}, bf16[512,128]{1,0:T(8,128)(2,1)S(1)}, u32[]{:S(2)}, u32[]{:S(2)}) collective-permute-start(bf16[512,128]{1,0:T(8,128)(2,1)S(1)} %collective-permute-done.47.refs_4_), channel_id=1, source_target_pairs={{2,0},{4,2},{6,4},{7,6},{5,7},{3,5},{1,3},{0,1},{10,8},{12,10},{14... | collective-permute-start | bytes 393224 | tf_op jit(solution)/shard_map/ppermute | solution.py:135
  99.2 7.7 %collective-permute-start.48 = (bf16[512,128]{1,0:T(8,128)(2,1)S(1)}, bf16[512,128]{1,0:T(8,128)(2,1)S(1)}, u32[]{:S(2)}, u32[]{:S(2)}) collective-permute-start(bf16[512,128]{1,0:T(8,128)(2,1)S(1)} %collective-permute-done.44.refs_1_), channel_id=1, source_target_pairs={{0,2},{2,4},{4,6},{6,7},{7,5},{5,3},{3,1},{1,0},{8,10},{10,12},{12... | collective-permute-start | bytes 393224 | tf_op jit(solution)/shard_map/ppermute | solution.py:134
  100.8 7.6 %collective-permute-start.52 = (bf16[512,128]{1,0:T(8,128)(2,1)S(1)}, bf16[512,128]{1,0:T(8,128)(2,1)S(1)}, u32[]{:S(2)}, u32[]{:S(2)}) collective-permute-start(bf16[512,128]{1,0:T(8,128)(2,1)S(1)} %collective-permute-done.49.refs_2_), channel_id=1, source_target_pairs={{0,2},{2,4},{4,6},{6,7},{7,5},{5,3},{3,1},{1,0},{8,10},{10,12},{12... | collective-permute-start | bytes 393224 | tf_op jit(solution)/shard_map/ppermute | solution.py:134
  102.3 8.2 %collective-permute-start.53 = (bf16[512,128]{1,0:T(8,128)(2,1)S(1)}, bf16[512,128]{1,0:T(8,128)(2,1)S(1)}, u32[]{:S(2)}, u32[]{:S(2)}) collective-permute-start(bf16[512,128]{1,0:T(8,128)(2,1)S(1)} %collective-permute-done.50.refs_3_), channel_id=1, source_target_pairs={{2,0},{4,2},{6,4},{7,6},{5,7},{3,5},{1,3},{0,1},{10,8},{12,10},{14... | collective-permute-start | bytes 393224 | tf_op jit(solution)/shard_map/ppermute | solution.py:135
  103.0 6.9 %collective-permute-start.54 = (bf16[512,128]{1,0:T(8,128)(2,1)S(1)}, bf16[512,128]{1,0:T(8,128)(2,1)S(1)}, u32[]{:S(2)}, u32[]{:S(2)}) collective-permute-start(bf16[512,128]{1,0:T(8,128)(2,1)S(1)} %collective-permute-done.51.refs_4_), channel_id=1, source_target_pairs={{2,0},{4,2},{6,4},{7,6},{5,7},{3,5},{1,3},{0,1},{10,8},{12,10},{14... | collective-permute-start | bytes 393224 | tf_op jit(solution)/shard_map/ppermute | solution.py:135
  106.9 10.3 %collective-permute-start.55 = (bf16[512,128]{1,0:T(8,128)(2,1)S(1)}, bf16[512,128]{1,0:T(8,128)(2,1)S(1)}, u32[]{:S(2)}, u32[]{:S(2)}) collective-permute-start(bf16[512,128]{1,0:T(8,128)(2,1)S(1)} %collective-permute-done.48.refs_1_), channel_id=1, source_target_pairs={{0,2},{2,4},{4,6},{6,7},{7,5},{5,3},{3,1},{1,0},{8,10},{10,12},{12... | collective-permute-start | bytes 393224 | tf_op jit(solution)/shard_map/ppermute | solution.py:134
  108.4 5.4 %collective-permute-start.60 = (bf16[512,128]{1,0:T(8,128)(2,1)S(1)}, bf16[512,128]{1,0:T(8,128)(2,1)S(1)}, u32[]{:S(2)}, u32[]{:S(2)}) collective-permute-start(bf16[512,128]{1,0:T(8,128)(2,1)S(1)} %collective-permute-done.52.refs_2_), channel_id=1, source_target_pairs={{0,2},{2,4},{4,6},{6,7},{7,5},{5,3},{3,1},{1,0},{8,10},{10,12},{12... | collective-permute-start | bytes 393224 | tf_op jit(solution)/shard_map/ppermute | solution.py:134
  109.9 5.0 %collective-permute-start.61 = (bf16[512,128]{1,0:T(8,128)(2,1)S(1)}, bf16[512,128]{1,0:T(8,128)(2,1)S(1)}, u32[]{:S(2)}, u32[]{:S(2)}) collective-permute-start(bf16[512,128]{1,0:T(8,128)(2,1)S(1)} %collective-permute-done.54.refs_4_), channel_id=1, source_target_pairs={{2,0},{4,2},{6,4},{7,6},{5,7},{3,5},{1,3},{0,1},{10,8},{12,10},{14... | collective-permute-start | bytes 393224 | tf_op jit(solution)/shard_map/ppermute | solution.py:135
  110.5 6.7 %collective-permute-start.56 = (bf16[512,128]{1,0:T(8,128)(2,1)S(1)}, bf16[512,128]{1,0:T(8,128)(2,1)S(1)}, u32[]{:S(2)}, u32[]{:S(2)}) collective-permute-start(bf16[512,128]{1,0:T(8,128)(2,1)S(1)} %collective-permute-done.53.refs_3_), channel_id=1, source_target_pairs={{2,0},{4,2},{6,4},{7,6},{5,7},{3,5},{1,3},{0,1},{10,8},{12,10},{14... | collective-permute-start | bytes 393224 | tf_op jit(solution)/shard_map/ppermute | solution.py:135
  122.3 4.3 %collective-permute-start.58 = (bf16[256,128]{1,0:T(8,128)(2,1)S(1)}, bf16[256,128]{1,0:T(8,128)(2,1)S(1)}, u32[]{:S(2)}, u32[]{:S(2)}) collective-permute-start(bf16[256,128]{1,0:T(8,128)(2,1)S(1)} %convolution_convert_fusion.5), channel_id=1, source_target_pairs={{0,16},{8,24},{16,0},{24,8},{1,17},{9,25},{17,1},{25,9},{2,18},{10... | collective-permute-start | bytes 196616 | tf_op jit(solution)/shard_map/ppermute | solution.py:192
  123.9 4.2 %collective-permute-start.57 = (bf16[256,128]{1,0:T(8,128)(2,1)S(1)}, bf16[256,128]{1,0:T(8,128)(2,1)S(1)}, u32[]{:S(2)}, u32[]{:S(2)}) collective-permute-start(bf16[256,128]{1,0:T(8,128)(2,1)S(1)} %convolution_convert_fusion.6), channel_id=1, source_target_pairs={{0,8},{8,0},{16,24},{24,16},{1,9},{9,1},{17,25},{25,17},{2,10},{10... | collective-permute-start | bytes 196616 | tf_op jit(solution)/shard_map/ppermute | solution.py:192
  124.0 3.9 %collective-permute-start.59 = (bf16[256,128]{1,0:T(8,128)(2,1)S(1)}, bf16[256,128]{1,0:T(8,128)(2,1)S(1)}, u32[]{:S(2)}, u32[]{:S(2)}) collective-permute-start(bf16[256,128]{1,0:T(8,128)(2,1)S(1)} %convolution_convert_fusion.4), channel_id=1, source_target_pairs={{0,24},{8,16},{16,8},{24,0},{1,25},{9,17},{17,9},{25,1},{2,26},{10... | collective-permute-start | bytes 196616 | tf_op jit(solution)/shard_map/ppermute | solution.py:192
  124.8 6.5 %collective-permute-start.62 = (bf16[256,128]{1,0:T(8,128)(2,1)S(1)}, bf16[256,128]{1,0:T(8,128)(2,1)S(1)}, u32[]{:S(2)}, u32[]{:S(2)}) collective-permute-start(bf16[256,128]{1,0:T(8,128)(2,1)S(1)} %convolution_convert_fusion.2), channel_id=1, source_target_pairs={{0,8},{8,0},{16,24},{24,16},{1,9},{9,1},{17,25},{25,17},{2,10},{10... | collective-permute-start | bytes 196616 | tf_op jit(solution)/shard_map/ppermute | solution.py:192
  124.9 5.2 %collective-permute-start.63 = (bf16[256,128]{1,0:T(8,128)(2,1)S(1)}, bf16[256,128]{1,0:T(8,128)(2,1)S(1)}, u32[]{:S(2)}, u32[]{:S(2)}) collective-permute-start(bf16[256,128]{1,0:T(8,128)(2,1)S(1)} %convolution_convert_fusion.1), channel_id=1, source_target_pairs={{0,16},{8,24},{16,0},{24,8},{1,17},{9,25},{17,1},{25,9},{2,18},{10... | collective-permute-start | bytes 196616 | tf_op jit(solution)/shard_map/ppermute | solution.py:192
  126.6 4.5 %collective-permute-start.64 = (bf16[256,128]{1,0:T(8,128)(2,1)S(1)}, bf16[256,128]{1,0:T(8,128)(2,1)S(1)}, u32[]{:S(2)}, u32[]{:S(2)}) collective-permute-start(bf16[256,128]{1,0:T(8,128)(2,1)S(1)} %convolution_convert_fusion), channel_id=1, source_target_pairs={{0,24},{8,16},{16,8},{24,0},{1,25},{9,17},{17,9},{25,1},{2,26},{10... | collective-permute-start | bytes 196616 | tf_op jit(solution)/shard_map/ppermute | solution.py:192
  (6 other events, 29.8 us)

commit v3 on v1

--- a/solution.py
+++ b/solution.py
@@ -8,26 +8,7 @@
 
 CAPACITY = 2
 LANES = 128
-ROUTING_STEPS = (2, 4)
-
-
-def ring_order(count):
-    if count % 8:
-        return list(range(count))
-    depth = 4
-    columns = count // depth
-    walk = [z * columns for z in range(depth)]
-    for step, z in enumerate(range(depth - 1, -1, -1)):
-        ys = range(1, columns) if step % 2 == 0 else range(columns - 1, 0, -1)
-        walk += [z * columns + y for y in ys]
-    return walk
-
-
-def lookup(table, index):
-    result = jnp.int32(table[0])
-    for place in range(1, len(table)):
-        result = jnp.where(index == place, jnp.int32(table[place]), result)
-    return result
+DEPTH = 4
 
 
 def row_major(array):
@@ -54,13 +35,12 @@
         cost_estimate=pl.CostEstimate(
             flops=0, bytes_accessed=2 * matrix.size * matrix.dtype.itemsize, transcendentals=0
         ),
-    )(matrix)
+    )(pltpu.with_memory_space_constraint(matrix, pltpu.HBM))
 
 
 def body(inv_diag, below, rhs, tile_count, tile_owner, tile_rows, parent_rhs):
     width = rhs.shape[2]
     rows = rhs.shape[1]
-    half = rows // 2
     tiles = tile_owner.shape[1]
     height = tile_rows.shape[2]
     parent_height = parent_rhs.shape[1]
@@ -68,41 +48,53 @@
     wide = lax.axis_size("wide")
     me = lax.axis_index("front")
     wide_index = lax.axis_index("wide")
-    order = ring_order(wide)
-    place = lookup([order.index(i) for i in range(wide)], wide_index)
-    onward = [(order[i], order[(i + 1) % wide]) for i in range(wide)]
-    backward = [(b, a) for a, b in onward]
-    from_left = [lookup(order, (place + wide - step) % wide) for step in range(wide)]
-    from_right = [lookup(order, (place + step) % wide) for step in range(wide)]
+    depth = DEPTH if wide % DEPTH == 0 else 1
+    across = wide // depth
+    z, y = wide_index // across, wide_index % across
+    z_ring = [(i, (i + across) % wide) for i in range(wide)]
+    y_shifts = [
+        [(i, i // across * across + (i + shift) % across) for i in range(wide)]
+        for shift in range(across)
+    ]
 
-    def part(matrix, index, offset, values):
-        columns = lax.dynamic_slice_in_dim(matrix, index * rows + offset, values.shape[0], 1)
+    def block_of(step, shift):
+        return (z + depth - step) % depth * across + (y + across - shift) % across
+
+    def part(matrix, step, shift, values):
+        columns = lax.dynamic_slice_in_dim(matrix, block_of(step, shift) * rows, rows, 1)
         return dot(columns, values)
 
-    def ring_products(matrix, blocks, aside=None):
-        travelling = [(block[:half], block[half:]) for block in blocks]
-        total = part(matrix, wide_index, 0, jnp.concatenate(blocks, axis=1))
+    def gathered_product(matrix, blocks, later=None, aside=None):
+        column_count = len(blocks)
+        held_now = list(blocks)
+        total = part(matrix, 0, 0, jnp.concatenate(blocks, axis=1))
+        waiting = []
         extra = None
-        for step in range(1, wide):
-            for column, (first, second) in enumerate(travelling):
-                first = lax.ppermute(first, "wide", onward)
-                second = lax.ppermute(second, "wide", backward)
-                if aside and column == 0 and step == ROUTING_STEPS[0]:
-                    extra, first = aside(first)
-                if aside and column == 0 and step == ROUTING_STEPS[1]:
-                    first, extra = lax.optimization_barrier((first, extra))
-                travelling[column] = (first, second)
-            if step < wide - 1:
-                firsts, seconds = [jnp.concatenate(pieces, axis=1) for pieces in zip(*travelling)]
-                total = total + part(matrix, from_left[step], 0, firsts)
-                total = total + part(matrix, from_right[step], half, seconds)
+        for step in range(depth):
+            if step:
+                held_now = following
+                held_now[0], total, later = lax.optimization_barrier((held_now[0], total, later))
+            if aside and step == 1:
+                extra, held_now[0] = aside(held_now[0])
+            if aside and step == depth - 1:
+                held_now[0], extra = lax.optimization_barrier((held_now[0], extra))
+            following = [lax.ppermute(b, "wide", z_ring) for b in held_now] if step < depth - 1 else None
+            passed = [
+                [lax.ppermute(b, "wide", y_shifts[shift]) for b in held_now]
+                for shift in range(1, across)
+            ]
+            if step:
+                total = total + part(matrix, step, 0, jnp.concatenate(held_now, axis=1))
+            for at, shift, pieces in waiting:
+                total = total + part(matrix, at, shift, jnp.concatenate(pieces, axis=1))
+            waiting = [(step, shift, passed[shift - 1]) for shift in range(1, across)]
         results = []
-        for column, (first, second) in enumerate(travelling):
+        for column in range(column_count):
             piece = total[:, column * LANES:(column + 1) * LANES]
-            piece = piece + part(matrix, from_left[wide - 1], 0, first)
-            piece = piece + part(matrix, from_right[wide - 1], half, second)
+            for at, shift, pieces in waiting:
+                piece = piece + part(matrix, at, shift, pieces[column])
             results.append(piece.astype(jnp.bfloat16))
-        return results, extra
+        return results, later, extra
 
     swaps = [[(i, i ^ delta) for i in range(fronts)] for delta in range(fronts)]
 
@@ -135,12 +127,12 @@
         return (rows_in, picker, alive_rows), after
 
     cuts = range(0, width, LANES)
-    solved, (rows_in, picker, alive_rows) = ring_products(
-        held(inv_diag[0]), [rhs[0][:, c:c + LANES] for c in cuts], routing
+    solved, below_rows, (rows_in, picker, alive_rows) = gathered_product(
+        held(inv_diag[0]), [rhs[0][:, c:c + LANES] for c in cuts], held(below[0]), routing
     )
     numbers = jnp.arange(parent_height, dtype=jnp.int32)[:, None]
 
-    updates, _ = ring_products(held(below[0]), solved)
+    updates, _, _ = gathered_product(below_rows, solved)
     results = []
     for c, update in zip(cuts, updates):
         update = jnp.where(alive_rows, update, jnp.zeros_like(update))

time: 159 us -> 142 us (0.89)
  starting transfers between devices: 65 us -> 35.9 us
  waiting for transfers between devices: 23.8 us -> 45.7 us
  local copies, waits for them, and re-layouts: 22.6 us -> 11.4 us
  Pallas kernels: 2 us -> 10.4 us
  matrix products: 39.4 us -> 33.4 us
    ppermute x56 -> x28, starting transfers between devices: 60.5 us -> 30.7 us  [the longest x16 15.9 us: gathered_product(): lax.ppermute(b, 'wide', y_shifts[shift])]
    ppermute x56 -> x28, waiting for transfers between devices: 19.1 us -> 42.1 us  [the longest x16 32.2 us: gathered_product(): lax.ppermute(b, 'wide', y_shifts[shift])]
    unnamed x33 -> x19, local copies, waits for them, and re-layouts: 20.9 us -> 10.4 us
    pallas_call x2, Pallas kernels: 2 us -> 10.4 us  [held(): pl.pallas_call(kernel, out_shape=pltpu.VMEM(matrix.shape, matrix.dtype),...]
    dot_general x48 -> x32, matrix products: 39.4 us -> 33.4 us  [dot(): return row_major(jnp.dot(a, b, preferred_element_type=jnp.float32))]
  transfers between devices with their start and end apart: 65 -> 37, of which waited for: 23 -> 16; matrix products, arithmetic and copies ran while one was open for 24% -> 23% of each run, Pallas kernels for 1% -> 7%
where the time goes in v3:
time: 142 us
  waiting for transfers between devices  45.7 us (32%)
  starting transfers between devices  35.9 us (25%)
  matrix products  33.4 us (24%)
  local copies, waits for them, and re-layouts  11.4 us (8%)
  Pallas kernels  10.4 us (7%)
  other arithmetic  3.8 us (3%)
    dot_general x32, matrix products, dot(): return row_major(jnp.dot(a, b, preferred_element_type=jnp.float32))  33.4 us
    ppermute x16, waiting for transfers between devices, gathered_product(): lax.ppermute(b, 'wide', y_shifts[shift])  32.2 us
    ppermute x16, starting transfers between devices, gathered_product(): lax.ppermute(b, 'wide', y_shifts[shift])  15.9 us
    ppermute x12, starting transfers between devices, gathered_product(): lax.ppermute(b, 'wide', z_ring)  14.7 us
    pallas_call x2, Pallas kernels, held(): pl.pallas_call(kernel, out_shape=pltpu.VMEM(matrix.shape, matrix.dtype),...  10.4 us
    unnamed x19, local copies, waits for them, and re-layouts  10.4 us
    ppermute x12, waiting for transfers between devices, gathered_product(): lax.ppermute(b, 'wide', z_ring)  9.84 us
    ppermute x6, starting transfers between devices, body(): lax.ppermute(values_out[delta], 'front', swaps[delta])  3.7 us
  transfers between devices with their start and end apart: 37, of which 16 were waited for; matrix products, arithmetic and copies ran while one was open for 23% of the time, Pallas kernels for 7%

profile of v3, /device:TPU:0, one launch (start us, length us, event | category | flops | bytes accessed | tf_op | source)
XLA Modules:
  0.0 141.7 jit_solution(8164287330406094206)
XLA Ops:
  0.6 1.1 fusion.197
  1.7 3.1 %collective-permute-start.2 = (bf16[1024,128]{1,0:T(8,128)(2,1)S(1)}, bf16[1024,128]{1,0:T(8,128)(2,1)S(1)}, u32[]{:S(2)}, u32[]{:S(2)}) collective-permute-start(bf16[1024,128]{1,0:T(8,128)(2,1)S(1)} %get-tuple-element.57), channel_id=1, source_target_pairs={{0,2},{1,3},{2,4},{3,5},{4,6},{5,7},{6,0},{7,1},{8,10},{9,11},{10,... | collective-permute-start | bytes 786440 | tf_op jit(solution)/shard_map/ppermute | solution.py:81
  4.8 1.5 %collective-permute-start.4 = (bf16[1024,128]{1,0:T(8,128)(2,1)S(1)}, bf16[1024,128]{1,0:T(8,128)(2,1)S(1)}, u32[]{:S(2)}, u32[]{:S(2)}) collective-permute-start(bf16[1024,128]{1,0:T(8,128)(2,1)S(1)} %get-tuple-element.57), channel_id=1, source_target_pairs={{0,1},{1,0},{2,3},{3,2},{4,5},{5,4},{6,7},{7,6},{8,9},{9,8},{10,11... | collective-permute-start | bytes 786440 | tf_op jit(solution)/shard_map/ppermute | solution.py:83
  6.3 1.6 %collective-permute-start = (bf16[1024,128]{1,0:T(8,128)(2,1)S(1)}, bf16[1024,128]{1,0:T(8,128)(2,1)S(1)}, u32[]{:S(2)}, u32[]{:S(2)}) collective-permute-start(bf16[1024,128]{1,0:T(8,128)(2,1)S(1)} %get-tuple-element.56), channel_id=1, source_target_pairs={{0,2},{1,3},{2,4},{3,5},{4,6},{5,7},{6,0},{7,1},{8,10},{9,11},{10,... | collective-permute-start | bytes 786440 | tf_op jit(solution)/shard_map/ppermute | solution.py:81
  8.4 5.8 %shard_map.86 = bf16[1024,8192]{1,0:T(8,128)(2,1)S(1)} custom-call(bf16[1024,8192]{1,0:T(8,128)(2,1)} %bitcast.73), custom_call_target="tpu_custom_call" | custom-call | bytes 33554432 | tf_op jit(solution)/shard_map/pallas_call | solution.py:28
  14.2 5.8 %copy-done = bf16[1024,8192]{1,0:T(8,128)(2,1)} copy-done((bf16[1024,8192]{1,0:T(8,128)(2,1)}, bf16[1024,8192]{1,0:T(8,128)(2,1)S(1)}, u32[]{:S(2)}) %copy-start) | copy-done | bytes 16777240
  19.9 4.6 %shard_map.87 = bf16[768,8192]{1,0:T(8,128)(2,1)S(1)} custom-call(bf16[768,8192]{1,0:T(8,128)(2,1)} %bitcast.74), custom_call_target="tpu_custom_call" | custom-call | bytes 25165824 | tf_op jit(solution)/shard_map/pallas_call | solution.py:28
  24.6 4.5 %copy-done.2 = bf16[768,8192]{1,0:T(8,128)(2,1)} copy-done((bf16[768,8192]{1,0:T(8,128)(2,1)}, bf16[768,8192]{1,0:T(8,128)(2,1)S(1)}, u32[]{:S(2)}) %copy-start.2) | copy-done | bytes 12582936
  29.1 2.4 %fusion.12 = f32[1024,256]{1,0:T(8,128)S(1)} fusion(bf16[1024,8192]{1,0:T(8,128)(2,1)} %copy-done, s32[]{:T(128)S(6)} %select_n.153, bf16[1,1024,256]{2,1,0:T(8,128)(2,1)S(1)} %copy-done.3), kind=kOutput, calls=%fused_computation.13 | convolution fusion | flops 536870912 | bytes 3670020 | tf_op jit(solution)/shard_map/dot_general | solution.py:19
  31.6 1.6 %collective-permute-start.1 = (bf16[1024,128]{1,0:T(8,128)(2,1)S(1)}, bf16[1024,128]{1,0:T(8,128)(2,1)S(1)}, u32[]{:S(2)}, u32[]{:S(2)}) collective-permute-start(bf16[1024,128]{1,0:T(8,128)(2,1)S(1)} %collective-permute-done), channel_id=1, source_target_pairs={{0,2},{1,3},{2,4},{3,5},{4,6},{5,7},{6,0},{7,1},{8,10},{9,11},{10,... | collective-permute-start | bytes 786440 | tf_op jit(solution)/shard_map/ppermute | solution.py:81
  33.2 1.5 %collective-permute-start.7 = (bf16[1024,128]{1,0:T(8,128)(2,1)S(1)}, bf16[1024,128]{1,0:T(8,128)(2,1)S(1)}, u32[]{:S(2)}, u32[]{:S(2)}) collective-permute-start(bf16[1024,128]{1,0:T(8,128)(2,1)S(1)} %collective-permute-done), channel_id=1, source_target_pairs={{0,1},{1,0},{2,3},{3,2},{4,5},{5,4},{6,7},{7,6},{8,9},{9,8},{10,11... | collective-permute-start | bytes 786440 | tf_op jit(solution)/shard_map/ppermute | solution.py:83
  36.6 2.3 %fusion.10 = f32[1024,256]{1,0:T(8,128)S(1)} fusion(bf16[1024,8192]{1,0:T(8,128)(2,1)} %copy-done, s32[]{:T(128)S(6)} %select_n.155, bf16[1024,128]{1,0:T(8,128)(2,1)S(1)} %collective-permute-done.2, bf16[1024,128]{1,0:T(8,128)(2,1)S(1)} %collective-permute-done), kind=kOutput, calls=%fused_computation.11 | convolution fusion | flops 537919488 | bytes 3670020 | tf_op jit(solution)/shard_map/dot_general | solution.py:19
  39.3 0.8 collective-permute-start.6
  40.7 2.4 %add_add_fusion = f32[1024,256]{1,0:T(8,128)S(1)} fusion(f32[1024,256]{1,0:T(8,128)S(1)} %fusion.12, f32[1024,256]{1,0:T(8,128)S(1)} %fusion.10, bf16[1024,8192]{1,0:T(8,128)(2,1)} %copy-done, s32[]{:T(128)S(6)} %select_n.157, bf16[1024,128]{1,0:T(8,128)(2,1)S(1)} %collective-permute-done.4, bf16[1024,128]{1,0:T(8,128)(2,1)S(1)} %collective-permute-done.3), kind=kOutput, calls=%fused_computation.66 | convolution fusion | flops 538443776 | bytes 5767172 | tf_op jit(solution)/shard_map/dot_general | solution.py:19
  43.0 1.2 collective-permute-start.5
  44.3 4.2 %collective-permute-done.8 = bf16[1024,128]{1,0:T(8,128)(2,1)S(1)} collective-permute-done((bf16[1024,128]{1,0:T(8,128)(2,1)S(1)}, bf16[1024,128]{1,0:T(8,128)(2,1)S(1)}, u32[]{:S(2)}, u32[]{:S(2)}) %collective-permute-start.8) | collective-permute-done | bytes 262176 | tf_op jit(solution)/shard_map/ppermute | solution.py:83
  48.5 1.5 %collective-permute-start.10 = (s32[256]{0:T(256)S(1)}, s32[256]{0:T(256)S(1)}, u32[]{:S(2)}, u32[]{:S(2)}) collective-permute-start(s32[256]{0:T(256)S(1)} %get-tuple-element.59), channel_id=1, source_target_pairs={{0,16},{8,24},{16,0},{24,8},{1,17},{9,25},{17,1},{25,9},{2,18},{10... | collective-permute-start | bytes 3080 | tf_op jit(solution)/shard_map/ppermute | solution.py:119
  50.0 0.7 fusion.4
  50.7 0.8 collective-permute-start.13
  51.5 1.0 collective-permute-start.12
  52.6 2.9 %collective-permute-done.5 = bf16[1024,128]{1,0:T(8,128)(2,1)S(1)} collective-permute-done((bf16[1024,128]{1,0:T(8,128)(2,1)S(1)}, bf16[1024,128]{1,0:T(8,128)(2,1)S(1)}, u32[]{:S(2)}, u32[]{:S(2)}) %collective-permute-start.5) | collective-permute-done | bytes 262176 | tf_op jit(solution)/shard_map/ppermute | solution.py:81
  56.1 0.7 fusion.39
  56.9 1.4 collective-permute-start.15
  58.3 3.5 %collective-permute-done.12 = bf16[1024,128]{1,0:T(8,128)(2,1)S(1)} collective-permute-done((bf16[1024,128]{1,0:T(8,128)(2,1)S(1)}, bf16[1024,128]{1,0:T(8,128)(2,1)S(1)}, u32[]{:S(2)}, u32[]{:S(2)}) %collective-permute-start.12) | collective-permute-done | bytes 262176 | tf_op jit(solution)/shard_map/ppermute | solution.py:81
  61.8 1.4 %collective-permute-start.16 = (bf16[1024,128]{1,0:T(8,128)(2,1)S(1)}, bf16[1024,128]{1,0:T(8,128)(2,1)S(1)}, u32[]{:S(2)}, u32[]{:S(2)}) collective-permute-start(bf16[1024,128]{1,0:T(8,128)(2,1)S(1)} %collective-permute-done.12), channel_id=1, source_target_pairs={{0,1},{1,0},{2,3},{3,2},{4,5},{5,4},{6,7},{7,6},{8,9},{9,8},{10,11... | collective-permute-start | bytes 786440 | tf_op jit(solution)/shard_map/ppermute | solution.py:83
  63.2 2.4 %collective-permute-done.14 = bf16[1024,128]{1,0:T(8,128)(2,1)S(1)} collective-permute-done((bf16[1024,128]{1,0:T(8,128)(2,1)S(1)}, bf16[1024,128]{1,0:T(8,128)(2,1)S(1)}, u32[]{:S(2)}, u32[]{:S(2)}) %collective-permute-start.14) | collective-permute-done | bytes 262176 | tf_op jit(solution)/shard_map/ppermute | solution.py:83
  65.6 0.7 fusion
  66.3 0.7 fusion.45
  67.0 4.2 %collective-permute-done.15 = bf16[1024,128]{1,0:T(8,128)(2,1)S(1)} collective-permute-done((bf16[1024,128]{1,0:T(8,128)(2,1)S(1)}, bf16[1024,128]{1,0:T(8,128)(2,1)S(1)}, u32[]{:S(2)}, u32[]{:S(2)}) %collective-permute-start.15) | collective-permute-done | bytes 262176 | tf_op jit(solution)/shard_map/ppermute | solution.py:83
  71.2 0.7 fusion.79
  71.9 1.1 collective-permute-start.17
  73.0 3.4 %collective-permute-done.16 = bf16[1024,128]{1,0:T(8,128)(2,1)S(1)} collective-permute-done((bf16[1024,128]{1,0:T(8,128)(2,1)S(1)}, bf16[1024,128]{1,0:T(8,128)(2,1)S(1)}, u32[]{:S(2)}, u32[]{:S(2)}) %collective-permute-start.16) | collective-permute-done | bytes 262176 | tf_op jit(solution)/shard_map/ppermute | solution.py:83
  76.5 0.7 fusion.63
  77.2 1.1 collective-permute-start.19
  78.4 0.7 collective-permute-start.21
  79.1 1.4 collective-permute-start.20
  80.4 0.8 fusion.149
  81.3 2.0 %fusion.30 = f32[768,256]{1,0:T(8,128)S(1)} fusion(bf16[768,8192]{1,0:T(8,128)(2,1)} %copy-done.2, s32[]{:T(128)S(6)} %select_n.153, bf16[1024,128]{1,0:T(8,128)(2,1)S(1)} %fusion.63, bf16[1024,128]{1,0:T(8,128)(2,1)S(1)} %fusion.79), kind=kOutput, calls=%fused_computation.31 | convolution fusion | flops 403701760 | bytes 2883588 | tf_op jit(solution)/shard_map/dot_general | solution.py:19
  83.3 1.6 %collective-permute-start.18 = (bf16[1024,128]{1,0:T(8,128)(2,1)S(1)}, bf16[1024,128]{1,0:T(8,128)(2,1)S(1)}, u32[]{:S(2)}, u32[]{:S(2)}) collective-permute-start(bf16[1024,128]{1,0:T(8,128)(2,1)S(1)} %collective-permute-done.17), channel_id=1, source_target_pairs={{0,2},{1,3},{2,4},{3,5},{4,6},{5,7},{6,0},{7,1},{8,10},{9,11},{10,... | collective-permute-start | bytes 786440 | tf_op jit(solution)/shard_map/ppermute | solution.py:81
  85.6 1.8 %collective-permute-done.19 = bf16[1024,128]{1,0:T(8,128)(2,1)S(1)} collective-permute-done((bf16[1024,128]{1,0:T(8,128)(2,1)S(1)}, bf16[1024,128]{1,0:T(8,128)(2,1)S(1)}, u32[]{:S(2)}, u32[]{:S(2)}) %collective-permute-start.19) | collective-permute-done | bytes 262176 | tf_op jit(solution)/shard_map/ppermute | solution.py:81
  87.4 2.0 %fusion.28 = f32[768,256]{1,0:T(8,128)S(1)} fusion(bf16[768,8192]{1,0:T(8,128)(2,1)} %copy-done.2, s32[]{:T(128)S(6)} %select_n.155, bf16[1024,128]{1,0:T(8,128)(2,1)S(1)} %collective-permute-done.19, bf16[1024,128]{1,0:T(8,128)(2,1)S(1)} %collective-permute-done.17), kind=kOutput, calls=%fused_computation.29 | convolution fusion | flops 403701760 | bytes 2883588 | tf_op jit(solution)/shard_map/dot_general | solution.py:19
  89.4 1.2 collective-permute-start.25
  90.6 2.7 %collective-permute-done.20 = bf16[1024,128]{1,0:T(8,128)(2,1)S(1)} collective-permute-done((bf16[1024,128]{1,0:T(8,128)(2,1)S(1)}, bf16[1024,128]{1,0:T(8,128)(2,1)S(1)}, u32[]{:S(2)}, u32[]{:S(2)}) %collective-permute-start.20) | collective-permute-done | bytes 262176 | tf_op jit(solution)/shard_map/ppermute | solution.py:83
  93.3 2.0 %add_add_fusion.1 = f32[768,256]{1,0:T(8,128)S(1)} fusion(f32[768,256]{1,0:T(8,128)S(1)} %fusion.30, f32[768,256]{1,0:T(8,128)S(1)} %fusion.28, bf16[768,8192]{1,0:T(8,128)(2,1)} %copy-done.2, s32[]{:T(128)S(6)} %select_n.157, bf16[1024,128]{1,0:T(8,128)(2,1)S(1)} %collective-permute-done.21, bf16[1024,128]{1,0:T(8,128)(2,1)S(1)} %collective-permute-done.20), kind=kOutput, calls=%fused_computation.67 | convolution fusion | flops 404094976 | bytes 4456452 | tf_op jit(solution)/shard_map/dot_general | solution.py:19
  95.3 0.7 collective-permute-start.27
  96.1 1.6 %collective-permute-start.22 = (bf16[1024,128]{1,0:T(8,128)(2,1)S(1)}, bf16[1024,128]{1,0:T(8,128)(2,1)S(1)}, u32[]{:S(2)}, u32[]{:S(2)}) collective-permute-start(bf16[1024,128]{1,0:T(8,128)(2,1)S(1)} %collective-permute-done.18), channel_id=1, source_target_pairs={{0,2},{1,3},{2,4},{3,5},{4,6},{5,7},{6,0},{7,1},{8,10},{9,11},{10,... | collective-permute-start | bytes 786440 | tf_op jit(solution)/shard_map/ppermute | solution.py:81
  97.6 1.7 %collective-permute-done.23 = bf16[1024,128]{1,0:T(8,128)(2,1)S(1)} collective-permute-done((bf16[1024,128]{1,0:T(8,128)(2,1)S(1)}, bf16[1024,128]{1,0:T(8,128)(2,1)S(1)}, u32[]{:S(2)}, u32[]{:S(2)}) %collective-permute-start.23) | collective-permute-done | bytes 262176 | tf_op jit(solution)/shard_map/ppermute | solution.py:81
  99.3 5.2 %collective-permute-done.25 = bf16[1024,128]{1,0:T(8,128)(2,1)S(1)} collective-permute-done((bf16[1024,128]{1,0:T(8,128)(2,1)S(1)}, bf16[1024,128]{1,0:T(8,128)(2,1)S(1)}, u32[]{:S(2)}, u32[]{:S(2)}) %collective-permute-start.25) | collective-permute-done | bytes 262176 | tf_op jit(solution)/shard_map/ppermute | solution.py:83
  105.2 2.0 %fusion.22 = f32[768,256]{1,0:T(8,128)S(1)} fusion(bf16[768,8192]{1,0:T(8,128)(2,1)} %copy-done.2, s32[]{:T(128)S(6)} %select_n.160, bf16[1024,128]{1,0:T(8,128)(2,1)S(1)} %collective-permute-done.25, bf16[1024,128]{1,0:T(8,128)(2,1)S(1)} %collective-permute-done.24), kind=kOutput, calls=%fused_computation.23 | convolution fusion | flops 403701760 | bytes 2883588 | tf_op jit(solution)/shard_map/dot_general | solution.py:19
  107.2 2.0 %fusion.51 = f32[768,256]{1,0:T(8,128)S(1)} fusion(f32[768,256]{1,0:T(8,128)S(1)} %fusion.22, f32[768,256]{1,0:T(8,128)S(1)} %add_add_fusion.1, bf16[768,8192]{1,0:T(8,128)(2,1)} %copy-done.2, s32[]{:T(128)S(6)} %select_n.159, bf16[1024,128]{1,0:T(8,128)(2,1)S(1)} %collective-permute-done.23, bf16[1024,128]{1,0:T(8,128)(2,1)S(1)} %collective-permute-done.18), kind=kOutput, calls=%fused_computation.42 | convolution fusion | flops 404094976 | bytes 4456452 | tf_op jit(solution)/shard_map/dot_general | solution.py:19
  109.2 1.4 collective-permute-start.29
  111.3 4.4 %collective-permute-done.28 = bf16[1024,128]{1,0:T(8,128)(2,1)S(1)} collective-permute-done((bf16[1024,128]{1,0:T(8,128)(2,1)S(1)}, bf16[1024,128]{1,0:T(8,128)(2,1)S(1)}, u32[]{:S(2)}, u32[]{:S(2)}) %collective-permute-start.28) | collective-permute-done | bytes 262176 | tf_op jit(solution)/shard_map/ppermute | solution.py:83
  115.8 2.0 %fusion.18 = f32[768,256]{1,0:T(8,128)S(1)} fusion(bf16[768,8192]{1,0:T(8,128)(2,1)} %copy-done.2, s32[]{:T(128)S(6)} %select_n.166, bf16[1024,128]{1,0:T(8,128)(2,1)S(1)} %collective-permute-done.28, bf16[1024,128]{1,0:T(8,128)(2,1)S(1)} %collective-permute-done.27), kind=kOutput, calls=%fused_computation.19 | convolution fusion | flops 403701760 | bytes 2883588 | tf_op jit(solution)/shard_map/dot_general | solution.py:19
  117.8 2.0 %fusion.57 = f32[768,256]{1,0:T(8,128)S(1)} fusion(f32[768,256]{1,0:T(8,128)S(1)} %fusion.18, f32[768,256]{1,0:T(8,128)S(1)} %fusion.51, bf16[768,8192]{1,0:T(8,128)(2,1)} %copy-done.2, s32[]{:T(128)S(6)} %select_n.162, bf16[1024,128]{1,0:T(8,128)(2,1)S(1)} %collective-permute-done.26, bf16[1024,128]{1,0:T(8,128)(2,1)S(1)} %collective-permute-done.22), kind=kOutput, calls=%fused_computation.44 | convolution fusion | flops 404094976 | bytes 4456452 | tf_op jit(solution)/shard_map/dot_general | solution.py:19
  119.8 5.7 %collective-permute-done.33 = bf16[1024,128]{1,0:T(8,128)(2,1)S(1)} collective-permute-done((bf16[1024,128]{1,0:T(8,128)(2,1)S(1)}, bf16[1024,128]{1,0:T(8,128)(2,1)S(1)}, u32[]{:S(2)}, u32[]{:S(2)}) %collective-permute-start.33) | collective-permute-done | bytes 262176 | tf_op jit(solution)/shard_map/ppermute | solution.py:83
  125.5 2.0 %fusion.76 = bf16[768,128]{1,0:T(8,128)(2,1)S(1)} fusion(bf16[1024,128]{1,0:T(8,128)(2,1)S(1)} %collective-permute-done.33, bf16[768,8192]{1,0:T(8,128)(2,1)} %copy-done.2, s32[]{:T(128)S(6)} %select_n.167, f32[768,256]{1,0:T(8,128)S(1)} %fusion.57, pred[768]{0:T(1024)(128)(4,1)S(1)} %reduce), kind=kOutput, calls=%fused_computation.57 | convolution fusion | flops 201621504 | bytes 2425604 | tf_op jit(solution)/shard_map/dot_general | solution.py:19
  128.2 2.0 %fusion.158 = bf16[768,128]{1,0:T(8,128)(2,1)S(1)} fusion(f32[768,256]{1,0:T(8,128)S(1)} %fusion.57, pred[768]{0:T(1024)(128)(4,1)S(1)} %reduce, bf16[1024,128]{1,0:T(8,128)(2,1)S(1)} %collective-permute-done.29, bf16[768,8192]{1,0:T(8,128)(2,1)} %copy-done.2, s32[]{:T(128)S(6)} %select_n.167), kind=kOutput, calls=%fused_computation.143 | convolution fusion | flops 201621504 | bytes 2425604 | tf_op jit(solution)/shard_map/dot_general | solution.py:19
  132.6 1.1 collective-permute-start.35
  134.2 1.0 collective-permute-start.32
  135.2 0.7 collective-permute-start.31
  136.6 1.0 collective-permute-done.35
  138.1 1.2 collective-permute-done.32
  139.5 0.9 collective-permute-done.31
  140.9 0.8 maximum_bitcast_fusion
  (79 shorter events, 11.6 us)
Async XLA Ops:
  1.7 34.8 %collective-permute-start.2 = (bf16[1024,128]{1,0:T(8,128)(2,1)S(1)}, bf16[1024,128]{1,0:T(8,128)(2,1)S(1)}, u32[]{:S(2)}, u32[]{:S(2)}) collective-permute-start(bf16[1024,128]{1,0:T(8,128)(2,1)S(1)} %get-tuple-element.57), channel_id=1, source_target_pairs={{0,2},{1,3},{2,4},{3,5},{4,6},{5,7},{6,0},{7,1},{8,10},{9,11},{10,... | collective-permute-start | bytes 786440 | tf_op jit(solution)/shard_map/ppermute | solution.py:81
  4.8 34.5 %collective-permute-start.4 = (bf16[1024,128]{1,0:T(8,128)(2,1)S(1)}, bf16[1024,128]{1,0:T(8,128)(2,1)S(1)}, u32[]{:S(2)}, u32[]{:S(2)}) collective-permute-start(bf16[1024,128]{1,0:T(8,128)(2,1)S(1)} %get-tuple-element.57), channel_id=1, source_target_pairs={{0,1},{1,0},{2,3},{3,2},{4,5},{5,4},{6,7},{7,6},{8,9},{9,8},{10,11... | collective-permute-start | bytes 786440 | tf_op jit(solution)/shard_map/ppermute | solution.py:83
  6.3 25.3 %collective-permute-start = (bf16[1024,128]{1,0:T(8,128)(2,1)S(1)}, bf16[1024,128]{1,0:T(8,128)(2,1)S(1)}, u32[]{:S(2)}, u32[]{:S(2)}) collective-permute-start(bf16[1024,128]{1,0:T(8,128)(2,1)S(1)} %get-tuple-element.56), channel_id=1, source_target_pairs={{0,2},{1,3},{2,4},{3,5},{4,6},{5,7},{6,0},{7,1},{8,10},{9,11},{10,... | collective-permute-start | bytes 786440 | tf_op jit(solution)/shard_map/ppermute | solution.py:81
  7.9 32.2 %collective-permute-start.3 = (bf16[1024,128]{1,0:T(8,128)(2,1)S(1)}, bf16[1024,128]{1,0:T(8,128)(2,1)S(1)}, u32[]{:S(2)}, u32[]{:S(2)}) collective-permute-start(bf16[1024,128]{1,0:T(8,128)(2,1)S(1)} %get-tuple-element.56), channel_id=1, source_target_pairs={{0,1},{1,0},{2,3},{3,2},{4,5},{5,4},{6,7},{7,6},{8,9},{9,8},{10,11... | collective-permute-start | bytes 786440 | tf_op jit(solution)/shard_map/ppermute | solution.py:83
  14.2 5.8 %copy-start = (bf16[1024,8192]{1,0:T(8,128)(2,1)}, bf16[1024,8192]{1,0:T(8,128)(2,1)S(1)}, u32[]{:S(2)}) copy-start(bf16[1024,8192]{1,0:T(8,128)(2,1)S(1)} %shard_map.86) | copy-start | bytes 50331652
  19.9 9.2 %copy-start.3 = (bf16[1,1024,256]{2,1,0:T(8,128)(2,1)S(1)}, bf16[1,1024,256]{2,1,0:T(8,128)(2,1)}, u32[]{:S(2)}) copy-start(bf16[1,1024,256]{2,1,0:T(8,128)(2,1)} %param.9) | copy-start | bytes 1572868
  19.9 14.8 %copy-start.7 = (s32[4]{0:T(128)S(1)}, s32[4]{0:T(128)}, u32[]{:S(2)}) copy-start(s32[4]{0:T(128)} %param.10) | copy-start | bytes 52
  19.9 16.1 %copy-start.4 = (s32[1,6,128]{2,0,1:T(1,128)S(1)}, s32[1,6,128]{2,0,1:T(1,128)}, u32[]{:S(2)}) copy-start(s32[1,6,128]{2,0,1:T(1,128)} %param.12) | copy-start | bytes 9220
  19.9 16.2 %copy-start.5 = (s32[1,6,1]{1,2,0:T(1,128)S(1)}, s32[1,6,1]{1,2,0:T(1,128)}, u32[]{:S(2)}) copy-start(s32[1,6,1]{1,2,0:T(1,128)} %param.11) | copy-start | bytes 76
  24.6 4.5 %copy-start.2 = (bf16[768,8192]{1,0:T(8,128)(2,1)}, bf16[768,8192]{1,0:T(8,128)(2,1)S(1)}, u32[]{:S(2)}) copy-start(bf16[768,8192]{1,0:T(8,128)(2,1)S(1)} %shard_map.87) | copy-start | bytes 37748740
  29.1 20.9 %copy-start.1 = (bf16[1024,8192]{1,0:T(8,128)(2,1)S(1)}, bf16[1024,8192]{1,0:T(8,128)(2,1)}, u32[]{:S(2)}) copy-start(bf16[1024,8192]{1,0:T(8,128)(2,1)} %copy-done) | copy-start | bytes 50331652
  31.6 11.5 %collective-permute-start.1 = (bf16[1024,128]{1,0:T(8,128)(2,1)S(1)}, bf16[1024,128]{1,0:T(8,128)(2,1)S(1)}, u32[]{:S(2)}, u32[]{:S(2)}) collective-permute-start(bf16[1024,128]{1,0:T(8,128)(2,1)S(1)} %collective-permute-done), channel_id=1, source_target_pairs={{0,2},{1,3},{2,4},{3,5},{4,6},{5,7},{6,0},{7,1},{8,10},{9,11},{10,... | collective-permute-start | bytes 786440 | tf_op jit(solution)/shard_map/ppermute | solution.py:81
  33.2 16.8 %collective-permute-start.7 = (bf16[1024,128]{1,0:T(8,128)(2,1)S(1)}, bf16[1024,128]{1,0:T(8,128)(2,1)S(1)}, u32[]{:S(2)}, u32[]{:S(2)}) collective-permute-start(bf16[1024,128]{1,0:T(8,128)(2,1)S(1)} %collective-permute-done), channel_id=1, source_target_pairs={{0,1},{1,0},{2,3},{3,2},{4,5},{5,4},{6,7},{7,6},{8,9},{9,8},{10,11... | collective-permute-start | bytes 786440 | tf_op jit(solution)/shard_map/ppermute | solution.py:83
  36.5 14.2 %collective-permute-start.9 = (s32[256]{0:T(256)S(1)}, s32[256]{0:T(256)S(1)}, u32[]{:S(2)}, u32[]{:S(2)}) collective-permute-start(s32[256]{0:T(256)S(1)} %get-tuple-element.60), channel_id=1, source_target_pairs={{0,8},{8,0},{16,24},{24,16},{1,9},{9,1},{17,25},{25,17},{2,10},{10... | collective-permute-start | bytes 3080 | tf_op jit(solution)/shard_map/ppermute | solution.py:119
  39.3 12.3 %collective-permute-start.6 = (bf16[1024,128]{1,0:T(8,128)(2,1)S(1)}, bf16[1024,128]{1,0:T(8,128)(2,1)S(1)}, u32[]{:S(2)}, u32[]{:S(2)}) collective-permute-start(bf16[1024,128]{1,0:T(8,128)(2,1)S(1)} %collective-permute-done.2), channel_id=1, source_target_pairs={{0,2},{1,3},{2,4},{3,5},{4,6},{5,7},{6,0},{7,1},{8,10},{9,11},{10,... | collective-permute-start | bytes 786440 | tf_op jit(solution)/shard_map/ppermute | solution.py:81
  40.1 8.4 %collective-permute-start.8 = (bf16[1024,128]{1,0:T(8,128)(2,1)S(1)}, bf16[1024,128]{1,0:T(8,128)(2,1)S(1)}, u32[]{:S(2)}, u32[]{:S(2)}) collective-permute-start(bf16[1024,128]{1,0:T(8,128)(2,1)S(1)} %collective-permute-done.2), channel_id=1, source_target_pairs={{0,1},{1,0},{2,3},{3,2},{4,5},{5,4},{6,7},{7,6},{8,9},{9,8},{10,11... | collective-permute-start | bytes 786440 | tf_op jit(solution)/shard_map/ppermute | solution.py:83
  43.0 12.4 %collective-permute-start.5 = (bf16[1024,128]{1,0:T(8,128)(2,1)S(1)}, bf16[1024,128]{1,0:T(8,128)(2,1)S(1)}, u32[]{:S(2)}, u32[]{:S(2)}) collective-permute-start(bf16[1024,128]{1,0:T(8,128)(2,1)S(1)} %collective-permute-done.1), channel_id=1, source_target_pairs={{0,2},{1,3},{2,4},{3,5},{4,6},{5,7},{6,0},{7,1},{8,10},{9,11},{10,... | collective-permute-start | bytes 786440 | tf_op jit(solution)/shard_map/ppermute | solution.py:81
  48.5 8.4 %collective-permute-start.10 = (s32[256]{0:T(256)S(1)}, s32[256]{0:T(256)S(1)}, u32[]{:S(2)}, u32[]{:S(2)}) collective-permute-start(s32[256]{0:T(256)S(1)} %get-tuple-element.59), channel_id=1, source_target_pairs={{0,16},{8,24},{16,0},{24,8},{1,17},{9,25},{17,1},{25,9},{2,18},{10... | collective-permute-start | bytes 3080 | tf_op jit(solution)/shard_map/ppermute | solution.py:119
  50.0 6.9 %collective-permute-start.11 = (s32[256]{0:T(256)S(1)}, s32[256]{0:T(256)S(1)}, u32[]{:S(2)}, u32[]{:S(2)}) collective-permute-start(s32[256]{0:T(256)S(1)} %get-tuple-element.58), channel_id=1, source_target_pairs={{0,24},{8,16},{16,8},{24,0},{1,25},{9,17},{17,9},{25,1},{2,26},{10... | collective-permute-start | bytes 3080 | tf_op jit(solution)/shard_map/ppermute | solution.py:119
  50.7 14.9 %collective-permute-start.13 = (bf16[1024,128]{1,0:T(8,128)(2,1)S(1)}, bf16[1024,128]{1,0:T(8,128)(2,1)S(1)}, u32[]{:S(2)}, u32[]{:S(2)}) collective-permute-start(bf16[1024,128]{1,0:T(8,128)(2,1)S(1)} %collective-permute-done.1), channel_id=1, source_target_pairs={{0,1},{1,0},{2,3},{3,2},{4,5},{5,4},{6,7},{7,6},{8,9},{9,8},{10,11... | collective-permute-start | bytes 786440 | tf_op jit(solution)/shard_map/ppermute | solution.py:83
  51.5 10.2 %collective-permute-start.12 = (bf16[1024,128]{1,0:T(8,128)(2,1)S(1)}, bf16[1024,128]{1,0:T(8,128)(2,1)S(1)}, u32[]{:S(2)}, u32[]{:S(2)}) collective-permute-start(bf16[1024,128]{1,0:T(8,128)(2,1)S(1)} %collective-permute-done.6), channel_id=1, source_target_pairs={{0,2},{1,3},{2,4},{3,5},{4,6},{5,7},{6,0},{7,1},{8,10},{9,11},{10,... | collective-permute-start | bytes 786440 | tf_op jit(solution)/shard_map/ppermute | solution.py:81
  55.4 10.2 %collective-permute-start.14 = (bf16[1024,128]{1,0:T(8,128)(2,1)S(1)}, bf16[1024,128]{1,0:T(8,128)(2,1)S(1)}, u32[]{:S(2)}, u32[]{:S(2)}) collective-permute-start(bf16[1024,128]{1,0:T(8,128)(2,1)S(1)} %collective-permute-done.6), channel_id=1, source_target_pairs={{0,1},{1,0},{2,3},{3,2},{4,5},{5,4},{6,7},{7,6},{8,9},{9,8},{10,11... | collective-permute-start | bytes 786440 | tf_op jit(solution)/shard_map/ppermute | solution.py:83
  56.9 14.3 %collective-permute-start.15 = (bf16[1024,128]{1,0:T(8,128)(2,1)S(1)}, bf16[1024,128]{1,0:T(8,128)(2,1)S(1)}, u32[]{:S(2)}, u32[]{:S(2)}) collective-permute-start(bf16[1024,128]{1,0:T(8,128)(2,1)S(1)} %collective-permute-done.5), channel_id=1, source_target_pairs={{0,1},{1,0},{2,3},{3,2},{4,5},{5,4},{6,7},{7,6},{8,9},{9,8},{10,11... | collective-permute-start | bytes 786440 | tf_op jit(solution)/shard_map/ppermute | solution.py:83
  61.8 14.7 %collective-permute-start.16 = (bf16[1024,128]{1,0:T(8,128)(2,1)S(1)}, bf16[1024,128]{1,0:T(8,128)(2,1)S(1)}, u32[]{:S(2)}, u32[]{:S(2)}) collective-permute-start(bf16[1024,128]{1,0:T(8,128)(2,1)S(1)} %collective-permute-done.12), channel_id=1, source_target_pairs={{0,1},{1,0},{2,3},{3,2},{4,5},{5,4},{6,7},{7,6},{8,9},{9,8},{10,11... | collective-permute-start | bytes 786440 | tf_op jit(solution)/shard_map/ppermute | solution.py:83
  71.9 11.4 %collective-permute-start.17 = (bf16[1024,128]{1,0:T(8,128)(2,1)S(1)}, bf16[1024,128]{1,0:T(8,128)(2,1)S(1)}, u32[]{:S(2)}, u32[]{:S(2)}) collective-permute-start(bf16[1024,128]{1,0:T(8,128)(2,1)S(1)} %fusion.79), channel_id=1, source_target_pairs={{0,2},{1,3},{2,4},{3,5},{4,6},{5,7},{6,0},{7,1},{8,10},{9,11},{10,... | collective-permute-start | bytes 786440 | tf_op jit(solution)/shard_map/ppermute | solution.py:81
  77.2 10.2 %collective-permute-start.19 = (bf16[1024,128]{1,0:T(8,128)(2,1)S(1)}, bf16[1024,128]{1,0:T(8,128)(2,1)S(1)}, u32[]{:S(2)}, u32[]{:S(2)}) collective-permute-start(bf16[1024,128]{1,0:T(8,128)(2,1)S(1)} %fusion.63), channel_id=1, source_target_pairs={{0,2},{1,3},{2,4},{3,5},{4,6},{5,7},{6,0},{7,1},{8,10},{9,11},{10,... | collective-permute-start | bytes 786440 | tf_op jit(solution)/shard_map/ppermute | solution.py:81
  78.4 11.0 %collective-permute-start.21 = (bf16[1024,128]{1,0:T(8,128)(2,1)S(1)}, bf16[1024,128]{1,0:T(8,128)(2,1)S(1)}, u32[]{:S(2)}, u32[]{:S(2)}) collective-permute-start(bf16[1024,128]{1,0:T(8,128)(2,1)S(1)} %fusion.63), channel_id=1, source_target_pairs={{0,1},{1,0},{2,3},{3,2},{4,5},{5,4},{6,7},{7,6},{8,9},{9,8},{10,11... | collective-permute-start | bytes 786440 | tf_op jit(solution)/shard_map/ppermute | solution.py:83
  79.1 14.2 %collective-permute-start.20 = (bf16[1024,128]{1,0:T(8,128)(2,1)S(1)}, bf16[1024,128]{1,0:T(8,128)(2,1)S(1)}, u32[]{:S(2)}, u32[]{:S(2)}) collective-permute-start(bf16[1024,128]{1,0:T(8,128)(2,1)S(1)} %fusion.79), channel_id=1, source_target_pairs={{0,1},{1,0},{2,3},{3,2},{4,5},{5,4},{6,7},{7,6},{8,9},{9,8},{10,11... | collective-permute-start | bytes 786440 | tf_op jit(solution)/shard_map/ppermute | solution.py:83
  83.3 12.0 %collective-permute-start.18 = (bf16[1024,128]{1,0:T(8,128)(2,1)S(1)}, bf16[1024,128]{1,0:T(8,128)(2,1)S(1)}, u32[]{:S(2)}, u32[]{:S(2)}) collective-permute-start(bf16[1024,128]{1,0:T(8,128)(2,1)S(1)} %collective-permute-done.17), channel_id=1, source_target_pairs={{0,2},{1,3},{2,4},{3,5},{4,6},{5,7},{6,0},{7,1},{8,10},{9,11},{10,... | collective-permute-start | bytes 786440 | tf_op jit(solution)/shard_map/ppermute | solution.py:81
  84.9 20.3 %collective-permute-start.24 = (bf16[1024,128]{1,0:T(8,128)(2,1)S(1)}, bf16[1024,128]{1,0:T(8,128)(2,1)S(1)}, u32[]{:S(2)}, u32[]{:S(2)}) collective-permute-start(bf16[1024,128]{1,0:T(8,128)(2,1)S(1)} %collective-permute-done.17), channel_id=1, source_target_pairs={{0,1},{1,0},{2,3},{3,2},{4,5},{5,4},{6,7},{7,6},{8,9},{9,8},{10,11... | collective-permute-start | bytes 786440 | tf_op jit(solution)/shard_map/ppermute | solution.py:83
  87.4 11.9 %collective-permute-start.23 = (bf16[1024,128]{1,0:T(8,128)(2,1)S(1)}, bf16[1024,128]{1,0:T(8,128)(2,1)S(1)}, u32[]{:S(2)}, u32[]{:S(2)}) collective-permute-start(bf16[1024,128]{1,0:T(8,128)(2,1)S(1)} %collective-permute-done.19), channel_id=1, source_target_pairs={{0,2},{1,3},{2,4},{3,5},{4,6},{5,7},{6,0},{7,1},{8,10},{9,11},{10,... | collective-permute-start | bytes 786440 | tf_op jit(solution)/shard_map/ppermute | solution.py:81
  89.4 15.1 %collective-permute-start.25 = (bf16[1024,128]{1,0:T(8,128)(2,1)S(1)}, bf16[1024,128]{1,0:T(8,128)(2,1)S(1)}, u32[]{:S(2)}, u32[]{:S(2)}) collective-permute-start(bf16[1024,128]{1,0:T(8,128)(2,1)S(1)} %collective-permute-done.19), channel_id=1, source_target_pairs={{0,1},{1,0},{2,3},{3,2},{4,5},{5,4},{6,7},{7,6},{8,9},{9,8},{10,11... | collective-permute-start | bytes 786440 | tf_op jit(solution)/shard_map/ppermute | solution.py:83
  95.3 20.4 %collective-permute-start.27 = (bf16[1024,128]{1,0:T(8,128)(2,1)S(1)}, bf16[1024,128]{1,0:T(8,128)(2,1)S(1)}, u32[]{:S(2)}, u32[]{:S(2)}) collective-permute-start(bf16[1024,128]{1,0:T(8,128)(2,1)S(1)} %collective-permute-done.18), channel_id=1, source_target_pairs={{0,1},{1,0},{2,3},{3,2},{4,5},{5,4},{6,7},{7,6},{8,9},{9,8},{10,11... | collective-permute-start | bytes 786440 | tf_op jit(solution)/shard_map/ppermute | solution.py:83
  96.1 13.1 %collective-permute-start.22 = (bf16[1024,128]{1,0:T(8,128)(2,1)S(1)}, bf16[1024,128]{1,0:T(8,128)(2,1)S(1)}, u32[]{:S(2)}, u32[]{:S(2)}) collective-permute-start(bf16[1024,128]{1,0:T(8,128)(2,1)S(1)} %collective-permute-done.18), channel_id=1, source_target_pairs={{0,2},{1,3},{2,4},{3,5},{4,6},{5,7},{6,0},{7,1},{8,10},{9,11},{10,... | collective-permute-start | bytes 786440 | tf_op jit(solution)/shard_map/ppermute | solution.py:81
  99.3 11.3 %collective-permute-start.26 = (bf16[1024,128]{1,0:T(8,128)(2,1)S(1)}, bf16[1024,128]{1,0:T(8,128)(2,1)S(1)}, u32[]{:S(2)}, u32[]{:S(2)}) collective-permute-start(bf16[1024,128]{1,0:T(8,128)(2,1)S(1)} %collective-permute-done.23), channel_id=1, source_target_pairs={{0,2},{1,3},{2,4},{3,5},{4,6},{5,7},{6,0},{7,1},{8,10},{9,11},{10,... | collective-permute-start | bytes 786440 | tf_op jit(solution)/shard_map/ppermute | solution.py:81
  104.5 11.2 %collective-permute-start.28 = (bf16[1024,128]{1,0:T(8,128)(2,1)S(1)}, bf16[1024,128]{1,0:T(8,128)(2,1)S(1)}, u32[]{:S(2)}, u32[]{:S(2)}) collective-permute-start(bf16[1024,128]{1,0:T(8,128)(2,1)S(1)} %collective-permute-done.23), channel_id=1, source_target_pairs={{0,1},{1,0},{2,3},{3,2},{4,5},{5,4},{6,7},{7,6},{8,9},{9,8},{10,11... | collective-permute-start | bytes 786440 | tf_op jit(solution)/shard_map/ppermute | solution.py:83
  109.2 19.0 %collective-permute-start.29 = (bf16[1024,128]{1,0:T(8,128)(2,1)S(1)}, bf16[1024,128]{1,0:T(8,128)(2,1)S(1)}, u32[]{:S(2)}, u32[]{:S(2)}) collective-permute-start(bf16[1024,128]{1,0:T(8,128)(2,1)S(1)} %collective-permute-done.22), channel_id=1, source_target_pairs={{0,1},{1,0},{2,3},{3,2},{4,5},{5,4},{6,7},{7,6},{8,9},{9,8},{10,11... | collective-permute-start | bytes 786440 | tf_op jit(solution)/shard_map/ppermute | solution.py:83
  110.6 14.8 %collective-permute-start.33 = (bf16[1024,128]{1,0:T(8,128)(2,1)S(1)}, bf16[1024,128]{1,0:T(8,128)(2,1)S(1)}, u32[]{:S(2)}, u32[]{:S(2)}) collective-permute-start(bf16[1024,128]{1,0:T(8,128)(2,1)S(1)} %collective-permute-done.26), channel_id=1, source_target_pairs={{0,1},{1,0},{2,3},{3,2},{4,5},{5,4},{6,7},{7,6},{8,9},{9,8},{10,11... | collective-permute-start | bytes 786440 | tf_op jit(solution)/shard_map/ppermute | solution.py:83
  128.2 2.6 %copy-start.6 = (bf16[1,512,256]{2,1,0:T(8,128)(2,1)S(1)}, bf16[1,512,256]{2,1,0:T(8,128)(2,1)}, u32[]{:S(2)}) copy-start(bf16[1,512,256]{2,1,0:T(8,128)(2,1)} %param.13) | copy-start | bytes 786436
  131.9 4.5 %collective-permute-start.36 = (bf16[256,128]{1,0:T(8,128)(2,1)S(1)}, bf16[256,128]{1,0:T(8,128)(2,1)S(1)}, u32[]{:S(2)}, u32[]{:S(2)}) collective-permute-start(bf16[256,128]{1,0:T(8,128)(2,1)S(1)} %convolution_convert_fusion), channel_id=1, source_target_pairs={{0,24},{8,16},{16,8},{24,0},{1,25},{9,17},{17,9},{25,1},{2,26},{10... | collective-permute-start | bytes 196616 | tf_op jit(solution)/shard_map/ppermute | solution.py:141
  132.6 5.0 %collective-permute-start.35 = (bf16[256,128]{1,0:T(8,128)(2,1)S(1)}, bf16[256,128]{1,0:T(8,128)(2,1)S(1)}, u32[]{:S(2)}, u32[]{:S(2)}) collective-permute-start(bf16[256,128]{1,0:T(8,128)(2,1)S(1)} %convolution_convert_fusion.1), channel_id=1, source_target_pairs={{0,16},{8,24},{16,0},{24,8},{1,17},{9,25},{17,1},{25,9},{2,18},{10... | collective-permute-start | bytes 196616 | tf_op jit(solution)/shard_map/ppermute | solution.py:141
  133.7 4.1 %collective-permute-start.34 = (bf16[256,128]{1,0:T(8,128)(2,1)S(1)}, bf16[256,128]{1,0:T(8,128)(2,1)S(1)}, u32[]{:S(2)}, u32[]{:S(2)}) collective-permute-start(bf16[256,128]{1,0:T(8,128)(2,1)S(1)} %convolution_convert_fusion.2), channel_id=1, source_target_pairs={{0,8},{8,0},{16,24},{24,16},{1,9},{9,1},{17,25},{25,17},{2,10},{10... | collective-permute-start | bytes 196616 | tf_op jit(solution)/shard_map/ppermute | solution.py:141
  134.2 5.1 %collective-permute-start.32 = (bf16[256,128]{1,0:T(8,128)(2,1)S(1)}, bf16[256,128]{1,0:T(8,128)(2,1)S(1)}, u32[]{:S(2)}, u32[]{:S(2)}) collective-permute-start(bf16[256,128]{1,0:T(8,128)(2,1)S(1)} %convolution_convert_fusion.4), channel_id=1, source_target_pairs={{0,24},{8,16},{16,8},{24,0},{1,25},{9,17},{17,9},{25,1},{2,26},{10... | collective-permute-start | bytes 196616 | tf_op jit(solution)/shard_map/ppermute | solution.py:141
  135.2 5.2 %collective-permute-start.31 = (bf16[256,128]{1,0:T(8,128)(2,1)S(1)}, bf16[256,128]{1,0:T(8,128)(2,1)S(1)}, u32[]{:S(2)}, u32[]{:S(2)}) collective-permute-start(bf16[256,128]{1,0:T(8,128)(2,1)S(1)} %convolution_convert_fusion.5), channel_id=1, source_target_pairs={{0,16},{8,24},{16,0},{24,8},{1,17},{9,25},{17,1},{25,9},{2,18},{10... | collective-permute-start | bytes 196616 | tf_op jit(solution)/shard_map/ppermute | solution.py:141
  136.4 4.3 %collective-permute-start.30 = (bf16[256,128]{1,0:T(8,128)(2,1)S(1)}, bf16[256,128]{1,0:T(8,128)(2,1)S(1)}, u32[]{:S(2)}, u32[]{:S(2)}) collective-permute-start(bf16[256,128]{1,0:T(8,128)(2,1)S(1)} %convolution_convert_fusion.6), channel_id=1, source_target_pairs={{0,8},{8,0},{16,24},{24,16},{1,9},{9,1},{17,25},{25,17},{2,10},{10... | collective-permute-start | bytes 196616 | tf_op jit(solution)/shard_map/ppermute | solution.py:141

commit v4 on v0

v4 whole, which is shorter than its diff:
```python
import jax
import jax.numpy as jnp
from jax import lax
from jax.experimental.layout import Layout, with_layout_constraint
from jax.sharding import PartitionSpec as P

CAPACITY = 2
DEPTH = 4


def row_major(array):
    return with_layout_constraint(array, Layout(major_to_minor=tuple(range(array.ndim))))


def dot(a, b):
    return row_major(jnp.dot(a, b, preferred_element_type=jnp.float32))


def body(inv_diag, below, rhs, tile_count, tile_owner, tile_rows, parent_rhs):
    rows = rhs.shape[1]
    tiles = tile_owner.shape[1]
    height = tile_rows.shape[2]
    parent_height = parent_rhs.shape[1]
    fronts = lax.axis_size("front")
    wide = lax.axis_size("wide")
    me = lax.axis_index("front")
    wide_index = lax.axis_index("wide")
    depth = DEPTH if wide % DEPTH == 0 else 1
    across = wide // depth
    y = wide_index % across
    z_groups = [[i * across + j for i in range(depth)] for j in range(across)]
    y_shifts = [
        [(i, i // across * across + (i + shift) % across) for i in range(wide)]
        for shift in range(across)
    ]
    quarter = rows // 4
    share = (rows - quarter) // 2

    def along_z(values):
        return lax.all_gather(values, "wide", axis=0, tiled=True, axis_index_groups=z_groups)

    def along_y(values):
        return [lax.ppermute(values, "wide", y_shifts[shift]) for shift in range(1, across)]

    def columns_of(matrix, shifts, offset, length):
        return jnp.concatenate(
            [
                lax.dynamic_slice_in_dim(
                    matrix,
                    (i * across + (y + across - shift) % across) * rows + offset,
                    length,
                    1,
                )
                for i in range(depth)
                for shift in shifts
            ],
            axis=1,
        )

    def assembled(matrix):
        result = []
        for part in range(2):
            for shift in range(across):
                result.append(columns_of(matrix, [shift], part * share, share))
        result.append(columns_of(matrix, range(across), 2 * share, quarter))
        return result

    def gathered_product(matrices, block, later=None, aside=None):
        extra = None
        corner = block[2 * share:]
        corners = [corner] + along_y(corner)
        first_part, second_part = block[:share], block[share:2 * share]
        first = along_z(first_part)
        second_part, corners = lax.optimization_barrier((second_part, corners))
        second = along_z(second_part)
        first, matrices, corners = lax.optimization_barrier((first, matrices, corners))
        third = along_z(jnp.concatenate(corners, axis=0))
        passed = along_y(first)
        if aside:
            extra, passed[0] = aside(passed[0])
            second, later, extra = lax.optimization_barrier((second, later, extra))
        arrived = [first] + passed + [second] + along_y(second) + [third]
        total = None
        for matrix, values in zip(matrices, arrived):
            product = dot(matrix, values)
            total = product if total is None else total + product
        return total.astype(jnp.bfloat16), later, extra

    swaps = [[(i, i ^ delta) for i in range(fronts)] for delta in range(fronts)]

    def routing(after):
        counts, owners, places, after = lax.optimization_barrier(
            (tile_count, tile_owner, tile_rows, after)
        )
        serial = jnp.arange(tiles, dtype=jnp.int32)
        live_count = jnp.sum(jnp.where(jnp.arange(fronts) == me, counts, 0))
        alive = wide_index * tiles + serial < live_count
        owners = owners[0, :, 0]
        same_owner = owners[:, None] == owners[None, :]
        earlier = serial[None, :] < serial[:, None]
        slot = jnp.sum((same_owner & earlier).astype(jnp.int32), axis=1)
        seat = (owners ^ me) * CAPACITY + slot
        slots = fronts * CAPACITY
        chosen = jnp.arange(slots, dtype=jnp.int32)[:, None] == seat[None, :]
        shifted = jnp.where(alive[:, None], places[0] - parent_height, 0)
        rows_out = parent_height + jnp.sum(jnp.where(chosen[:, :, None], shifted[None], 0), axis=1)
        rows_out = rows_out.reshape(fronts, CAPACITY * height)
        rows_in = [rows_out[0]] + [
            lax.ppermute(rows_out[delta], "front", swaps[delta]) for delta in range(1, fronts)
        ]
        picker = (
            jnp.arange(slots * height, dtype=jnp.int32)[:, None]
            == (seat[:, None] * height + jnp.arange(height, dtype=jnp.int32)[None, :]).reshape(1, -1)
        ).astype(jnp.bfloat16)
        picker = picker.reshape(fronts, CAPACITY * height, tiles * height)
        alive_rows = jnp.broadcast_to(alive[:, None], (tiles, height)).reshape(-1, 1)
        return (rows_in, picker, alive_rows), after

    solved, below_parts, (rows_in, picker, alive_rows) = gathered_product(
        assembled(inv_diag[0]), rhs[0], assembled(below[0]), routing
    )
    numbers = jnp.arange(parent_height, dtype=jnp.int32)[:, None]

    update, _, _ = gathered_product(below_parts, solved)
    update = jnp.where(alive_rows, update, jnp.zeros_like(update))
    values_out = [dot(picker[delta], update).astype(jnp.bfloat16) for delta in range(fronts)]
    values_in = [values_out[0]] + [
        lax.ppermute(values_out[delta], "front", swaps[delta]) for delta in range(1, fronts)
    ]
    parent_new = parent_rhs[0].astype(jnp.float32)
    for rows_here, values in zip(rows_in, values_in):
        hits = (numbers == rows_here[None, :]).astype(jnp.bfloat16)
        parent_new = parent_new - dot(hits, values)
    return (solved[None], parent_new[None])


def solution(mesh):
    split = P("front", "wide", None)
    return jax.shard_map(
        body,
        mesh=mesh,
        in_specs=(split, split, split, P(), split, split, split),
        out_specs=(split, split),
        check_vma=False,
    )
```

time: 176 us -> 235 us (1.34)
  blocking collectives: 0 us -> 86.1 us
  matrix products: 86.7 us -> 28.7 us
  starting transfers between devices: 69.9 us -> 12.6 us
  local copies, waits for them, and re-layouts: 6.9 us -> 53.5 us
  other arithmetic: 2.2 us -> 18.6 us
  waiting for transfers between devices: 6 us -> 19.5 us
  between operations: 1.9 us -> 14.6 us
    all_gather x0 -> x4, blocking collectives: none -> 86.1 us  [along_z(): lax.all_gather(values, 'wide', axis=0, tiled=True, axis_index_groups=z_gr...]
    dot_general x74 -> x17, matrix products: 86.7 us -> 28.7 us  [dot(): return row_major(jnp.dot(a, b, preferred_element_type=jnp.float32))]
    ppermute x56 -> x6, starting transfers between devices: 64.1 us -> 8.7 us  [along_y(): lax.ppermute(values, 'wide', y_shifts[shift])]
    unnamed x24 -> x93, local copies, waits for them, and re-layouts: 3.78 us -> 30.7 us
    dynamic_slice x0 -> x2, local copies, waits for them, and re-layouts: none -> 17.1 us  [columns_of(): lax.dynamic_slice_in_dim(matrix, (i * across + (y + across - shift) % acr...]
    concatenate x0 -> x6, other arithmetic: none -> 15.2 us  [the longest x4 12.9 us: columns_of(): jnp.concatenate([lax.dynamic_slice_in_dim(matrix, (i * across + (y + acro...]
    ppermute x56 -> x6, waiting for transfers between devices: 2.42 us -> 13.3 us  [along_y(): lax.ppermute(values, 'wide', y_shifts[shift])]
    concatenate x0 -> x2, local copies, waits for them, and re-layouts: none -> 3.73 us  [columns_of(): jnp.concatenate([lax.dynamic_slice_in_dim(matrix, (i * across + (y + acro...]
  transfers between devices with their start and end apart: 65 -> 14, of which waited for: 7 -> 7; matrix products, arithmetic and copies ran while one was open for 51% -> 37% of each run, Pallas kernels for 0% -> 0%
where the time goes in v4:
time: 235 us; the launch traced here: 234 us
  blocking collectives  86.1 us (37%)
  local copies, waits for them, and re-layouts  53.5 us (23%)
  matrix products  28.7 us (12%)
  waiting for transfers between devices  19.5 us (8%)
  other arithmetic  18.6 us (8%)
  between operations  14.6 us (6%)
  starting transfers between devices  12.6 us (5%)
    all_gather x4, blocking collectives, along_z(): lax.all_gather(values, 'wide', axis=0, tiled=True, axis_index_groups=z_gr...  86.1 us
    unnamed x93, local copies, waits for them, and re-layouts  30.7 us
    dot_general x17, matrix products, dot(): return row_major(jnp.dot(a, b, preferred_element_type=jnp.float32))  28.7 us
    dynamic_slice x2, local copies, waits for them, and re-layouts, columns_of(): lax.dynamic_slice_in_dim(matrix, (i * across + (y + across - shift) % acr...  17.1 us
    ppermute x6, waiting for transfers between devices, along_y(): lax.ppermute(values, 'wide', y_shifts[shift])  13.3 us
    concatenate x4, other arithmetic, columns_of(): jnp.concatenate([lax.dynamic_slice_in_dim(matrix, (i * across + (y + acro...  12.9 us
    ppermute x6, starting transfers between devices, along_y(): lax.ppermute(values, 'wide', y_shifts[shift])  8.7 us
  transfers between devices with their start and end apart: 14, of which 7 were waited for; matrix products, arithmetic and copies ran while one was open for 37% of the time, Pallas kernels for 0%

profile of v4, /device:TPU:0, one launch (start us, length us, event | category | flops | bytes accessed | tf_op | source)
XLA Modules:
  0.0 233.6 jit_solution(11231418533722696189)
XLA Ops:
  7.2 0.9 slice_bitcast_fusion.1
  8.1 3.0 %collective-permute-start = (bf16[256,256]{1,0:T(8,128)(2,1)S(1)}, bf16[256,256]{1,0:T(8,128)(2,1)}, u32[]{:S(2)}, u32[]{:S(2)}) collective-permute-start(bf16[256,256]{1,0:T(8,128)(2,1)S(1)} %slice_bitcast_fusion.1), channel_id=1, source_target_pairs={{0,1},{1,0},{2,3},{3,2},{4,5},{5,4},{6,7},{7,6},{8,9},{9,8},{10,11... | collective-permute-start | bytes 393224 | tf_op jit(solution)/shard_map/ppermute | solution.py:43
  11.2 1.0 slice_bitcast_fusion
  12.2 1.9 bitcast_dynamic-update-slice_fusion.7
  14.2 9.6 %dynamic-slice_bitcast_fusion.3 = (bf16[1024,384]{1,0:T(8,128)(2,1)}, bf16[1024,384]{1,0:T(8,128)(2,1)}, bf16[1024,384]{1,0:T(8,128)(2,1)}, bf16[1024,384]{1,0:T...) fusion(bf16[1,1024,8192]{2,1,0:T(8,128)(2,1)} %param.7, ...), kind=kLoop, calls=%fused_computation.31 | loop fusion | bytes 25165888 | tf_op jit(solution)/shard_map/dynamic_slice | solution.py:48
  23.8 7.5 %dynamic-slice_bitcast_fusion.19 = (bf16[768,384]{1,0:T(8,128)(2,1)}, bf16[768,384]{1,0:T(8,128)(2,1)}, bf16[768,384]{1,0:T(8,128)(2,1)}, bf16[768,384]{1,0:T(8,...) fusion(bf16[1,768,8192]{2,1,0:T(8,128)(2,1)} %param.8, ...), kind=kLoop, calls=%fused_computation.47 | loop fusion | bytes 18874432 | tf_op jit(solution)/shard_map/dynamic_slice | solution.py:48
  31.3 1.8 bitcast_dynamic-update-slice_fusion.15
  33.1 20.3 %all-gather = bf16[1,1536,256]{2,1,0:T(8,128)(2,1)} all-gather(bf16[1,384,256]{2,1,0:T(8,128)(2,1)S(1)} %get-tuple-element.115), channel_id=2, replica_groups={{0,2,4,6},{1,3,5,7},{8,10,12,14},{9,11,13,15},{16,18,20,22},{17,19,21,2..., dimensions={1}, use_global_device_ids=true | all-gather | bytes 983040 | tf_op jit(solution)/shard_map/all_gather | solution.py:40
  53.4 1.9 bitcast_dynamic-update-slice_fusion.6
  55.3 1.8 bitcast_dynamic-update-slice_fusion.14
  57.1 1.9 bitcast_dynamic-update-slice_fusion.5
  59.0 1.8 bitcast_dynamic-update-slice_fusion.13
  60.8 1.9 bitcast_dynamic-update-slice_fusion.4
  62.7 1.8 bitcast_dynamic-update-slice_fusion.12
  64.5 1.9 bitcast_dynamic-update-slice_fusion.3
  66.5 1.8 bitcast_dynamic-update-slice_fusion.11
  68.3 1.9 bitcast_dynamic-update-slice_fusion.2
  70.2 1.8 bitcast_dynamic-update-slice_fusion.10
  72.0 1.9 bitcast_dynamic-update-slice_fusion.1
  73.9 1.8 bitcast_dynamic-update-slice_fusion.9
  75.8 4.4 %pad_maximum_fusion.2 = (bf16[1024,1536]{1,0:T(8,128)(2,1)S(1)}, bf16[1024,1536]{1,0:T(8,128)(2,1)}) fusion(bf16[1024,384]{1,0:T(8,128)(2,1)} %get-tuple-element.84, bf16[1024,384]{1,0:T(8,128)(2,1)} %get-tuple-element.85, bf16[1024,384]{1,0:T(8,128)(2,1)} %get-tuple-element.86, bf16[1024,384]{1,0:T(8,128)(2,1)} %get-tuple-element.87, ...), kind=kLoop, calls=%fused_computation.2 | loop fusion | flops 25165824 | bytes 12582912 | tf_op jit(solution)/shard_map/concatenate | solution.py:46
  80.3 0.5 copy-done.6
  81.6 3.5 %pad_maximum_fusion = (bf16[1024,1536]{1,0:T(8,128)(2,1)}, bf16[1024,1536]{1,0:T(8,128)(2,1)}) fusion(bf16[1024,384]{1,0:T(8,128)(2,1)S(1)} %copy-done.6, bf16[1024,384]{1,0:T(8,128)(2,1)S(1)} %copy-done.7, bf16[1024,384]{1,0:T(8,128)(2,1)S(1)} %copy-done.8, bf16[1024,384]{1,0:T(8,128)(2,1)S(1)} %copy-done.9, bf16[1024,384]{1,0:T(8,128)(2,1)S(1)} %copy-done.2, ...), kind=kLoop, calls=%fused_computation | loop fusion | flops 25165824 | bytes 12582912 | tf_op jit(solution)/shard_map/concatenate | solution.py:46
  85.2 0.6 copy-done.26
  86.1 2.6 %pad_maximum_fusion.6 = (bf16[768,1536]{1,0:T(8,128)(2,1)}, bf16[768,1536]{1,0:T(8,128)(2,1)}) fusion(bf16[768,384]{1,0:T(8,128)(2,1)S(1)} %copy-done.24, bf16[768,384]{1,0:T(8,128)(2,1)S(1)} %copy-done.25, bf16[768,384]{1,0:T(8,128)(2,1)S(1)} %copy-done.26, bf16[768,384]{1,0:T(8,128)(2,1)S(1)} %copy-done.27, bf16[768,384]{1,0:T(8,128)(2,1)S(1)} %copy-done.21, ...), kind=kLoop, calls=%fused_computation.7 | loop fusion | flops 18874368 | bytes 9437184 | tf_op jit(solution)/shard_map/concatenate | solution.py:46
  88.8 0.5 copy-done.16
  89.3 0.4 copy-done.17
  90.1 2.4 %pad_maximum_fusion.4 = (bf16[768,1536]{1,0:T(8,128)(2,1)}, bf16[768,1536]{1,0:T(8,128)(2,1)}) fusion(bf16[768,384]{1,0:T(8,128)(2,1)S(1)} %copy-done.16, bf16[768,384]{1,0:T(8,128)(2,1)S(1)} %copy-done.17, bf16[768,384]{1,0:T(8,128)(2,1)S(1)} %copy-done.18, bf16[768,384]{1,0:T(8,128)(2,1)S(1)} %copy-done.19, bf16[768,384]{1,0:T(8,128)(2,1)S(1)} %copy-done.12, ...), kind=kLoop, calls=%fused_computation.5 | loop fusion | flops 18874368 | bytes 9437184 | tf_op jit(solution)/shard_map/concatenate | solution.py:46
  92.5 1.8 bitcast_dynamic-update-slice_fusion.8
  94.3 1.9 bitcast_dynamic-update-slice_fusion
  96.2 0.5 collective-permute-start.1
  96.7 1.6 pad_maximum_fusion.8
  98.4 21.8 %all_gather.19 = bf16[1536,256]{1,0:T(8,128)(2,1)} all-gather(bf16[384,256]{1,0:T(8,128)(2,1)S(1)} %get-tuple-element.47), channel_id=1, replica_groups={{0,2,4,6},{1,3,5,7},{8,10,12,14},{9,11,13,15},{16,18,20,22},{17,19,21,2..., dimensions={0}, use_global_device_ids=true | all-gather | bytes 983040 | tf_op jit(solution)/shard_map/all_gather | solution.py:40
  120.2 3.2 %fusion.27 = f32[1024,256]{1,0:T(8,128)S(1)} fusion(bf16[1024,1536]{1,0:T(8,128)(2,1)} %get-tuple-element.42, bf16[1536,256]{1,0:T(8,128)(2,1)} %bitcast), kind=kOutput, calls=%fused_computation.121 | convolution fusion | flops 805306368 | bytes 4980736 | tf_op jit(solution)/shard_map/dot_general | solution.py:16
  123.8 0.6 fusion.25
  124.4 0.7 add_compare_fusion
  125.3 1.5 collective-permute-start.3
  126.8 0.4 collective-permute-start.4
  127.3 1.5 compare_convert_fusion
  129.0 0.8 collective-permute-done.4
  129.8 1.6 collective-permute-start.5
  131.4 3.1 %convolution_add_fusion.1 = f32[1024,256]{1,0:T(8,128)} fusion(f32[1024,256]{1,0:T(8,128)S(1)} %fusion.27, bf16[1024,1536]{1,0:T(8,128)(2,1)S(1)} %copy-done.11, bf16[1536,256]{1,0:T(8,128)(2,1)} %collective-permute-done.1), kind=kOutput, calls=%fused_computation.10 | convolution fusion | flops 805568512 | bytes 6029312 | tf_op jit(solution)/shard_map/dot_general | solution.py:16
  134.5 3.9 %fusion.29 = f32[1024,256]{1,0:T(8,128)S(1)} fusion(bf16[1024,2048]{1,0:T(8,128)(2,1)} %bitcast_dynamic-update-slice_fusion, bf16[2048,256]{1,0:T(8,128)(2,1)} %all-gather.4.cloned.1.call-done), kind=kOutput, calls=%fused_computation.123 | convolution fusion | flops 1073741824 | bytes 6291456 | tf_op jit(solution)/shard_map/dot_general | solution.py:16
  138.4 11.7 %collective-permute-done.5 = bf16[1536,256]{1,0:T(8,128)(2,1)} collective-permute-done((bf16[1536,256]{1,0:T(8,128)(2,1)}, bf16[1536,256]{1,0:T(8,128)(2,1)}, u32[]{:S(2)}, u32[]{:S(2)}) %collective-permute-start.5) | collective-permute-done | bytes 786464 | tf_op jit(solution)/shard_map/ppermute | solution.py:43
  150.1 2.1 fusion.28
  152.2 2.1 fusion.2
  154.4 0.7 copy-done
  155.2 1.3 collective-permute-start.6
  156.5 20.0 %all_gather.21 = bf16[1536,256]{1,0:T(8,128)(2,1)S(1)} all-gather(bf16[384,256]{1,0:T(8,128)(2,1)S(1)} %get-tuple-element.113), channel_id=1, replica_groups={{0,2,4,6},{1,3,5,7},{8,10,12,14},{9,11,13,15},{16,18,20,22},{17,19,21,2..., dimensions={0}, use_global_device_ids=true | all-gather | bytes 983040 | tf_op jit(solution)/shard_map/all_gather | solution.py:40
  176.5 0.7 pad_maximum_fusion.9
  177.7 24.0 %all_gather.22 = bf16[1536,256]{1,0:T(8,128)(2,1)} all-gather(bf16[384,256]{1,0:T(8,128)(2,1)S(1)} %get-tuple-element.70), channel_id=1, replica_groups={{0,2,4,6},{1,3,5,7},{8,10,12,14},{9,11,13,15},{16,18,20,22},{17,19,21,2..., dimensions={0}, use_global_device_ids=true | all-gather | bytes 983040 | tf_op jit(solution)/shard_map/all_gather | solution.py:40
  201.7 1.8 collective-permute-start.8
  203.5 0.8 fusion.30
  204.3 2.1 convolution_add_fusion.4
  206.4 1.9 convolution_add_fusion.3
  208.3 0.9 all-gather.6.cloned.1.call-done
  209.2 3.2 %fusion.31 = f32[768,256]{1,0:T(8,128)S(1)} fusion(bf16[768,2048]{1,0:T(8,128)(2,1)} %bitcast_dynamic-update-slice_fusion.8, bf16[2048,256]{1,0:T(8,128)(2,1)} %all-gather.6.cloned.1.call-done), kind=kOutput, calls=%fused_computation.125 | convolution fusion | flops 805306368 | bytes 4980736 | tf_op jit(solution)/shard_map/dot_general | solution.py:16
  212.3 1.6 collective-permute-done.8
  214.0 1.9 fusion.4
  217.4 1.7 collective-permute-start.11
  219.0 1.8 convolution_subtract_fusion.1
  220.8 2.7 %collective-permute-done.10 = bf16[256,256]{1,0:T(8,128)(2,1)S(1)} collective-permute-done((bf16[256,256]{1,0:T(8,128)(2,1)S(1)}, bf16[256,256]{1,0:T(8,128)(2,1)S(1)}, u32[]{:S(2)}, u32[]{:S(2)}) %collective-permute-start.10) | collective-permute-done | bytes 131104 | tf_op jit(solution)/shard_map/ppermute | solution.py:128
  223.8 1.7 collective-permute-done.11
  225.7 1.0 fusion.7
  (107 shorter events, 5.0 us)
Async XLA Ops:
  7.2 127.4 %all-gather.4.cloned.1.call-start = ((), (), s32[]{:S(2)}) async-start(), calls=%async_computation | async-start | bytes 1310720 | tf_op jit(solution)/shard_map/all_gather | solution.py:40
  8.1 88.1 %collective-permute-start = (bf16[256,256]{1,0:T(8,128)(2,1)S(1)}, bf16[256,256]{1,0:T(8,128)(2,1)}, u32[]{:S(2)}, u32[]{:S(2)}) collective-permute-start(bf16[256,256]{1,0:T(8,128)(2,1)S(1)} %slice_bitcast_fusion.1), channel_id=1, source_target_pairs={{0,1},{1,0},{2,3},{3,2},{4,5},{5,4},{6,7},{7,6},{8,9},{9,8},{10,11... | collective-permute-start | bytes 393224 | tf_op jit(solution)/shard_map/ppermute | solution.py:43
  75.7 4.4 %copy-start.2 = (bf16[1024,384]{1,0:T(8,128)(2,1)S(1)}, bf16[1024,384]{1,0:T(8,128)(2,1)}, u32[]{:S(2)}) copy-start(bf16[1024,384]{1,0:T(8,128)(2,1)} %get-tuple-element.88) | copy-start | bytes 2359300
  75.7 4.4 %copy-start.3 = (bf16[1024,384]{1,0:T(8,128)(2,1)S(1)}, bf16[1024,384]{1,0:T(8,128)(2,1)}, u32[]{:S(2)}) copy-start(bf16[1024,384]{1,0:T(8,128)(2,1)} %get-tuple-element.89) | copy-start | bytes 2359300
  75.7 4.4 %copy-start.4 = (bf16[1024,384]{1,0:T(8,128)(2,1)S(1)}, bf16[1024,384]{1,0:T(8,128)(2,1)}, u32[]{:S(2)}) copy-start(bf16[1024,384]{1,0:T(8,128)(2,1)} %get-tuple-element.90) | copy-start | bytes 2359300
  75.7 4.6 %copy-start.5 = (bf16[1024,384]{1,0:T(8,128)(2,1)S(1)}, bf16[1024,384]{1,0:T(8,128)(2,1)}, u32[]{:S(2)}) copy-start(bf16[1024,384]{1,0:T(8,128)(2,1)} %get-tuple-element.91) | copy-start | bytes 2359300
  75.7 5.1 %copy-start.6 = (bf16[1024,384]{1,0:T(8,128)(2,1)S(1)}, bf16[1024,384]{1,0:T(8,128)(2,1)}, u32[]{:S(2)}) copy-start(bf16[1024,384]{1,0:T(8,128)(2,1)} %get-tuple-element.92) | copy-start | bytes 2359300
  75.7 5.3 %copy-start.7 = (bf16[1024,384]{1,0:T(8,128)(2,1)S(1)}, bf16[1024,384]{1,0:T(8,128)(2,1)}, u32[]{:S(2)}) copy-start(bf16[1024,384]{1,0:T(8,128)(2,1)} %get-tuple-element.93) | copy-start | bytes 2359300
  75.7 5.5 %copy-start.8 = (bf16[1024,384]{1,0:T(8,128)(2,1)S(1)}, bf16[1024,384]{1,0:T(8,128)(2,1)}, u32[]{:S(2)}) copy-start(bf16[1024,384]{1,0:T(8,128)(2,1)} %get-tuple-element.94) | copy-start | bytes 2359300
  75.8 5.8 %copy-start.9 = (bf16[1024,384]{1,0:T(8,128)(2,1)S(1)}, bf16[1024,384]{1,0:T(8,128)(2,1)}, u32[]{:S(2)}) copy-start(bf16[1024,384]{1,0:T(8,128)(2,1)} %get-tuple-element.95) | copy-start | bytes 2359300
  81.5 3.5 %copy-start.20 = (bf16[768,384]{1,0:T(8,128)(2,1)S(1)}, bf16[768,384]{1,0:T(8,128)(2,1)}, u32[]{:S(2)}) copy-start(bf16[768,384]{1,0:T(8,128)(2,1)} %get-tuple-element.96) | copy-start | bytes 1769476
  81.5 3.5 %copy-start.21 = (bf16[768,384]{1,0:T(8,128)(2,1)S(1)}, bf16[768,384]{1,0:T(8,128)(2,1)}, u32[]{:S(2)}) copy-start(bf16[768,384]{1,0:T(8,128)(2,1)} %get-tuple-element.97) | copy-start | bytes 1769476
  81.5 3.5 %copy-start.22 = (bf16[768,384]{1,0:T(8,128)(2,1)S(1)}, bf16[768,384]{1,0:T(8,128)(2,1)}, u32[]{:S(2)}) copy-start(bf16[768,384]{1,0:T(8,128)(2,1)} %get-tuple-element.98) | copy-start | bytes 1769476
  81.5 3.5 %copy-start.23 = (bf16[768,384]{1,0:T(8,128)(2,1)S(1)}, bf16[768,384]{1,0:T(8,128)(2,1)}, u32[]{:S(2)}) copy-start(bf16[768,384]{1,0:T(8,128)(2,1)} %get-tuple-element.99) | copy-start | bytes 1769476
  81.5 3.5 %copy-start.24 = (bf16[768,384]{1,0:T(8,128)(2,1)S(1)}, bf16[768,384]{1,0:T(8,128)(2,1)}, u32[]{:S(2)}) copy-start(bf16[768,384]{1,0:T(8,128)(2,1)} %get-tuple-element.100) | copy-start | bytes 1769476
  81.5 3.7 %copy-start.25 = (bf16[768,384]{1,0:T(8,128)(2,1)S(1)}, bf16[768,384]{1,0:T(8,128)(2,1)}, u32[]{:S(2)}) copy-start(bf16[768,384]{1,0:T(8,128)(2,1)} %get-tuple-element.101) | copy-start | bytes 1769476
  81.6 4.3 %copy-start.26 = (bf16[768,384]{1,0:T(8,128)(2,1)S(1)}, bf16[768,384]{1,0:T(8,128)(2,1)}, u32[]{:S(2)}) copy-start(bf16[768,384]{1,0:T(8,128)(2,1)} %get-tuple-element.102) | copy-start | bytes 1769476
  81.6 4.5 %copy-start.27 = (bf16[768,384]{1,0:T(8,128)(2,1)S(1)}, bf16[768,384]{1,0:T(8,128)(2,1)}, u32[]{:S(2)}) copy-start(bf16[768,384]{1,0:T(8,128)(2,1)} %get-tuple-element.103) | copy-start | bytes 1769476
  86.1 2.7 %copy-start.12 = (bf16[768,384]{1,0:T(8,128)(2,1)S(1)}, bf16[768,384]{1,0:T(8,128)(2,1)}, u32[]{:S(2)}) copy-start(bf16[768,384]{1,0:T(8,128)(2,1)} %get-tuple-element.104) | copy-start | bytes 1769476
  86.1 2.7 %copy-start.13 = (bf16[768,384]{1,0:T(8,128)(2,1)S(1)}, bf16[768,384]{1,0:T(8,128)(2,1)}, u32[]{:S(2)}) copy-start(bf16[768,384]{1,0:T(8,128)(2,1)} %get-tuple-element.105) | copy-start | bytes 1769476
  86.1 2.7 %copy-start.14 = (bf16[768,384]{1,0:T(8,128)(2,1)S(1)}, bf16[768,384]{1,0:T(8,128)(2,1)}, u32[]{:S(2)}) copy-start(bf16[768,384]{1,0:T(8,128)(2,1)} %get-tuple-element.106) | copy-start | bytes 1769476
  86.1 2.7 %copy-start.15 = (bf16[768,384]{1,0:T(8,128)(2,1)S(1)}, bf16[768,384]{1,0:T(8,128)(2,1)}, u32[]{:S(2)}) copy-start(bf16[768,384]{1,0:T(8,128)(2,1)} %get-tuple-element.107) | copy-start | bytes 1769476
  86.1 3.2 %copy-start.16 = (bf16[768,384]{1,0:T(8,128)(2,1)S(1)}, bf16[768,384]{1,0:T(8,128)(2,1)}, u32[]{:S(2)}) copy-start(bf16[768,384]{1,0:T(8,128)(2,1)} %get-tuple-element.108) | copy-start | bytes 1769476
  86.1 3.6 %copy-start.17 = (bf16[768,384]{1,0:T(8,128)(2,1)S(1)}, bf16[768,384]{1,0:T(8,128)(2,1)}, u32[]{:S(2)}) copy-start(bf16[768,384]{1,0:T(8,128)(2,1)} %get-tuple-element.109) | copy-start | bytes 1769476
  86.1 3.8 %copy-start.18 = (bf16[768,384]{1,0:T(8,128)(2,1)S(1)}, bf16[768,384]{1,0:T(8,128)(2,1)}, u32[]{:S(2)}) copy-start(bf16[768,384]{1,0:T(8,128)(2,1)} %get-tuple-element.110) | copy-start | bytes 1769476
  86.1 4.0 %copy-start.19 = (bf16[768,384]{1,0:T(8,128)(2,1)S(1)}, bf16[768,384]{1,0:T(8,128)(2,1)}, u32[]{:S(2)}) copy-start(bf16[768,384]{1,0:T(8,128)(2,1)} %get-tuple-element.111) | copy-start | bytes 1769476
  96.2 27.2 %collective-permute-start.1 = (bf16[1536,256]{1,0:T(8,128)(2,1)}, bf16[1536,256]{1,0:T(8,128)(2,1)}, u32[]{:S(2)}, u32[]{:S(2)}) collective-permute-start(bf16[1536,256]{1,0:T(8,128)(2,1)} %bitcast), channel_id=1, source_target_pairs={{0,1},{1,0},{2,3},{3,2},{4,5},{5,4},{6,7},{7,6},{8,9},{9,8},{10,11... | collective-permute-start | bytes 2359304 | tf_op jit(solution)/shard_map/ppermute | solution.py:43
  98.4 110.8 %all-gather.6.cloned.1.call-start = ((), (), s32[]{:S(2)}) async-start(), calls=%async_computation.1 | async-start | bytes 1310720 | tf_op jit(solution)/shard_map/all_gather | solution.py:40
  120.2 3.3 %copy-start.34 = (s32[1,6,1]{1,2,0:T(1,128)S(1)}, s32[1,6,1]{1,2,0:T(1,128)}, u32[]{:S(2)}) copy-start(s32[1,6,1]{1,2,0:T(1,128)} %param.11) | copy-start | bytes 76
  120.2 3.5 %copy-start.36 = (s32[4]{0:T(128)S(1)}, s32[4]{0:T(128)}, u32[]{:S(2)}) copy-start(s32[4]{0:T(128)} %param.10) | copy-start | bytes 52
  120.2 4.8 %copy-start.33 = (s32[1,6,128]{2,0,1:T(1,128)S(1)}, s32[1,6,128]{2,0,1:T(1,128)}, u32[]{:S(2)}) copy-start(s32[1,6,128]{2,0,1:T(1,128)} %param.12) | copy-start | bytes 9220
  120.2 11.2 %copy-start.11 = (bf16[1024,1536]{1,0:T(8,128)(2,1)S(1)}, bf16[1024,1536]{1,0:T(8,128)(2,1)}, u32[]{:S(2)}) copy-start(bf16[1024,1536]{1,0:T(8,128)(2,1)} %get-tuple-element.44) | copy-start | bytes 9437188
  125.2 3.6 %collective-permute-start.2 = (s32[256]{0:T(256)S(1)}, s32[256]{0:T(256)S(1)}, u32[]{:S(2)}, u32[]{:S(2)}) collective-permute-start(s32[256]{0:T(256)S(1)} %get-tuple-element.118), channel_id=1, source_target_pairs={{0,8},{8,0},{16,24},{24,16},{1,9},{9,1},{17,25},{25,17},{2,10},{10... | collective-permute-start | bytes 3080 | tf_op jit(solution)/shard_map/ppermute | solution.py:109
  125.3 3.6 %collective-permute-start.3 = (s32[256]{0:T(256)S(1)}, s32[256]{0:T(256)S(1)}, u32[]{:S(2)}, u32[]{:S(2)}) collective-permute-start(s32[256]{0:T(256)S(1)} %get-tuple-element.117), channel_id=1, source_target_pairs={{0,16},{8,24},{16,0},{24,8},{1,17},{9,25},{17,1},{25,9},{2,18},{10... | collective-permute-start | bytes 3080 | tf_op jit(solution)/shard_map/ppermute | solution.py:109
  126.8 3.0 %collective-permute-start.4 = (s32[256]{0:T(256)S(1)}, s32[256]{0:T(256)S(1)}, u32[]{:S(2)}, u32[]{:S(2)}) collective-permute-start(s32[256]{0:T(256)S(1)} %get-tuple-element.116), channel_id=1, source_target_pairs={{0,24},{8,16},{16,8},{24,0},{1,25},{9,17},{17,9},{25,1},{2,26},{10... | collective-permute-start | bytes 3080 | tf_op jit(solution)/shard_map/ppermute | solution.py:109
  129.8 20.3 %collective-permute-start.5 = (bf16[1536,256]{1,0:T(8,128)(2,1)}, bf16[1536,256]{1,0:T(8,128)(2,1)}, u32[]{:S(2)}, u32[]{:S(2)}) collective-permute-start(bf16[1536,256]{1,0:T(8,128)(2,1)} %all_gather.19), channel_id=1, source_target_pairs={{0,1},{1,0},{2,3},{3,2},{4,5},{5,4},{6,7},{7,6},{8,9},{9,8},{10,11... | collective-permute-start | bytes 2359304 | tf_op jit(solution)/shard_map/ppermute | solution.py:43
  134.5 15.6 %copy-start.10 = (bf16[1024,1536]{1,0:T(8,128)(2,1)S(1)}, bf16[1024,1536]{1,0:T(8,128)(2,1)}, u32[]{:S(2)}) copy-start(bf16[1024,1536]{1,0:T(8,128)(2,1)} %get-tuple-element.52) | copy-start | bytes 9437188
  138.4 13.8 %copy-start.1 = (f32[1024,256]{1,0:T(8,128)S(1)}, f32[1024,256]{1,0:T(8,128)}, u32[]{:S(2)}) copy-start(f32[1024,256]{1,0:T(8,128)} %convolution_add_fusion.1) | copy-start | bytes 3145732
  154.4 0.8 copy-start
  154.4 49.1 %copy-start.31 = (bf16[768,1536]{1,0:T(8,128)(2,1)S(1)}, bf16[768,1536]{1,0:T(8,128)(2,1)}, u32[]{:S(2)}) copy-start(bf16[768,1536]{1,0:T(8,128)(2,1)} %get-tuple-element.66) | copy-start | bytes 7077892
  155.2 21.3 %collective-permute-start.6 = (bf16[256,256]{1,0:T(8,128)(2,1)S(1)}, bf16[256,256]{1,0:T(8,128)(2,1)S(1)}, u32[]{:S(2)}, u32[]{:S(2)}) collective-permute-start(bf16[256,256]{1,0:T(8,128)(2,1)S(1)} %slice.74), channel_id=1, source_target_pairs={{0,1},{1,0},{2,3},{3,2},{4,5},{5,4},{6,7},{7,6},{8,9},{9,8},{10,11... | collective-permute-start | bytes 393224 | tf_op jit(solution)/shard_map/ppermute | solution.py:43
  177.2 27.1 %collective-permute-start.7 = (bf16[1536,256]{1,0:T(8,128)(2,1)S(1)}, bf16[1536,256]{1,0:T(8,128)(2,1)}, u32[]{:S(2)}, u32[]{:S(2)}) collective-permute-start(bf16[1536,256]{1,0:T(8,128)(2,1)S(1)} %all_gather.21), channel_id=1, source_target_pairs={{0,1},{1,0},{2,3},{3,2},{4,5},{5,4},{6,7},{7,6},{8,9},{9,8},{10,11... | collective-permute-start | bytes 2359304 | tf_op jit(solution)/shard_map/ppermute | solution.py:43
  177.6 26.6 %copy-start.30 = (bf16[768,1536]{1,0:T(8,128)(2,1)S(1)}, bf16[768,1536]{1,0:T(8,128)(2,1)}, u32[]{:S(2)}) copy-start(bf16[768,1536]{1,0:T(8,128)(2,1)} %get-tuple-element.68) | copy-start | bytes 7077892
  201.7 12.3 %collective-permute-start.8 = (bf16[1536,256]{1,0:T(8,128)(2,1)}, bf16[1536,256]{1,0:T(8,128)(2,1)}, u32[]{:S(2)}, u32[]{:S(2)}) collective-permute-start(bf16[1536,256]{1,0:T(8,128)(2,1)} %all_gather.22), channel_id=1, source_target_pairs={{0,1},{1,0},{2,3},{3,2},{4,5},{5,4},{6,7},{7,6},{8,9},{9,8},{10,11... | collective-permute-start | bytes 2359304 | tf_op jit(solution)/shard_map/ppermute | solution.py:43
  204.3 2.1 copy-start.29
  208.3 5.7 %copy-start.28 = (bf16[768,1536]{1,0:T(8,128)(2,1)S(1)}, bf16[768,1536]{1,0:T(8,128)(2,1)}, u32[]{:S(2)}) copy-start(bf16[768,1536]{1,0:T(8,128)(2,1)} %get-tuple-element.71) | copy-start | bytes 7077892
  212.3 3.6 %copy-start.32 = (bf16[4,256,768]{2,1,0:T(8,128)(2,1)S(1)}, bf16[4,256,768]{2,1,0:T(8,128)(2,1)}, u32[]{:S(2)}) copy-start(bf16[4,256,768]{2,1,0:T(8,128)(2,1)} %compare_convert_fusion) | copy-start | bytes 4718596
  215.9 1.5 copy-start.37
  215.9 3.1 %copy-start.35 = (bf16[1,512,256]{2,1,0:T(8,128)(2,1)S(1)}, bf16[1,512,256]{2,1,0:T(8,128)(2,1)}, u32[]{:S(2)}) copy-start(bf16[1,512,256]{2,1,0:T(8,128)(2,1)} %param.13) | copy-start | bytes 786436
  217.1 8.6 %collective-permute-start.9 = (bf16[256,256]{1,0:T(8,128)(2,1)S(1)}, bf16[256,256]{1,0:T(8,128)(2,1)S(1)}, u32[]{:S(2)}, u32[]{:S(2)}) collective-permute-start(bf16[256,256]{1,0:T(8,128)(2,1)S(1)} %convolution_convert_fusion.2), channel_id=1, source_target_pairs={{0,8},{8,0},{16,24},{24,16},{1,9},{9,1},{17,25},{25,17},{2,10},{10... | collective-permute-start | bytes 393224 | tf_op jit(solution)/shard_map/ppermute | solution.py:128
  217.2 6.4 %collective-permute-start.10 = (bf16[256,256]{1,0:T(8,128)(2,1)S(1)}, bf16[256,256]{1,0:T(8,128)(2,1)S(1)}, u32[]{:S(2)}, u32[]{:S(2)}) collective-permute-start(bf16[256,256]{1,0:T(8,128)(2,1)S(1)} %convolution_convert_fusion.1), channel_id=1, source_target_pairs={{0,16},{8,24},{16,0},{24,8},{1,17},{9,25},{17,1},{25,9},{2,18},{10... | collective-permute-start | bytes 393224 | tf_op jit(solution)/shard_map/ppermute | solution.py:128
  217.4 8.1 %collective-permute-start.11 = (bf16[256,256]{1,0:T(8,128)(2,1)S(1)}, bf16[256,256]{1,0:T(8,128)(2,1)S(1)}, u32[]{:S(2)}, u32[]{:S(2)}) collective-permute-start(bf16[256,256]{1,0:T(8,128)(2,1)S(1)} %convolution_convert_fusion), channel_id=1, source_target_pairs={{0,24},{8,16},{16,8},{24,0},{1,25},{9,17},{17,9},{25,1},{2,26},{10... | collective-permute-start | bytes 393224 | tf_op jit(solution)/shard_map/ppermute | solution.py:128
Sparse Core Ops, SparseCore 0:
  98.5 31.8 all-gather.3
  177.3 31.7 all-gather.5
